TPU v7x, 32 devices: a whole 2x2x4 slice. The times are simulated.
32 devices in a mesh: row: 2 (over y), col: 16 (over z, x, core).
Axes of the slice: x: 2, y: 2, z: 4, core: 2. Of those that a mesh axis runs over, the one named last changes fastest.
Arguments:
- features: bfloat16 [32768, 256], P('col', 'row'), may hold values from -6 to 6
- block_values: bfloat16 [2, 16, 256, 128, 128], P('row', 'col'), may hold values from -0.09375 to 0.09375
- block_coords: int32 [2, 16, 2, 256], P('row', 'col'), may hold values from 0 to 127, as said below
- live_blocks: int32 [2, 16], P('row', 'col'), may hold values from 32 to 256, as said below
- weight: bfloat16 [256, 256], replicated, may hold values from -0.375 to 0.375
- bias: float32 [256], replicated, may hold values from -3 to 3
- cotangent: bfloat16 [32768, 256], P(('row', 'col')), may hold values from -6 to 6
Outputs:
- out: bfloat16 [32768, 256], P(('row', 'col'))
- grad_x: bfloat16 [32768, 256], P('col', 'row')
- grad_weight: float32 [256, 256], replicated
- grad_bias: float32 [256], replicated
Inputs may be any that keep to these rules, and one draw needn't show every extreme that they name: `block_coords`: within one tile the 256 slots name distinct pairs of a row block (0 to 127) and a column block (0 to 15). Only the first live_blocks[i, j] slots of tile (i, j) belong to the adjacency; some tile has all 256 slots live.
All inputs are finite; a program needn't handle non-finite values.
Results may differ from a plain program's by a relative error of at most 0.0075.
Values may be sent and summed in bfloat16 or wider, within the bound.
No kernel may reach another device: no remote copies, remote signals or barrier semaphores. Data moves between devices by JAX's collectives and lax.ppermute only.
A program may use at most 128 MiB of HBM per device.

v0:
```python
import math

import jax
import jax.numpy as jnp
from jax import lax
from jax.sharding import PartitionSpec as P


def block_products(block_vals, source, dst_index, src_index, live_count, out_blocks, transposed):
    slot_total = block_vals.shape[0]
    block_size = block_vals.shape[1]
    feat_width = source.shape[2]
    group_size = math.gcd(slot_total, 64)
    pattern = "sab,saf->sbf" if transposed else "sab,sbf->saf"
    offsets = jnp.arange(group_size, dtype=jnp.int32)

    def one_group(turn, totals):
        first_slot = turn * group_size
        slab_vals = lax.dynamic_slice_in_dim(block_vals, first_slot, group_size, 0)
        take_from = lax.dynamic_slice_in_dim(src_index, first_slot, group_size, 0)
        put_to = lax.dynamic_slice_in_dim(dst_index, first_slot, group_size, 0)
        picked = jnp.take(source, take_from, axis=0)
        products = jnp.einsum(pattern, slab_vals, picked, preferred_element_type=jnp.float32)
        alive_mask = first_slot + offsets < live_count
        products = jnp.where(alive_mask[:, None, None], products, 0.0)
        return totals.at[put_to].add(products)

    start_totals = jnp.zeros((out_blocks, block_size, feat_width), jnp.float32)
    turns = slot_total // group_size
    return lax.fori_loop(0, turns, one_group, start_totals)


def on_device(features, block_values, block_coords, live_blocks, weight, bias, cotangent):
    block_vals = block_values[0, 0]
    row_ids = block_coords[0, 0, 0]
    col_ids = block_coords[0, 0, 1]
    live_count = live_blocks[0, 0]
    block_size = block_vals.shape[1]
    feat_width = weight.shape[0]
    col_count = lax.axis_size("col")
    feat_tile = lax.all_gather(features, "row", axis=1, tiled=True)
    col_blocks = feat_tile.shape[0] // block_size
    row_blocks = cotangent.shape[0] * col_count // block_size
    feat_blocks = feat_tile.reshape(col_blocks, block_size, feat_width)
    partial_value = block_products(
        block_vals, feat_blocks, row_ids, col_ids, live_count, row_blocks, False
    )
    partial_value = partial_value.reshape(row_blocks * block_size, feat_width)
    aggregate = lax.psum_scatter(partial_value, "col", scatter_dimension=0, tiled=True).astype(
        jnp.bfloat16
    )
    preact = jnp.dot(aggregate, weight, preferred_element_type=jnp.float32) + bias
    sigmoid_v = jax.nn.sigmoid(preact)
    out = (preact * sigmoid_v).astype(jnp.bfloat16)
    derivative = sigmoid_v * (1.0 + preact * (1.0 - sigmoid_v))
    grad_pre = (cotangent.astype(jnp.float32) * derivative).astype(jnp.bfloat16)
    weight_term = lax.dot_general(
        aggregate, grad_pre, (((0,), (0,)), ((), ())), preferred_element_type=jnp.float32
    )
    bias_term = jnp.sum(grad_pre.astype(jnp.float32), axis=0)
    weight_sum, bias_sum = lax.psum((weight_term, bias_term), ("row", "col"))
    norm_factor = (feat_tile.shape[0] * col_count) ** (-0.5)
    grad_weight = weight_sum * norm_factor
    grad_bias = bias_sum * norm_factor
    grad_agg = lax.dot_general(
        grad_pre, weight, (((1,), (1,)), ((), ())), preferred_element_type=jnp.float32
    ).astype(jnp.bfloat16)
    grad_tile = lax.all_gather(grad_agg, "col", axis=0, tiled=True)
    grad_blocks = grad_tile.reshape(row_blocks, block_size, feat_width)
    partial_x = block_products(
        block_vals, grad_blocks, col_ids, row_ids, live_count, col_blocks, True
    )
    partial_x = partial_x.reshape(col_blocks * block_size, feat_width)
    grad_x = lax.psum_scatter(partial_x, "row", scatter_dimension=1, tiled=True).astype(
        jnp.bfloat16
    )
    return (out, grad_x, grad_weight, grad_bias)


def solution(mesh):
    in_specs = (
        P("col", "row"),
        P("row", "col", None, None, None),
        P("row", "col", None, None),
        P("row", "col"),
        P(),
        P(),
        P(("row", "col"), None),
    )
    out_specs = (P(("row", "col"), None), P("col", "row"), P(), P())
    return jax.shard_map(
        on_device, mesh=mesh, in_specs=in_specs, out_specs=out_specs, check_vma=False
    )
```

profile of v0, /device:TPU:0, one launch (start us, length us, event | category | flops | bytes accessed | tf_op | source)
XLA Modules:
  0.0 592.2 jit_solution(2794704451919862035)
XLA Ops:
  8.7 24.8 %all-gather.3.cloned.1.call-done = bf16[2048,256]{1,0:T(8,128)(2,1)} async-done(((bf16[2048,128]{1,0:T(8,128)(2,1)}), bf16[2048,256]{1,0:T(8,128)(2,1)}) %all-gather.3.cloned.1.call-update) | async-done | bytes 1048592 | tf_op jit(solution)/shard_map/all_gather | solution.py:41
  33.6 7.8 %broadcast_in_dim.123 = f32[128,128,256]{2,1,0:T(8,128)} broadcast(f32[]{:T(128)} %constant.148.clone.1), dimensions={} | broadcast | bytes 16777220 | tf_op jit(solution)/shard_map/broadcast_in_dim | solution.py:28
  41.4 122.4 %while.28 = (s32[]{:T(128)}, f32[128,128,256]{2,1,0:T(8,128)}, s32[256]{0:T(256)S(1)}, s32[]{:T(128)}, bf16[256,128,128]{2,1,0:T(8,128)(2,1)}, /*index=5*/s32[25...) while((s32[]{:T(128)}, f32[128,128,256]{2,1,0:T(8,128)}, ...), condition=%wide.region_2.3_spmd.clone, body=%wide.region_0.2_spmd.clone.sunk | while | flops 543164096 | bytes 48240816 | solution.py:30
  42.1 2.8 gather_fusion
  44.9 7.4 %broadcast_select_fusion.4 = f32[64,128,256]{2,1,0:T(8,128)} fusion(pred[64]{0:T(512)(128)(4,1)S(1)} %get-tuple-element.447, bf16[64,128,256]{2,1,0:T(8,128)(2,1)} %gather_fusion, pred[64]{0:T(512)(128)(4,1)S(1)} %get-tuple-element.449, bf16[256,128,128]{2,1,0:T(8,128)(2,1)} %get-tuple-element.486, s32[]{:T(128)S(6)} %select_n.117), kind=kOutput, calls=%fused_computation.6.clone.1 | convolution fusion | flops 541065216 | bytes 14680196 | tf_op jit(solution)/shard_map/while/body/eval_jaxpr/sab,sbf->saf/dot_general | solution.py:23
  52.4 19.7 %scatter_fusion = f32[128,128,256]{2,1,0:T(8,128)} fusion(f32[128,128,256]{2,1,0:T(8,128)} %get-tuple-element.472, s32[64]{0:T(128)S(1)} %compare_select_fusion.8, f32[64,128,256]{2,1,0:T(8,128)} %broadcast_select_fusion.4), kind=kCustom, calls=%fused_computation.2.clone.clone.1 | custom fusion | flops 2097152 | bytes 25166080 | tf_op jit(solution)/shard_map/while/body/eval_jaxpr/scatter-add | solution.py:26
  72.8 2.8 gather_fusion
  75.6 7.4 %broadcast_select_fusion.4 = f32[64,128,256]{2,1,0:T(8,128)} fusion(pred[64]{0:T(512)(128)(4,1)S(1)} %get-tuple-element.447, bf16[64,128,256]{2,1,0:T(8,128)(2,1)} %gather_fusion, pred[64]{0:T(512)(128)(4,1)S(1)} %get-tuple-element.449, bf16[256,128,128]{2,1,0:T(8,128)(2,1)} %get-tuple-element.486, s32[]{:T(128)S(6)} %select_n.117), kind=kOutput, calls=%fused_computation.6.clone.1 | convolution fusion | flops 541065216 | bytes 14680196 | tf_op jit(solution)/shard_map/while/body/eval_jaxpr/sab,sbf->saf/dot_general | solution.py:23
  83.0 19.6 %scatter_fusion = f32[128,128,256]{2,1,0:T(8,128)} fusion(f32[128,128,256]{2,1,0:T(8,128)} %get-tuple-element.472, s32[64]{0:T(128)S(1)} %compare_select_fusion.8, f32[64,128,256]{2,1,0:T(8,128)} %broadcast_select_fusion.4), kind=kCustom, calls=%fused_computation.2.clone.clone.1 | custom fusion | flops 2097152 | bytes 25166080 | tf_op jit(solution)/shard_map/while/body/eval_jaxpr/scatter-add | solution.py:26
  103.4 2.8 gather_fusion
  106.2 7.4 %broadcast_select_fusion.4 = f32[64,128,256]{2,1,0:T(8,128)} fusion(pred[64]{0:T(512)(128)(4,1)S(1)} %get-tuple-element.447, bf16[64,128,256]{2,1,0:T(8,128)(2,1)} %gather_fusion, pred[64]{0:T(512)(128)(4,1)S(1)} %get-tuple-element.449, bf16[256,128,128]{2,1,0:T(8,128)(2,1)} %get-tuple-element.486, s32[]{:T(128)S(6)} %select_n.117), kind=kOutput, calls=%fused_computation.6.clone.1 | convolution fusion | flops 541065216 | bytes 14680196 | tf_op jit(solution)/shard_map/while/body/eval_jaxpr/sab,sbf->saf/dot_general | solution.py:23
  113.6 19.6 %scatter_fusion = f32[128,128,256]{2,1,0:T(8,128)} fusion(f32[128,128,256]{2,1,0:T(8,128)} %get-tuple-element.472, s32[64]{0:T(128)S(1)} %compare_select_fusion.8, f32[64,128,256]{2,1,0:T(8,128)} %broadcast_select_fusion.4), kind=kCustom, calls=%fused_computation.2.clone.clone.1 | custom fusion | flops 2097152 | bytes 25166080 | tf_op jit(solution)/shard_map/while/body/eval_jaxpr/scatter-add | solution.py:26
  136.7 7.4 %broadcast_select_fusion.4 = f32[64,128,256]{2,1,0:T(8,128)} fusion(pred[64]{0:T(512)(128)(4,1)S(1)} %get-tuple-element.447, bf16[64,128,256]{2,1,0:T(8,128)(2,1)} %gather_fusion, pred[64]{0:T(512)(128)(4,1)S(1)} %get-tuple-element.449, bf16[256,128,128]{2,1,0:T(8,128)(2,1)} %get-tuple-element.486, s32[]{:T(128)S(6)} %select_n.117), kind=kOutput, calls=%fused_computation.6.clone.1 | convolution fusion | flops 541065216 | bytes 14680196 | tf_op jit(solution)/shard_map/while/body/eval_jaxpr/sab,sbf->saf/dot_general | solution.py:23
  144.2 19.6 %scatter_fusion = f32[128,128,256]{2,1,0:T(8,128)} fusion(f32[128,128,256]{2,1,0:T(8,128)} %get-tuple-element.472, s32[64]{0:T(128)S(1)} %compare_select_fusion.8, f32[64,128,256]{2,1,0:T(8,128)} %broadcast_select_fusion.4), kind=kCustom, calls=%fused_computation.2.clone.clone.1 | custom fusion | flops 2097152 | bytes 25166080 | tf_op jit(solution)/shard_map/while/body/eval_jaxpr/scatter-add | solution.py:26
  163.9 179.0 %reduce-scatter.3.cloned.1.call-done = f32[1024,256]{1,0:T(8,128)} async-done(((f32[16384,256]{1,0:T(8,128)}), f32[1024,256]{1,0:T(8,128)}) %reduce-scatter.3.cloned.1.call-update) | async-done | bytes 1048592 | tf_op jit(solution)/shard_map/reduce_scatter | solution.py:49
  346.7 12.1 %copy.11 = bf16[1,1,256,128,128]{3,4,2,1,0:T(8,128)(2,1)} copy(bf16[1,1,256,128,128]{4,3,2,1,0:T(8,128)(2,1)} %bitcast.18) | data formatting | bytes 16777216 | tf_op args[1]
  359.9 60.8 %all-gather.5.cloned.1.call-done = bf16[16384,256]{1,0:T(8,128)(2,1)} async-done(((bf16[1024,256]{1,0:T(8,128)(2,1)}), bf16[16384,256]{1,0:T(8,128)(2,1)}) %all-gather.5.cloned.1.call-update) | async-done | bytes 8388624 | tf_op jit(solution)/shard_map/all_gather | solution.py:68
  420.9 107.5 %while.29 = (s32[]{:T(128)}, f32[16,128,256]{2,1,0:T(8,128)S(1)}, s32[256]{0:T(256)S(1)}, s32[]{:T(128)}, bf16[256,128,128]{1,2,0:T(8,128)(2,1)}, /*index=5*/s32...) while((s32[]{:T(128)}, f32[16,128,256]{2,1,0:T(8,128)S(1)}, ...), condition=%wide.region_6.7_spmd.clone, body=%wide.region_4.6_spmd.clone.sunk | while | flops 543164096 | bytes 48240816 | solution.py:30
  421.7 6.2 %gather_fusion.1 = bf16[64,128,256]{2,1,0:T(8,128)(2,1)} fusion(bf16[128,128,256]{2,1,0:T(8,128)(2,1)} %get-tuple-element.521, s32[1024]{0:T(1024)S(1)} %pad_clamp_fusion.5), kind=kCustom, calls=%fused_computation.1.clone.clone.1 | custom fusion | bytes 8388864 | tf_op jit(solution)/shard_map/while/body/eval_jaxpr/jit(_take)/gather | solution.py:22
  427.9 7.4 %broadcast_select_fusion.5 = f32[64,128,256]{2,1,0:T(8,128)} fusion(pred[64]{0:T(512)(128)(4,1)S(1)} %get-tuple-element.457, bf16[64,128,256]{2,1,0:T(8,128)(2,1)} %gather_fusion.1, pred[64]{0:T(512)(128)(4,1)S(1)} %get-tuple-element.459, bf16[256,128,128]{1,2,0:T(8,128)(2,1)} %get-tuple-element.519, s32[]{:T(128)S(6)} %select_n.121), kind=kOutput, calls=%fused_computation.20.clone.1 | convolution fusion | flops 541065216 | bytes 14680196 | tf_op jit(solution)/shard_map/while/body/eval_jaxpr/sab,saf->sbf/dot_general | solution.py:23
  435.3 12.5 %scatter_fusion.1 = f32[16,128,256]{2,1,0:T(8,128)S(1)} fusion(f32[16,128,256]{2,1,0:T(8,128)S(1)} %get-tuple-element.505, s32[64]{0:T(128)S(1)} %compare_select_fusion.9, f32[64,128,256]{2,1,0:T(8,128)} %broadcast_select_fusion.5), kind=kCustom, calls=%fused_computation.3.clone.clone.1 | custom fusion | flops 2097152 | bytes 25166080 | tf_op jit(solution)/shard_map/while/body/eval_jaxpr/scatter-add | solution.py:26
  448.6 6.2 %gather_fusion.1 = bf16[64,128,256]{2,1,0:T(8,128)(2,1)} fusion(bf16[128,128,256]{2,1,0:T(8,128)(2,1)} %get-tuple-element.521, s32[1024]{0:T(1024)S(1)} %pad_clamp_fusion.5), kind=kCustom, calls=%fused_computation.1.clone.clone.1 | custom fusion | bytes 8388864 | tf_op jit(solution)/shard_map/while/body/eval_jaxpr/jit(_take)/gather | solution.py:22
  454.8 7.4 %broadcast_select_fusion.5 = f32[64,128,256]{2,1,0:T(8,128)} fusion(pred[64]{0:T(512)(128)(4,1)S(1)} %get-tuple-element.457, bf16[64,128,256]{2,1,0:T(8,128)(2,1)} %gather_fusion.1, pred[64]{0:T(512)(128)(4,1)S(1)} %get-tuple-element.459, bf16[256,128,128]{1,2,0:T(8,128)(2,1)} %get-tuple-element.519, s32[]{:T(128)S(6)} %select_n.121), kind=kOutput, calls=%fused_computation.20.clone.1 | convolution fusion | flops 541065216 | bytes 14680196 | tf_op jit(solution)/shard_map/while/body/eval_jaxpr/sab,saf->sbf/dot_general | solution.py:23
  462.2 12.4 %scatter_fusion.1 = f32[16,128,256]{2,1,0:T(8,128)S(1)} fusion(f32[16,128,256]{2,1,0:T(8,128)S(1)} %get-tuple-element.505, s32[64]{0:T(128)S(1)} %compare_select_fusion.9, f32[64,128,256]{2,1,0:T(8,128)} %broadcast_select_fusion.5), kind=kCustom, calls=%fused_computation.3.clone.clone.1 | custom fusion | flops 2097152 | bytes 25166080 | tf_op jit(solution)/shard_map/while/body/eval_jaxpr/scatter-add | solution.py:26
  475.4 6.2 %gather_fusion.1 = bf16[64,128,256]{2,1,0:T(8,128)(2,1)} fusion(bf16[128,128,256]{2,1,0:T(8,128)(2,1)} %get-tuple-element.521, s32[1024]{0:T(1024)S(1)} %pad_clamp_fusion.5), kind=kCustom, calls=%fused_computation.1.clone.clone.1 | custom fusion | bytes 8388864 | tf_op jit(solution)/shard_map/while/body/eval_jaxpr/jit(_take)/gather | solution.py:22
  481.6 7.4 %broadcast_select_fusion.5 = f32[64,128,256]{2,1,0:T(8,128)} fusion(pred[64]{0:T(512)(128)(4,1)S(1)} %get-tuple-element.457, bf16[64,128,256]{2,1,0:T(8,128)(2,1)} %gather_fusion.1, pred[64]{0:T(512)(128)(4,1)S(1)} %get-tuple-element.459, bf16[256,128,128]{1,2,0:T(8,128)(2,1)} %get-tuple-element.519, s32[]{:T(128)S(6)} %select_n.121), kind=kOutput, calls=%fused_computation.20.clone.1 | convolution fusion | flops 541065216 | bytes 14680196 | tf_op jit(solution)/shard_map/while/body/eval_jaxpr/sab,saf->sbf/dot_general | solution.py:23
  489.1 12.5 %scatter_fusion.1 = f32[16,128,256]{2,1,0:T(8,128)S(1)} fusion(f32[16,128,256]{2,1,0:T(8,128)S(1)} %get-tuple-element.505, s32[64]{0:T(128)S(1)} %compare_select_fusion.9, f32[64,128,256]{2,1,0:T(8,128)} %broadcast_select_fusion.5), kind=kCustom, calls=%fused_computation.3.clone.clone.1 | custom fusion | flops 2097152 | bytes 25166080 | tf_op jit(solution)/shard_map/while/body/eval_jaxpr/scatter-add | solution.py:26
  502.3 6.2 %gather_fusion.1 = bf16[64,128,256]{2,1,0:T(8,128)(2,1)} fusion(bf16[128,128,256]{2,1,0:T(8,128)(2,1)} %get-tuple-element.521, s32[1024]{0:T(1024)S(1)} %pad_clamp_fusion.5), kind=kCustom, calls=%fused_computation.1.clone.clone.1 | custom fusion | bytes 8388864 | tf_op jit(solution)/shard_map/while/body/eval_jaxpr/jit(_take)/gather | solution.py:22
  508.5 7.4 %broadcast_select_fusion.5 = f32[64,128,256]{2,1,0:T(8,128)} fusion(pred[64]{0:T(512)(128)(4,1)S(1)} %get-tuple-element.457, bf16[64,128,256]{2,1,0:T(8,128)(2,1)} %gather_fusion.1, pred[64]{0:T(512)(128)(4,1)S(1)} %get-tuple-element.459, bf16[256,128,128]{1,2,0:T(8,128)(2,1)} %get-tuple-element.519, s32[]{:T(128)S(6)} %select_n.121), kind=kOutput, calls=%fused_computation.20.clone.1 | convolution fusion | flops 541065216 | bytes 14680196 | tf_op jit(solution)/shard_map/while/body/eval_jaxpr/sab,saf->sbf/dot_general | solution.py:23
  516.0 12.4 %scatter_fusion.1 = f32[16,128,256]{2,1,0:T(8,128)S(1)} fusion(f32[16,128,256]{2,1,0:T(8,128)S(1)} %get-tuple-element.505, s32[64]{0:T(128)S(1)} %compare_select_fusion.9, f32[64,128,256]{2,1,0:T(8,128)} %broadcast_select_fusion.5), kind=kCustom, calls=%fused_computation.3.clone.clone.1 | custom fusion | flops 2097152 | bytes 25166080 | tf_op jit(solution)/shard_map/while/body/eval_jaxpr/scatter-add | solution.py:26
  529.8 38.8 %psum.15 = f32[256]{0:T(256)S(1)} all-reduce(f32[256]{0:T(256)S(1)} %get-tuple-element.355), channel_id=1, replica_groups=mesh['row'=2,'col'=16] {'row','col'}, use_global_device_ids=true, to_apply=%region_10.11 | all-reduce | flops 256 | bytes 2048 | tf_op jit(solution)/shard_map/psum | solution.py:61
  570.9 12.7 %reduce-scatter.5.cloned.1.call-done = f32[2048,128]{1,0:T(8,128)} async-done(((f32[2048,256]{1,0:T(8,128)}), f32[2048,128]{1,0:T(8,128)}) %reduce-scatter.5.cloned.1.call-update) | async-done | bytes 1048592 | tf_op jit(solution)/shard_map/reduce_scatter | solution.py:74
  (58 shorter events, 21.7 us)
Async XLA Ops:
  7.2 335.7 %copy-start = (bf16[256,256]{1,0:T(8,128)(2,1)S(1)}, bf16[256,256]{1,0:T(8,128)(2,1)}, u32[]{:S(2)}) copy-start(bf16[256,256]{1,0:T(8,128)(2,1)} %param.15) | copy-start | bytes 393220
  7.2 26.4 %all-gather.3.cloned.1.call-start = ((), (), s32[]{:S(2)}) async-start(), calls=%async_computation.2 | async-start | bytes 1572864 | tf_op jit(solution)/shard_map/all_gather | solution.py:41
  7.9 334.9 %reduce-scatter.3.cloned.1.call-start = ((), (), s32[]{:S(2)}) async-start(), calls=%async_computation.3 | async-start | bytes 17825792 | tf_op jit(solution)/shard_map/reduce_scatter | solution.py:49
  33.6 7.8 %copy-start.3 = (bf16[2048,256]{1,0:T(8,128)(2,1)S(1)}, bf16[2048,256]{1,0:T(8,128)(2,1)}, u32[]{:S(2)}) copy-start(bf16[2048,256]{1,0:T(8,128)(2,1)} %all-gather.3.cloned.1.call-done) | copy-start | bytes 3145732
  163.8 179.1 %copy-start.5 = (bf16[1024,256]{1,0:T(8,128)(2,1)S(1)}, bf16[1024,256]{1,0:T(8,128)(2,1)}, u32[]{:S(2)}) copy-start(bf16[1024,256]{1,0:T(8,128)(2,1)} %param.17) | copy-start | bytes 1572868
  163.8 179.1 %copy-start.6 = (f32[256]{0:T(256)S(1)}, f32[256]{0:T(256)}, u32[]{:S(2)}) copy-start(f32[256]{0:T(256)} %param.16) | copy-start | bytes 3076
  163.8 256.9 %all-gather.5.cloned.1.call-start = ((), (), s32[]{:S(2)}) async-start(), calls=%async_computation.4 | async-start | bytes 8912896 | tf_op jit(solution)/shard_map/all_gather | solution.py:68
  346.7 12.1 %copy-start.4 = (f32[1024,256]{1,0:T(8,128)S(1)}, f32[1024,256]{1,0:T(8,128)}, u32[]{:S(2)}) copy-start(f32[1024,256]{1,0:T(8,128)} %reduce-scatter.3.cloned.1.call-done) | copy-start | bytes 3145732
  346.7 222.5 %all-reduce.2.cloned.1.call-start = ((), (), s32[]{:S(2)}) async-start(), calls=%async_computation.6 | async-start | bytes 524288 | tf_op jit(solution)/shard_map/psum | solution.py:61
  359.9 223.7 %reduce-scatter.5.cloned.1.call-start = ((), (), s32[]{:S(2)}) async-start(), calls=%async_computation.5 | async-start | bytes 3145728 | tf_op jit(solution)/shard_map/reduce_scatter | solution.py:74
  528.4 1.3 copy-start.2
  528.4 57.2 %copy-start.1 = (bf16[256,256]{1,0:T(8,128)(2,1)S(1)}, bf16[256,256]{1,0:T(8,128)(2,1)}, u32[]{:S(2)}) copy-start(bf16[256,256]{1,0:T(8,128)(2,1)} %param.15) | copy-start | bytes 393220
Sparse Core Ops, SparseCore 0:
  9.6 23.9 all-gather.2
  163.9 178.8 reduce-scatter.2
  346.8 73.8 all-gather.4
  426.7 123.2 all-reduce.1
  552.1 31.4 reduce-scatter.4
where the time goes:
time: 594 us; the launch traced here: 592 us
  waiting for transfers between devices  278 us (47%)
  other arithmetic  139 us (23%)
  matrix products  64 us (11%)
  local copies, waits for them, and re-layouts  58 us (10%)
  blocking collectives  38.8 us (7%)
  between operations  13.8 us (2%)
    reduce_scatter x1, waiting for transfers between devices, on_device(): lax.psum_scatter(partial_value, 'col', scatter_dimension=0, tiled=True)  179 us
    scatter-add x8, other arithmetic, one_group(): return totals.at[put_to].add(products)  128 us
    all_gather x1, waiting for transfers between devices, on_device(): grad_tile = lax.all_gather(grad_agg, 'col', axis=0, tiled=True)  60.8 us
    dot_general x8, matrix products, one_group(): jnp.einsum(pattern, slab_vals, picked, preferred_element_type=jnp.float32)  59.2 us
    psum x1, blocking collectives, on_device(): weight_sum, bias_sum = lax.psum((weight_term, bias_term), ('row', 'col'))  38.8 us
    gather x8, local copies, waits for them, and re-layouts, one_group(): picked = jnp.take(source, take_from, axis=0)  35.8 us
    all_gather x1, waiting for transfers between devices, on_device(): feat_tile = lax.all_gather(features, 'row', axis=1, tiled=True)  24.8 us
    unnamed x15, local copies, waits for them, and re-layouts  13.4 us
  transfers between devices with their start and end apart: 5, of which 4 were waited for; matrix products, arithmetic and copies ran while one was open for 21% of the time, Pallas kernels for 0%

commit v1 on v0

v1 whole, which is shorter than its diff:
```python
import functools

import jax
import jax.numpy as jnp
from jax import lax
from jax.experimental import pallas as pl
from jax.experimental.pallas import tpu as pltpu
from jax.sharding import PartitionSpec as P

BF16 = jnp.bfloat16
F32 = jnp.float32
GROUP = 32
VMEM_LIMIT = 56 * 1024 * 1024


def forward_kernel(live, dst, src, vals, feats, keep, send, totals):
    turn = pl.program_id(0)
    half = keep.shape[0]

    @pl.when(turn == 0)
    def _():
        def clear(at, _):
            totals[at] = jnp.zeros(totals.shape[1:], F32)
            return 0

        lax.fori_loop(0, totals.shape[0], clear, 0)

    @pl.when(turn * GROUP < live[0])
    def _():
        for u in range(GROUP):
            slot = turn * GROUP + u
            to = dst[slot]
            totals[to] += jnp.dot(vals[u], feats[src[slot]], preferred_element_type=F32)

    @pl.when(turn == pl.num_programs(0) - 1)
    def _():
        def write(at, _):
            keep[at] = totals[at].astype(BF16)
            send[at] = totals[half + at].astype(BF16)
            return 0

        lax.fori_loop(0, half, write, 0)


def forward_blocks(live, dst, src, vals, feats, rows):
    slots, size = vals.shape[0], vals.shape[1]
    width = feats.shape[2]
    half = rows // 2
    last = lambda live: jnp.maximum((live[0] + GROUP - 1) // GROUP - 1, 0)
    whole = lambda shape: pl.BlockSpec(shape, lambda t, *_: (0,) * len(shape))
    part = jax.ShapeDtypeStruct((half, size, width), BF16)
    return pl.pallas_call(
        forward_kernel,
        grid_spec=pltpu.PrefetchScalarGridSpec(
            num_scalar_prefetch=3,
            grid=(slots // GROUP,),
            in_specs=[
                pl.BlockSpec((GROUP, size, size), lambda t, live, *_: (jnp.minimum(t, last(live)), 0, 0)),
                whole(feats.shape),
            ],
            out_specs=[whole(part.shape), whole(part.shape)],
            scratch_shapes=[pltpu.VMEM((rows + 1, size, width), F32)],
        ),
        out_shape=[part, part],
        compiler_params=pltpu.CompilerParams(vmem_limit_bytes=VMEM_LIMIT),
        cost_estimate=pl.CostEstimate(
            flops=8 * slots * size * size * width, bytes_accessed=4 * vals.size, transcendentals=0
        ),
        name="forward_blocks",
    )(live, dst, src, vals, feats)


def backward_kernel(live, dst, src, vals, grads, out, totals):
    turn = pl.program_id(0)

    @pl.when(turn == 0)
    def _():
        def clear(at, _):
            totals[at] = jnp.zeros(totals.shape[1:], F32)
            return 0

        lax.fori_loop(0, totals.shape[0], clear, 0)

    @pl.when(turn * GROUP < live[0])
    def _():
        for u in range(GROUP):
            slot = turn * GROUP + u
            to = dst[slot]
            totals[to] += jnp.dot(grads[src[slot]], vals[u], preferred_element_type=F32)

    @pl.when(turn == pl.num_programs(0) - 1)
    def _():
        def write(at, _):
            out[at] = totals[at].T.astype(out.dtype)
            return 0

        lax.fori_loop(0, out.shape[0], write, 0)


def backward_blocks(live, dst, src, vals, grads, cols, kind):
    slots, size = vals.shape[0], vals.shape[1]
    width = grads.shape[1]
    last = lambda live: jnp.maximum((live[0] + GROUP - 1) // GROUP - 1, 0)
    whole = lambda shape: pl.BlockSpec(shape, lambda t, *_: (0,) * len(shape))
    result = jax.ShapeDtypeStruct((cols, size, width), kind)
    return pl.pallas_call(
        backward_kernel,
        grid_spec=pltpu.PrefetchScalarGridSpec(
            num_scalar_prefetch=3,
            grid=(slots // GROUP,),
            in_specs=[
                pl.BlockSpec((GROUP, size, size), lambda t, live, *_: (jnp.minimum(t, last(live)), 0, 0)),
                whole(grads.shape),
            ],
            out_specs=whole(result.shape),
            scratch_shapes=[pltpu.VMEM((cols + 1, width, size), F32)],
        ),
        out_shape=result,
        compiler_params=pltpu.CompilerParams(vmem_limit_bytes=VMEM_LIMIT),
        cost_estimate=pl.CostEstimate(
            flops=8 * slots * size * size * width, bytes_accessed=4 * vals.size, transcendentals=0
        ),
        name="backward_blocks",
    )(live, dst, src, vals, grads)


def dense_kernel(
    first, keep_a, got_a, keep_b, got_b, cot, weight, bias, out, grad_a, grad_b, terms
):
    half = keep_a.shape[1]
    size = grad_a.shape[2]
    at_a = pl.multiple_of(first[0] * half, half)
    at_b = pl.multiple_of((1 - first[0]) * half, half)
    total = lambda x, y: (x[...].astype(F32) + y[...].astype(F32)).astype(BF16)
    agg_a, agg_b = total(keep_a, got_a), total(keep_b, got_b)
    weight_a, weight_b = weight[pl.ds(at_a, half), :], weight[pl.ds(at_b, half), :]
    preact = jnp.dot(agg_a, weight_a, preferred_element_type=F32)
    preact += jnp.dot(agg_b, weight_b, preferred_element_type=F32)
    preact += bias[...]
    gate = jax.nn.sigmoid(preact)
    out[...] = (preact * gate).astype(BF16)
    slope = gate * (1.0 + preact * (1.0 - gate))
    grad_pre = (cot[...].astype(F32) * slope).astype(BF16)
    over_rows = (((0,), (0,)), ((), ()))
    over_outputs = (((1,), (1,)), ((), ()))
    terms[pl.ds(at_a, half), :] = lax.dot_general(agg_a, grad_pre, over_rows, preferred_element_type=F32)
    terms[pl.ds(at_b, half), :] = lax.dot_general(agg_b, grad_pre, over_rows, preferred_element_type=F32)
    sums = jnp.sum(grad_pre.astype(F32), axis=0, keepdims=True)
    terms[2 * half :, :] = jnp.broadcast_to(sums, (terms.shape[0] - 2 * half, sums.shape[1]))
    turned_a = lax.dot_general(weight_a, grad_pre, over_outputs, preferred_element_type=F32).astype(BF16)
    turned_b = lax.dot_general(weight_b, grad_pre, over_outputs, preferred_element_type=F32).astype(BF16)
    for at in range(grad_a.shape[0]):
        grad_a[at] = turned_a[:, at * size : (at + 1) * size]
        grad_b[at] = turned_b[:, at * size : (at + 1) * size]


def dense(first, keep_a, got_a, keep_b, got_b, cot, weight, bias, size):
    rows, half = keep_a.shape
    width = cot.shape[1]
    vmem = pl.BlockSpec(memory_space=pltpu.VMEM)
    turned = jax.ShapeDtypeStruct((rows // size, half, size), BF16)
    return pl.pallas_call(
        dense_kernel,
        in_specs=[pl.BlockSpec(memory_space=pltpu.SMEM)] + [vmem] * 7,
        out_specs=[vmem] * 4,
        out_shape=[
            jax.ShapeDtypeStruct((rows, width), BF16),
            turned,
            turned,
            jax.ShapeDtypeStruct((2 * half + 8, width), F32),
        ],
        compiler_params=pltpu.CompilerParams(vmem_limit_bytes=VMEM_LIMIT),
        cost_estimate=pl.CostEstimate(
            flops=8 * rows * width * width, bytes_accessed=8 * rows * width, transcendentals=rows * width
        ),
        name="dense_layer",
    )(first, keep_a, got_a, keep_b, got_b, cot, weight, bias)


def swap(array, axis, bit):
    return lax.ppermute(array, axis, [(at, at ^ bit) for at in range(lax.axis_size(axis))])


def add(x, y):
    return (x.astype(F32) + y.astype(F32)).astype(BF16)


def scatter_sum(keep, send):
    count = lax.axis_size("col")
    bit = 1
    while True:
        got = swap(send, "col", bit)
        bit *= 2
        if bit == count:
            return keep, got
        half = keep.shape[0] // 2
        keep, send = add(keep[:half], got[:half]), add(keep[half:], got[half:])


def gather(part):
    bit = lax.axis_size("col") // 2
    while bit:
        part = jnp.concatenate([part, swap(part, "col", bit)], axis=0)
        bit //= 2
    return part


def on_device(features, block_values, block_coords, live_blocks, weight, bias, cotangent):
    vals = block_values[0, 0]
    size = vals.shape[1]
    live = live_blocks[0]
    row_count, col_count = lax.axis_size("row"), lax.axis_size("col")
    me = lax.axis_index("col")
    width = weight.shape[0]
    half = width // 2
    per_device = cotangent.shape[0] // size
    rows = per_device * col_count
    cols = features.shape[0] // size

    row_ids, col_ids = block_coords[0, 0, 0], block_coords[0, 0, 1]
    owner = (row_ids // per_device) ^ me
    place = jnp.zeros_like(owner)
    bit, turned = 1, col_count // 2
    while bit < col_count:
        place = place + jnp.where((owner & bit) != 0, turned, 0)
        bit, turned = bit * 2, turned // 2
    row_place = place * per_device + row_ids % per_device
    alive = jnp.arange(vals.shape[0], dtype=jnp.int32) < live[0]
    row_dst = jnp.where(alive, row_place, rows)
    col_dst = jnp.where(alive, col_ids, cols)

    if row_count == 2:
        first = lax.axis_index("row").reshape(1)
        feats_a, feats_b = features, swap(features, "row", 1)
    else:
        first = jnp.zeros((1,), jnp.int32)
        feats = lax.all_gather(features, "row", axis=1, tiled=True)
        feats_a, feats_b = feats[:, :half], feats[:, half:]

    def aggregate_terms(feats):
        keep, send = forward_blocks(live, row_dst, col_ids, vals, feats.reshape(cols, size, half), rows)
        keep, got = scatter_sum(keep, send)
        return keep.reshape(-1, half), got.reshape(-1, half)

    keep_a, got_a = aggregate_terms(feats_a)
    keep_b, got_b = aggregate_terms(feats_b)
    out, grad_a, grad_b, terms = dense(
        first, keep_a, got_a, keep_b, got_b, cotangent, weight, bias.reshape(1, -1), size
    )
    sums = lax.psum(terms, ("row", "col")) * (cols * size * col_count) ** (-0.5)

    def input_grad(grad, kind):
        return backward_blocks(live, col_dst, row_place, vals, gather(grad), cols, kind).reshape(-1, half)

    if row_count == 2:
        theirs = swap(input_grad(grad_b, BF16), "row", 1)
        grad_x = (input_grad(grad_a, F32) + theirs.astype(F32)).astype(BF16)
    else:
        partial_x = jnp.concatenate([input_grad(grad_a, F32), input_grad(grad_b, F32)], axis=1)
        grad_x = lax.psum_scatter(partial_x, "row", scatter_dimension=1, tiled=True).astype(BF16)
    return out, grad_x, sums[:width], sums[width]


def solution(mesh):
    in_specs = (
        P("col", "row"),
        P("row", "col", None, None, None),
        P("row", "col", None, None),
        P("row", "col"),
        P(),
        P(),
        P(("row", "col"), None),
    )
    out_specs = (P(("row", "col"), None), P("col", "row"), P(), P())
    return jax.shard_map(
        on_device, mesh=mesh, in_specs=in_specs, out_specs=out_specs, check_vma=False
    )
```

time: 594 us -> 385 us (0.65)
  the two profiles are of different devices: /device:TPU:0 before, /device:TPU:14 now
where the time goes in v1:
time: 385 us; the launch traced here: 383 us
  waiting for transfers between devices  266 us (69%)
  Pallas kernels  52.4 us (14%)
  local copies, waits for them, and re-layouts  19.3 us (5%)
  starting transfers between devices  16.7 us (4%)
  between operations  14.9 us (4%)
  other arithmetic  13.9 us (4%)
    ppermute x18, waiting for transfers between devices, swap(): lax.ppermute(array, axis, [(at, at ^ bit) for at in range(lax.axis_size(a...  141 us
    psum x1, waiting for transfers between devices, on_device(): sums = lax.psum(terms, ('row', 'col')) * (cols * size * col_count) ** (-0.5)  125 us
    pallas_call x2, Pallas kernels, backward_blocks(): pl.pallas_call(backward_kernel, grid_spec=pltpu.PrefetchScalarGridSpec(nu...  25 us
    pallas_call x2, Pallas kernels, forward_blocks(): pl.pallas_call(forward_kernel, grid_spec=pltpu.PrefetchScalarGridSpec(num...  23.7 us
    ppermute x18, starting transfers between devices, swap(): lax.ppermute(array, axis, [(at, at ^ bit) for at in range(lax.axis_size(a...  16.6 us
    unnamed x29, local copies, waits for them, and re-layouts  11.5 us
  transfers between devices with their start and end apart: 19, of which 11 were waited for; matrix products, arithmetic and copies ran while one was open for 7% of the time, Pallas kernels for 13%

profile of v1, /device:TPU:14, one launch (start us, length us, event | category | flops | bytes accessed | tf_op | source)
XLA Modules:
  0.0 382.8 jit_solution(6520044701751663475)
XLA Ops:
  8.4 1.3 fusion.8
  10.4 11.7 %forward_blocks.2 = (bf16[64,128,128]{2,1,0:T(8,128)(2,1)}, bf16[64,128,128]{2,1,0:T(8,128)(2,1)}) custom-call(s32[1]{0:T(128)} %bitcast.19.live, s32[256]{0:T(256)} %get-tuple-element.20.dst, s32[256]{0:T(256)} %bitcast.27, bf16[256,128,128]{2,1,0:T(8,128)(2,1)} %bitcast.32, bf16[16,128,128]{2,1,0:T(8,128)(2,1)} %bitcast.36), custom_call_target="tpu_custom_call" | custom-call | flops 4294967296 | bytes 16777216 | tf_op jit(solution)/shard_map/forward_blocks/pallas_call | solution.py:52
  22.9 11.9 %forward_blocks.3 = (bf16[64,128,128]{2,1,0:T(8,128)(2,1)}, bf16[64,128,128]{2,1,0:T(8,128)(2,1)}) custom-call(s32[1]{0:T(128)} %bitcast.20.live, s32[256]{0:T(256)} %get-tuple-element.20.dst, s32[256]{0:T(256)} %bitcast.28, bf16[256,128,128]{2,1,0:T(8,128)(2,1)} %bitcast.33, bf16[16,128,128]{2,1,0:T(8,128)(2,1)} %bitcast.37), custom_call_target="tpu_custom_call" | custom-call | flops 4294967296 | bytes 16777216 | tf_op jit(solution)/shard_map/forward_blocks/pallas_call | solution.py:52
  35.7 3.5 collective-permute-done.5
  39.2 1.1 add_convert_fusion.1
  40.4 21.3 %collective-permute-done.1 = bf16[32,128,128]{2,1,0:T(8,128)(2,1)S(1)} collective-permute-done((bf16[32,128,128]{2,1,0:T(8,128)(2,1)S(1)}, bf16[32,128,128]{2,1,0:T(8,128)(2,1)S(1)}, u32[]{:S(2)}, u32[]{:S(2)}) %collective-permute-start.1) | collective-permute-done | bytes 1048608 | tf_op jit(solution)/shard_map/ppermute | solution.py:181
  62.2 21.6 %collective-permute-done.6 = bf16[32,128,128]{2,1,0:T(8,128)(2,1)S(1)} collective-permute-done((bf16[32,128,128]{2,1,0:T(8,128)(2,1)S(1)}, bf16[32,128,128]{2,1,0:T(8,128)(2,1)S(1)}, u32[]{:S(2)}, u32[]{:S(2)}) %collective-permute-start.6) | collective-permute-done | bytes 1048608 | tf_op jit(solution)/shard_map/ppermute | solution.py:181
  85.1 2.6 collective-permute-start.3
  87.7 13.5 %collective-permute-done.7 = bf16[16,128,128]{2,1,0:T(8,128)(2,1)S(1)} collective-permute-done((bf16[16,128,128]{2,1,0:T(8,128)(2,1)S(1)}, bf16[16,128,128]{2,1,0:T(8,128)(2,1)S(1)}, u32[]{:S(2)}, u32[]{:S(2)}) %collective-permute-start.7) | collective-permute-done | bytes 524320 | tf_op jit(solution)/shard_map/ppermute | solution.py:181
  102.0 4.2 %collective-permute-start.8 = (bf16[8,128,128]{2,1,0:T(8,128)(2,1)S(1)}, bf16[8,128,128]{2,1,0:T(8,128)(2,1)S(1)}, u32[]{:S(2)}, u32[]{:S(2)}) collective-permute-start(bf16[8,128,128]{2,1,0:T(8,128)(2,1)S(1)} %get-tuple-element.30), channel_id=1, source_target_pairs={{0,8},{1,9},{2,10},{3,11},{4,12},{5,13},{6,14},{7,15},{8,0},{9,1},... | collective-permute-start | bytes 786440 | tf_op jit(solution)/shard_map/ppermute | solution.py:181
  106.2 8.6 %collective-permute-done.8 = bf16[8,128,128]{2,1,0:T(8,128)(2,1)S(1)} collective-permute-done((bf16[8,128,128]{2,1,0:T(8,128)(2,1)S(1)}, bf16[8,128,128]{2,1,0:T(8,128)(2,1)S(1)}, u32[]{:S(2)}, u32[]{:S(2)}) %collective-permute-start.8) | collective-permute-done | bytes 262176 | tf_op jit(solution)/shard_map/ppermute | solution.py:181
  115.5 3.7 dense_layer.1
  119.3 3.4 collective-permute-start.13
  122.7 11.2 %collective-permute-done.13 = bf16[8,128,128]{2,1,0:T(8,128)(2,1)S(1)} collective-permute-done((bf16[8,128,128]{2,1,0:T(8,128)(2,1)}, bf16[8,128,128]{2,1,0:T(8,128)(2,1)S(1)}, u32[]{:S(2)}, u32[]{:S(2)}) %collective-permute-start.13) | collective-permute-done | bytes 262176 | tf_op jit(solution)/shard_map/ppermute | solution.py:181
  135.0 2.6 collective-permute-start.14
  138.4 17.6 %collective-permute-done.9 = bf16[8,128,128]{2,1,0:T(8,128)(2,1)S(1)} collective-permute-done((bf16[8,128,128]{2,1,0:T(8,128)(2,1)}, bf16[8,128,128]{2,1,0:T(8,128)(2,1)S(1)}, u32[]{:S(2)}, u32[]{:S(2)}) %collective-permute-start.9) | collective-permute-done | bytes 262176 | tf_op jit(solution)/shard_map/ppermute | solution.py:181
  156.0 1.1 pad_maximum_fusion.4
  158.3 12.2 %collective-permute-done.10 = bf16[16,128,128]{2,1,0:T(8,128)(2,1)S(1)} collective-permute-done((bf16[16,128,128]{2,1,0:T(8,128)(2,1)S(1)}, bf16[16,128,128]{2,1,0:T(8,128)(2,1)S(1)}, u32[]{:S(2)}, u32[]{:S(2)}) %collective-permute-start.10) | collective-permute-done | bytes 524320 | tf_op jit(solution)/shard_map/ppermute | solution.py:181
  171.6 11.9 %collective-permute-done.15 = bf16[32,128,128]{2,1,0:T(8,128)(2,1)S(1)} collective-permute-done((bf16[32,128,128]{2,1,0:T(8,128)(2,1)S(1)}, bf16[32,128,128]{2,1,0:T(8,128)(2,1)S(1)}, u32[]{:S(2)}, u32[]{:S(2)}) %collective-permute-start.15) | collective-permute-done | bytes 1048608 | tf_op jit(solution)/shard_map/ppermute | solution.py:181
  183.5 1.5 pad_maximum_fusion.1
  185.0 19.4 %collective-permute-done.11 = bf16[32,128,128]{2,1,0:T(8,128)(2,1)S(1)} collective-permute-done((bf16[32,128,128]{2,1,0:T(8,128)(2,1)S(1)}, bf16[32,128,128]{2,1,0:T(8,128)(2,1)S(1)}, u32[]{:S(2)}, u32[]{:S(2)}) %collective-permute-start.11) | collective-permute-done | bytes 1048608 | tf_op jit(solution)/shard_map/ppermute | solution.py:181
  204.4 1.6 pad_maximum_fusion
  206.6 1.9 constant_dynamic-update-slice_fusion.4
  208.5 124.8 %all-reduce.2.cloned.1.call-done = f32[264,256]{1,0:T(8,128)} async-done(((f32[264,256]{1,0:T(8,128)}), f32[264,256]{1,0:T(8,128)}) %all-reduce.2.cloned.1.call-update) | async-done | bytes 270352 | tf_op jit(solution)/shard_map/psum | solution.py:250
  335.5 1.7 constant_dynamic-update-slice_fusion.3
  339.6 1.1 constant_dynamic-update-slice_fusion.1
  341.7 3.2 constant_dynamic-update-slice_fusion.5.grads
  344.9 12.7 %backward_blocks.3 = bf16[16,128,128]{2,1,0:T(8,128)(2,1)} custom-call(s32[1]{0:T(128)} %bitcast.22.live, s32[256]{0:T(256)} %fusion.5.dst, s32[256]{0:T(256)} %get-tuple-element.21.src, bf16[256,128,128]{2,1,0:T(8,128)(2,1)} %bitcast.34, bf16[128,128,128]{2,1,0:T(8,128)(2,1)} %constant_dynamic-update-slice_fusion.5.grads), custom_call_target="tpu_custom_call" | custom-call | flops 4294967296 | bytes 16777216 | tf_op jit(solution)/shard_map/backward_blocks/pallas_call | solution.py:106
  357.6 2.0 constant_dynamic-update-slice_fusion.grads
  359.5 2.0 copy-done.6
  361.5 12.3 %backward_blocks.2 = f32[16,128,128]{2,1,0:T(8,128)} custom-call(s32[1]{0:T(128)} %bitcast.21.live, s32[256]{0:T(256)} %fusion.5.dst, s32[256]{0:T(256)} %get-tuple-element.21.src, bf16[256,128,128]{2,1,0:T(8,128)(2,1)} %bitcast.35, bf16[128,128,128]{2,1,0:T(8,128)(2,1)} %copy-done.6), custom_call_target="tpu_custom_call" | custom-call | flops 4294967296 | bytes 16777216 | tf_op jit(solution)/shard_map/backward_blocks/pallas_call | solution.py:106
  373.8 2.1 fusion
  (62 shorter events, 16.6 us)
Async XLA Ops:
  7.2 326.1 %all-reduce.2.cloned.1.call-start = ((), (), s32[]{:S(2)}) async-start(), calls=%async_computation | async-start | bytes 540672 | tf_op jit(solution)/shard_map/psum | solution.py:250
  7.2 14.9 %collective-permute-start.4 = (bf16[2048,128]{1,0:T(8,128)(2,1)}, bf16[2048,128]{1,0:T(8,128)(2,1)S(1)}, u32[]{:S(2)}, u32[]{:S(2)}) collective-permute-start(bf16[2048,128]{1,0:T(8,128)(2,1)} %param.7), channel_id=1, source_target_pairs={{0,16},{16,0},{1,17},{17,1},{2,18},{18,2},{3,19},{19,3},{4,20},{20... | collective-permute-start | bytes 1572872 | tf_op jit(solution)/shard_map/ppermute | solution.py:181
  22.1 12.7 %collective-permute-start = (bf16[64,128,128]{2,1,0:T(8,128)(2,1)}, bf16[64,128,128]{2,1,0:T(8,128)(2,1)S(1)}, u32[]{:S(2)}, u32[]{:S(2)}) collective-permute-start(bf16[64,128,128]{2,1,0:T(8,128)(2,1)} %get-tuple-element.13), channel_id=1, source_target_pairs={{0,1},{1,0},{2,3},{3,2},{4,5},{5,4},{6,7},{7,6},{8,9},{9,8},{10,11... | collective-permute-start | bytes 6291464 | tf_op jit(solution)/shard_map/ppermute | solution.py:181
  22.1 0.8 copy-start.8
  22.9 11.9 %copy-start.4 = (bf16[64,128,128]{2,1,0:T(8,128)(2,1)S(1)}, bf16[64,128,128]{2,1,0:T(8,128)(2,1)}, u32[]{:S(2)}) copy-start(bf16[64,128,128]{2,1,0:T(8,128)(2,1)} %get-tuple-element.12) | copy-start | bytes 6291460
  34.8 4.4 %collective-permute-start.5 = (bf16[64,128,128]{2,1,0:T(8,128)(2,1)}, bf16[64,128,128]{2,1,0:T(8,128)(2,1)S(1)}, u32[]{:S(2)}, u32[]{:S(2)}) collective-permute-start(bf16[64,128,128]{2,1,0:T(8,128)(2,1)} %get-tuple-element.15), channel_id=1, source_target_pairs={{0,1},{1,0},{2,3},{3,2},{4,5},{5,4},{6,7},{7,6},{8,9},{9,8},{10,11... | collective-permute-start | bytes 6291464 | tf_op jit(solution)/shard_map/ppermute | solution.py:181
  34.9 4.4 %copy-start.3 = (bf16[64,128,128]{2,1,0:T(8,128)(2,1)S(1)}, bf16[64,128,128]{2,1,0:T(8,128)(2,1)}, u32[]{:S(2)}) copy-start(bf16[64,128,128]{2,1,0:T(8,128)(2,1)} %get-tuple-element.14) | copy-start | bytes 6291460
  35.7 26.0 %collective-permute-start.1 = (bf16[32,128,128]{2,1,0:T(8,128)(2,1)S(1)}, bf16[32,128,128]{2,1,0:T(8,128)(2,1)S(1)}, u32[]{:S(2)}, u32[]{:S(2)}) collective-permute-start(bf16[32,128,128]{2,1,0:T(8,128)(2,1)S(1)} %get-tuple-element.25), channel_id=1, source_target_pairs={{0,2},{1,3},{2,0},{3,1},{4,6},{5,7},{6,4},{7,5},{8,10},{9,11},{10,... | collective-permute-start | bytes 3145736 | tf_op jit(solution)/shard_map/ppermute | solution.py:181
  40.3 43.4 %collective-permute-start.6 = (bf16[32,128,128]{2,1,0:T(8,128)(2,1)S(1)}, bf16[32,128,128]{2,1,0:T(8,128)(2,1)S(1)}, u32[]{:S(2)}, u32[]{:S(2)}) collective-permute-start(bf16[32,128,128]{2,1,0:T(8,128)(2,1)S(1)} %get-tuple-element.23), channel_id=1, source_target_pairs={{0,2},{1,3},{2,0},{3,1},{4,6},{5,7},{6,4},{7,5},{8,10},{9,11},{10,... | collective-permute-start | bytes 3145736 | tf_op jit(solution)/shard_map/ppermute | solution.py:181
  62.0 22.2 %collective-permute-start.2 = (bf16[16,128,128]{2,1,0:T(8,128)(2,1)S(1)}, bf16[16,128,128]{2,1,0:T(8,128)(2,1)S(1)}, u32[]{:S(2)}, u32[]{:S(2)}) collective-permute-start(bf16[16,128,128]{2,1,0:T(8,128)(2,1)S(1)} %get-tuple-element.29), channel_id=1, source_target_pairs={{0,4},{1,5},{2,6},{3,7},{4,0},{5,1},{6,2},{7,3},{8,12},{9,13},{10,... | collective-permute-start | bytes 1572872 | tf_op jit(solution)/shard_map/ppermute | solution.py:181
  84.1 17.0 %collective-permute-start.7 = (bf16[16,128,128]{2,1,0:T(8,128)(2,1)S(1)}, bf16[16,128,128]{2,1,0:T(8,128)(2,1)S(1)}, u32[]{:S(2)}, u32[]{:S(2)}) collective-permute-start(bf16[16,128,128]{2,1,0:T(8,128)(2,1)S(1)} %get-tuple-element.27), channel_id=1, source_target_pairs={{0,4},{1,5},{2,6},{3,7},{4,0},{5,1},{6,2},{7,3},{8,12},{9,13},{10,... | collective-permute-start | bytes 1572872 | tf_op jit(solution)/shard_map/ppermute | solution.py:181
  85.1 21.2 %collective-permute-start.3 = (bf16[8,128,128]{2,1,0:T(8,128)(2,1)S(1)}, bf16[8,128,128]{2,1,0:T(8,128)(2,1)S(1)}, u32[]{:S(2)}, u32[]{:S(2)}) collective-permute-start(bf16[8,128,128]{2,1,0:T(8,128)(2,1)S(1)} %get-tuple-element.32), channel_id=1, source_target_pairs={{0,8},{1,9},{2,10},{3,11},{4,12},{5,13},{6,14},{7,15},{8,0},{9,1},... | collective-permute-start | bytes 786440 | tf_op jit(solution)/shard_map/ppermute | solution.py:181
  102.0 12.8 %collective-permute-start.8 = (bf16[8,128,128]{2,1,0:T(8,128)(2,1)S(1)}, bf16[8,128,128]{2,1,0:T(8,128)(2,1)S(1)}, u32[]{:S(2)}, u32[]{:S(2)}) collective-permute-start(bf16[8,128,128]{2,1,0:T(8,128)(2,1)S(1)} %get-tuple-element.30), channel_id=1, source_target_pairs={{0,8},{1,9},{2,10},{3,11},{4,12},{5,13},{6,14},{7,15},{8,0},{9,1},... | collective-permute-start | bytes 786440 | tf_op jit(solution)/shard_map/ppermute | solution.py:181
  106.2 8.6 %copy-start.9 = (bf16[8,128,128]{2,1,0:T(8,128)(2,1)}, bf16[8,128,128]{2,1,0:T(8,128)(2,1)S(1)}, u32[]{:S(2)}) copy-start(bf16[8,128,128]{2,1,0:T(8,128)(2,1)S(1)} %collective-permute-done.3) | copy-start | bytes 786436
  114.8 0.7 copy-start.10
  119.3 38.0 %copy-start.2 = (bf16[8,128,128]{2,1,0:T(8,128)(2,1)S(1)}, bf16[8,128,128]{2,1,0:T(8,128)(2,1)}, u32[]{:S(2)}) copy-start(bf16[8,128,128]{2,1,0:T(8,128)(2,1)} %get-tuple-element.18) | copy-start | bytes 786436
  119.3 51.2 %copy-start.1 = (bf16[8,128,128]{2,1,0:T(8,128)(2,1)S(1)}, bf16[8,128,128]{2,1,0:T(8,128)(2,1)}, u32[]{:S(2)}) copy-start(bf16[8,128,128]{2,1,0:T(8,128)(2,1)} %get-tuple-element.17) | copy-start | bytes 786436
  119.3 14.7 %collective-permute-start.13 = (bf16[8,128,128]{2,1,0:T(8,128)(2,1)}, bf16[8,128,128]{2,1,0:T(8,128)(2,1)S(1)}, u32[]{:S(2)}, u32[]{:S(2)}) collective-permute-start(bf16[8,128,128]{2,1,0:T(8,128)(2,1)} %get-tuple-element.18), channel_id=1, source_target_pairs={{0,8},{1,9},{2,10},{3,11},{4,12},{5,13},{6,14},{7,15},{8,0},{9,1},... | collective-permute-start | bytes 786440 | tf_op jit(solution)/shard_map/ppermute | solution.py:181
  135.0 22.2 %collective-permute-start.14 = (bf16[16,128,128]{2,1,0:T(8,128)(2,1)S(1)}, bf16[16,128,128]{2,1,0:T(8,128)(2,1)S(1)}, u32[]{:S(2)}, u32[]{:S(2)}) collective-permute-start(bf16[16,128,128]{2,1,0:T(8,128)(2,1)S(1)} %pad_maximum_fusion.5), channel_id=1, source_target_pairs={{0,4},{1,5},{2,6},{3,7},{4,0},{5,1},{6,2},{7,3},{8,12},{9,13},{10,... | collective-permute-start | bytes 1572872 | tf_op jit(solution)/shard_map/ppermute | solution.py:181
  137.6 18.5 %collective-permute-start.9 = (bf16[8,128,128]{2,1,0:T(8,128)(2,1)}, bf16[8,128,128]{2,1,0:T(8,128)(2,1)S(1)}, u32[]{:S(2)}, u32[]{:S(2)}) collective-permute-start(bf16[8,128,128]{2,1,0:T(8,128)(2,1)} %get-tuple-element.17), channel_id=1, source_target_pairs={{0,8},{1,9},{2,10},{3,11},{4,12},{5,13},{6,14},{7,15},{8,0},{9,1},... | collective-permute-start | bytes 786440 | tf_op jit(solution)/shard_map/ppermute | solution.py:181
  156.0 48.4 %copy-start = (bf16[8,128,128]{2,1,0:T(8,128)(2,1)}, bf16[8,128,128]{2,1,0:T(8,128)(2,1)S(1)}, u32[]{:S(2)}) copy-start(bf16[8,128,128]{2,1,0:T(8,128)(2,1)S(1)} %collective-permute-done.9) | copy-start | bytes 786436
  157.1 13.4 %collective-permute-start.10 = (bf16[16,128,128]{2,1,0:T(8,128)(2,1)S(1)}, bf16[16,128,128]{2,1,0:T(8,128)(2,1)S(1)}, u32[]{:S(2)}, u32[]{:S(2)}) collective-permute-start(bf16[16,128,128]{2,1,0:T(8,128)(2,1)S(1)} %pad_maximum_fusion.4), channel_id=1, source_target_pairs={{0,4},{1,5},{2,6},{3,7},{4,0},{5,1},{6,2},{7,3},{8,12},{9,13},{10,... | collective-permute-start | bytes 1572872 | tf_op jit(solution)/shard_map/ppermute | solution.py:181
  157.3 26.2 %collective-permute-start.15 = (bf16[32,128,128]{2,1,0:T(8,128)(2,1)S(1)}, bf16[32,128,128]{2,1,0:T(8,128)(2,1)S(1)}, u32[]{:S(2)}, u32[]{:S(2)}) collective-permute-start(bf16[32,128,128]{2,1,0:T(8,128)(2,1)S(1)} %pad_maximum_fusion.3), channel_id=1, source_target_pairs={{0,2},{1,3},{2,0},{3,1},{4,6},{5,7},{6,4},{7,5},{8,10},{9,11},{10,... | collective-permute-start | bytes 3145736 | tf_op jit(solution)/shard_map/ppermute | solution.py:181
  170.6 33.8 %collective-permute-start.11 = (bf16[32,128,128]{2,1,0:T(8,128)(2,1)S(1)}, bf16[32,128,128]{2,1,0:T(8,128)(2,1)S(1)}, u32[]{:S(2)}, u32[]{:S(2)}) collective-permute-start(bf16[32,128,128]{2,1,0:T(8,128)(2,1)S(1)} %pad_maximum_fusion.2), channel_id=1, source_target_pairs={{0,2},{1,3},{2,0},{3,1},{4,6},{5,7},{6,4},{7,5},{8,10},{9,11},{10,... | collective-permute-start | bytes 3145736 | tf_op jit(solution)/shard_map/ppermute | solution.py:181
  185.0 21.0 %copy-start.7 = (s32[1,1,1,256]{3,2,1,0:T(1,128)S(1)}, s32[1,1,1,256]{3,2,1,0:T(1,128)}, u32[]{:S(2)}) copy-start(s32[1,1,1,256]{3,2,1,0:T(1,128)} %get-tuple-element.34) | copy-start | bytes 3076
  185.0 156.7 %collective-permute-start.16 = (bf16[64,128,128]{2,1,0:T(8,128)(2,1)}, bf16[64,128,128]{2,1,0:T(8,128)(2,1)}, u32[]{:S(2)}, u32[]{:S(2)}) collective-permute-start(bf16[64,128,128]{2,1,0:T(8,128)(2,1)} %pad_maximum_fusion.1), channel_id=1, source_target_pairs={{0,1},{1,0},{2,3},{3,2},{4,5},{5,4},{6,7},{7,6},{8,9},{9,8},{10,11... | collective-permute-start | bytes 6291464 | tf_op jit(solution)/shard_map/ppermute | solution.py:181
  206.0 151.5 %collective-permute-start.12 = (bf16[64,128,128]{2,1,0:T(8,128)(2,1)}, bf16[64,128,128]{2,1,0:T(8,128)(2,1)}, u32[]{:S(2)}, u32[]{:S(2)}) collective-permute-start(bf16[64,128,128]{2,1,0:T(8,128)(2,1)} %pad_maximum_fusion), channel_id=1, source_target_pairs={{0,1},{1,0},{2,3},{3,2},{4,5},{5,4},{6,7},{7,6},{8,9},{9,8},{10,11... | collective-permute-start | bytes 6291464 | tf_op jit(solution)/shard_map/ppermute | solution.py:181
  344.9 12.7 %copy-start.5 = (bf16[128,128,128]{2,1,0:T(8,128)(2,1)S(1)}, bf16[128,128,128]{2,1,0:T(8,128)(2,1)}, u32[]{:S(2)}) copy-start(bf16[128,128,128]{2,1,0:T(8,128)(2,1)} %constant_dynamic-update-slice_fusion.1) | copy-start | bytes 12582916
  357.5 16.3 %collective-permute-start.17 = (bf16[2048,128]{1,0:T(8,128)(2,1)}, bf16[2048,128]{1,0:T(8,128)(2,1)S(1)}, u32[]{:S(2)}, u32[]{:S(2)}) collective-permute-start(bf16[2048,128]{1,0:T(8,128)(2,1)} %bitcast.38), channel_id=1, source_target_pairs={{0,16},{16,0},{1,17},{17,1},{2,18},{18,2},{3,19},{19,3},{4,20},{20... | collective-permute-start | bytes 1572872 | tf_op jit(solution)/shard_map/ppermute | solution.py:181
  359.5 2.0 copy-start.6
Sparse Core Ops, SparseCore 0:
  206.2 127.0 all-reduce.1

commit v2 on v1

v2 whole, which is shorter than its diff:
```python
import functools

import jax
import jax.numpy as jnp
from jax import lax
from jax.experimental import pallas as pl
from jax.experimental.pallas import tpu as pltpu
from jax.sharding import PartitionSpec as P

BF16 = jnp.bfloat16
F32 = jnp.float32
GROUP = 32
PARTS = 2
VMEM_LIMIT = 56 * 1024 * 1024


def orders(count):
    bits = [1 << k for k in range(count.bit_length() - 1)]
    swapped = list(bits)
    swapped[1], swapped[2] = bits[2], bits[1]
    return bits, swapped


def spot_of(apart, order):
    spot = apart * 0
    for k, bit in enumerate(reversed(order)):
        spot = spot + jnp.where((apart & bit) != 0, 1 << k, 0)
    return spot


def split_row(row, me, count, per_device, parts):
    run = per_device // parts
    apart, at = (row // per_device) ^ me, row % per_device
    spots = [spot_of(apart, order) for order in orders(count)[:parts]]
    part = at // run
    spot = spots[0] if parts == 1 else jnp.where(part == 0, spots[0], spots[1])
    return spot, part, at % run


def prepare(live, totals, spots, index_of, clear_count):
    each = spots.shape[0] // clear_count

    def one(at, _):
        totals[at] = jnp.zeros(totals.shape[1:], F32)
        for k in range(each):
            slot = at * each + k
            spots[slot] = index_of(slot, slot < live[0])
        return 0

    lax.fori_loop(0, clear_count, one, 0)


def block_copies(vals, held, sems):
    groups = held.shape[0] // GROUP
    part = lambda at: pl.ds(at * GROUP, GROUP)
    return [pltpu.make_async_copy(vals.at[part(at)], held.at[part(at)], sems.at[at]) for at in range(groups)]


def over_blocks(live, copies, body):
    for at, copy in enumerate(copies):

        @pl.when(at * GROUP < live[0])
        def _(at=at, copy=copy):
            copy.wait()
            for u in range(GROUP):
                body(at * GROUP + u)


def start_blocks(live, copies):
    for at, copy in enumerate(copies):

        @pl.when(at * GROUP < live[0])
        def _(copy=copy):
            copy.start()


def forward_kernel(count, per_device, live, me, coords, vals, feats, keep, send, held, totals, rounded, spots, sems, out_sems):
    rows = count * per_device
    half, run, below = rows // 2, per_device // PARTS, count // 2
    copies = block_copies(vals, held, sems)
    start_blocks(live, copies)

    def index_of(slot, alive):
        spot, part, at = split_row(coords[0, slot], me[0], count, per_device, PARTS)
        to = (((spot // below) * PARTS + part) * below + spot % below) * run + at
        return jnp.where(alive, to, rows)

    prepare(live, totals, spots, index_of, rows)

    def one_slot(slot):
        to = spots[slot]
        totals[to] += jnp.dot(held[slot], feats[coords[1, slot]], preferred_element_type=F32)

    over_blocks(live, copies, one_slot)
    outs = []
    for at, out in ((1, send), (0, keep)):

        def write(k, _, at=at):
            rounded[at * half + k] = totals[at * half + k].astype(BF16)
            return 0

        lax.fori_loop(0, half, write, 0)
        outs.append(pltpu.make_async_copy(rounded.at[pl.ds(at * half, half)], out, out_sems.at[at]))
        outs[-1].start()
    for out in outs:
        out.wait()


def forward_blocks(live, me, coords, vals, feats, count, per_device):
    slots, size = vals.shape[0], vals.shape[1]
    width = feats.shape[2]
    rows = count * per_device
    part = jax.ShapeDtypeStruct((rows // 2, size, width), BF16)
    smem, hbm = pl.BlockSpec(memory_space=pltpu.SMEM), pl.BlockSpec(memory_space=pl.ANY)
    return pl.pallas_call(
        functools.partial(forward_kernel, count, per_device),
        in_specs=[smem, smem, smem, hbm, pl.BlockSpec(memory_space=pltpu.VMEM)],
        out_specs=[hbm, hbm],
        scratch_shapes=[
            pltpu.VMEM(vals.shape, BF16),
            pltpu.VMEM((rows + 1, size, width), F32),
            pltpu.VMEM((rows, size, width), BF16),
            pltpu.SMEM((slots,), jnp.int32),
            pltpu.SemaphoreType.DMA((slots // GROUP,)),
            pltpu.SemaphoreType.DMA((2,)),
        ],
        out_shape=[part, part],
        compiler_params=pltpu.CompilerParams(vmem_limit_bytes=VMEM_LIMIT),
        cost_estimate=pl.CostEstimate(
            flops=8 * slots * size * size * width, bytes_accessed=4 * vals.size, transcendentals=0
        ),
        name="forward_blocks",
    )(live, me, coords, vals, feats)


def backward_kernel(count, per_device, parts, lengths, live, me, coords, vals, *refs):
    pieces, (out, held, grads, totals, spots, sems, piece_sems) = refs[:-7], refs[-7:]
    run, cols = per_device // parts, out.shape[0]
    copies = block_copies(vals, held, sems)
    fetches, start = [], 0
    for at, (piece, length) in enumerate(zip(pieces, lengths)):
        fetches.append(pltpu.make_async_copy(piece, grads.at[pl.ds(start, length)], piece_sems.at[at]))
        fetches[-1].start()
        start += length
    start_blocks(live, copies)

    def index_of(slot, alive):
        spot, part, at = split_row(coords[0, slot], me[0], count, per_device, parts)
        return (part * count + spot) * run + at

    prepare(live, totals, spots, index_of, cols)
    for fetch in fetches:
        fetch.wait()

    def one_slot(slot):
        to = jnp.where(slot < live[0], coords[1, slot], cols)
        totals[to] += jnp.dot(grads[spots[slot]], held[slot], preferred_element_type=F32)

    over_blocks(live, copies, one_slot)

    def write(at, _):
        out[at] = totals[at].T.astype(out.dtype)
        return 0

    lax.fori_loop(0, cols, write, 0)


def backward_blocks(live, me, coords, vals, pieces, cols, kind, count, per_device, parts):
    slots, size = vals.shape[0], vals.shape[1]
    width = pieces[0].shape[1]
    lengths = tuple(piece.shape[0] for piece in pieces)
    smem, hbm = pl.BlockSpec(memory_space=pltpu.SMEM), pl.BlockSpec(memory_space=pl.ANY)
    return pl.pallas_call(
        functools.partial(backward_kernel, count, per_device, parts, lengths),
        in_specs=[smem, smem, smem, hbm] + [hbm] * len(pieces),
        out_specs=pl.BlockSpec(memory_space=pltpu.VMEM),
        scratch_shapes=[
            pltpu.VMEM(vals.shape, BF16),
            pltpu.VMEM((count * per_device, width, size), BF16),
            pltpu.VMEM((cols + 1, width, size), F32),
            pltpu.SMEM((slots,), jnp.int32),
            pltpu.SemaphoreType.DMA((slots // GROUP,)),
            pltpu.SemaphoreType.DMA((len(pieces),)),
        ],
        out_shape=jax.ShapeDtypeStruct((cols, size, width), kind),
        compiler_params=pltpu.CompilerParams(vmem_limit_bytes=VMEM_LIMIT),
        cost_estimate=pl.CostEstimate(
            flops=8 * slots * size * size * width, bytes_accessed=4 * vals.size, transcendentals=0
        ),
        name="backward_blocks",
    )(live, me, coords, vals, *pieces)


def dense_kernel(first, *refs):
    terms_a, terms_b, (cot, weight, bias, out, grad_a, grad_b, terms) = refs[:4], refs[4:8], refs[8:]
    half = weight.shape[0] // 2
    size = grad_a.shape[2]
    at_a = pl.multiple_of(first[0] * half, half)
    at_b = pl.multiple_of((1 - first[0]) * half, half)

    def total(keep_0, got_0, keep_1, got_1):
        add_up = lambda x, y: (x[...].astype(F32) + y[...].astype(F32)).astype(BF16).reshape(-1, half)
        return jnp.concatenate([add_up(keep_0, got_0), add_up(keep_1, got_1)])

    agg_a, agg_b = total(*terms_a), total(*terms_b)
    weight_a, weight_b = weight[pl.ds(at_a, half), :], weight[pl.ds(at_b, half), :]
    preact = jnp.dot(agg_a, weight_a, preferred_element_type=F32)
    preact += jnp.dot(agg_b, weight_b, preferred_element_type=F32)
    preact += bias[...]
    gate = jax.nn.sigmoid(preact)
    out[...] = (preact * gate).astype(BF16)
    slope = gate * (1.0 + preact * (1.0 - gate))
    grad_pre = (cot[...].astype(F32) * slope).astype(BF16)
    over_rows = (((0,), (0,)), ((), ()))
    over_outputs = (((1,), (1,)), ((), ()))
    turned_a = lax.dot_general(weight_a, grad_pre, over_outputs, preferred_element_type=F32).astype(BF16)
    turned_b = lax.dot_general(weight_b, grad_pre, over_outputs, preferred_element_type=F32).astype(BF16)
    for at in range(grad_a.shape[0]):
        grad_a[at] = turned_a[:, at * size : (at + 1) * size]
        grad_b[at] = turned_b[:, at * size : (at + 1) * size]
    terms[pl.ds(at_a, half), :] = lax.dot_general(agg_a, grad_pre, over_rows, preferred_element_type=F32)
    terms[pl.ds(at_b, half), :] = lax.dot_general(agg_b, grad_pre, over_rows, preferred_element_type=F32)
    sums = jnp.sum(grad_pre.astype(F32), axis=0, keepdims=True)
    terms[2 * half :, :] = jnp.broadcast_to(sums, (terms.shape[0] - 2 * half, sums.shape[1]))


def dense(first, terms_a, terms_b, cot, weight, bias):
    run, size, half = terms_b[0].shape
    rows, width = cot.shape
    vmem = pl.BlockSpec(memory_space=pltpu.VMEM)
    turned = jax.ShapeDtypeStruct((rows // size, half, size), BF16)
    return pl.pallas_call(
        dense_kernel,
        in_specs=[pl.BlockSpec(memory_space=pltpu.SMEM)] + [vmem] * 11,
        out_specs=[vmem] * 4,
        out_shape=[
            jax.ShapeDtypeStruct((rows, width), BF16),
            turned,
            turned,
            jax.ShapeDtypeStruct((2 * half + 32, width), F32),
        ],
        compiler_params=pltpu.CompilerParams(vmem_limit_bytes=VMEM_LIMIT),
        cost_estimate=pl.CostEstimate(
            flops=8 * rows * width * width, bytes_accessed=8 * rows * width, transcendentals=rows * width
        ),
        name="dense_layer",
    )(first, *terms_a, *terms_b, cot, weight, bias)


def swap(array, axis, bit):
    return lax.ppermute(array, axis, [(at, at ^ bit) for at in range(lax.axis_size(axis))])


def after(array, *others):
    return lax.optimization_barrier((array, *others))[0]


def add(x, y):
    return (x.astype(F32) + y.astype(F32)).astype(BF16)


def halves(keep, got):
    half = keep.shape[0] // 2
    send = add(keep[half:], got[half:])
    return add(keep[:half], got[:half]), send


class SumOverAll:
    def __init__(self, terms):
        self.terms = self.got = terms
        self.bits = [1 << k for k in range(lax.axis_size("col").bit_length() - 1)]
        if lax.axis_size("row") == 2:
            half = terms.shape[0] // 2
            self.mine = lax.axis_index("row")
            self.part = lax.dynamic_slice_in_dim(terms, self.mine * half, half)
            self.got = swap(lax.dynamic_slice_in_dim(terms, (1 - self.mine) * half, half), "row", 1)

    def step(self, take=lambda got: got):
        if lax.axis_size("row") == 2 and self.bits:
            self.part = self.part + take(self.got)
            self.got = swap(self.part, "col", self.bits.pop(0))

    def finish(self):
        if lax.axis_size("row") != 2:
            return lax.psum(self.terms, ("row", "col"))
        while self.bits:
            self.step()
        part = self.part + self.got
        other = swap(part, "row", 1)
        first, second = jnp.where(self.mine == 0, part, other), jnp.where(self.mine == 0, other, part)
        return jnp.concatenate([first, second])


def on_device(features, block_values, block_coords, live_blocks, weight, bias, cotangent):
    vals, coords, live = block_values[0, 0], block_coords[0, 0], live_blocks[0]
    size = vals.shape[1]
    row_count, count = lax.axis_size("row"), lax.axis_size("col")
    me = lax.axis_index("col").reshape(1)
    width = weight.shape[0]
    half = width // 2
    per_device = cotangent.shape[0] // size
    cols = features.shape[0] // size
    order_0, order_1 = orders(count)

    if row_count == 2:
        first = lax.axis_index("row").reshape(1)
        feats_a, feats_b = features, swap(features, "row", 1)
    else:
        first = jnp.zeros((1,), jnp.int32)
        feats = lax.all_gather(features, "row", axis=1, tiled=True)
        feats_a, feats_b = feats[:, :half], feats[:, half:]

    def core_sums(feats, *others):
        keep, send = forward_blocks(live, me, coords, vals, feats.reshape(cols, size, half), count, per_device)
        got = swap(after(send, *others), "col", 1)
        part = keep.shape[0] // 2
        return halves(keep[:part], got[:part]), halves(keep[part:], got[part:])

    def next_step(part, bit):
        keep, send = part
        return halves(keep, swap(send, "col", bit))

    a0, a1 = core_sums(feats_a, feats_b)
    feats_b = after(feats_b, a0[1], a1[1])
    a0, a1 = next_step(a0, order_0[1]), next_step(a1, order_1[1])
    b0, b1 = core_sums(feats_b, a0[1], a1[1])
    for bit_0, bit_1 in zip(order_0[2:-1], order_1[2:-1]):
        a0, a1 = next_step(a0, bit_0), next_step(a1, bit_1)
    for bit_0, bit_1 in zip(order_0[1:-1], order_1[1:-1]):
        b0, b1 = next_step(b0, bit_0), next_step(b1, bit_1)
    terms_a, terms_b = [], []
    for terms, parts in ((terms_a, (a0, a1)), (terms_b, (b0, b1))):
        for keep, send in parts:
            terms += [keep, swap(send, "col", order_0[-1])]
    out, grad_a, grad_b, terms = dense(first, terms_a, terms_b, cotangent, weight, bias.reshape(1, -1))
    run = per_device // PARTS

    def input_grad(pieces, parts, kind):
        result = backward_blocks(live, me, coords, vals, pieces, cols, kind, count, per_device, parts)
        return result.reshape(-1, half)

    taken = [grad_b]

    def take(got):
        taken[0] = after(got, taken[0])
        return taken[0]

    totals = SumOverAll(terms)
    outer, inner = list(reversed(order_0[2:])), order_0[1]
    got_b = swap(grad_b, "col", outer[0])
    pieces_a = [grad_a]
    crossed = [swap(grad_a, "col", inner)]
    sent_a = {bit: swap(grad_a, "col", bit) for bit in outer[1:]}
    crossed = [take(crossed[0])]
    totals.step(take)
    got_b = take(got_b)
    parts_b = [jnp.concatenate([grad_b[at : at + run], got_b[at : at + run]]) for at in (0, run)]
    steps_b = list(zip(reversed(order_0[1:-1]), reversed(order_1[1:-1])))

    def step_b(at):
        got = [swap(part, "col", bit) for part, bit in zip(parts_b, steps_b[at])]
        return got

    for at in range(len(steps_b)):
        got = step_b(at)
        if at == 0:
            got_a = swap(after(grad_a, got_b), "col", outer[0])
        got = [take(part) for part in got]
        parts_b = [jnp.concatenate([part, more]) for part, more in zip(parts_b, got)]
        totals.step(take)
        if at == 0:
            got_a = take(got_a)
            pieces_a = [grad_a, got_a]
            for bit in outer[1:]:
                pieces_a = pieces_a + [sent_a[bit]] + [swap(piece, "col", bit) for piece in pieces_a[1:]]
            crossed += [swap(piece, "col", inner) for piece in pieces_a[1:]]
    core_b = [swap(part, "col", 1) for part in parts_b]
    early = jnp.concatenate(pieces_a + [take(piece) for piece in crossed[:-1]])
    pieces_b = [parts_b[0], core_b[0], parts_b[1], core_b[1]]
    totals.step(take)
    pieces_b[0] = after(pieces_b[0], taken[0])
    core_early = swap(early, "col", 1)

    if row_count == 2:
        part_b = input_grad(pieces_b, PARTS, BF16)
        theirs = swap(part_b, "row", 1)
        late = after(crossed[-1], part_b)
        pieces_a = [early, late, core_early, swap(late, "col", 1)]
        grad_x = (input_grad(pieces_a, 1, F32) + theirs.astype(F32)).astype(BF16)
    else:
        part_b = input_grad(pieces_b, PARTS, F32)
        pieces_a = [early, crossed[-1], core_early, swap(crossed[-1], "col", 1)]
        partial_x = jnp.concatenate([input_grad(pieces_a, 1, F32), part_b], axis=1)
        grad_x = lax.psum_scatter(partial_x, "row", scatter_dimension=1, tiled=True).astype(BF16)
    totals.got = after(totals.got, part_b)
    sums = totals.finish() * (cols * size * count) ** (-0.5)
    return out, grad_x, sums[:width], sums[width]


def solution(mesh):
    in_specs = (
        P("col", "row"),
        P("row", "col", None, None, None),
        P("row", "col", None, None),
        P("row", "col"),
        P(),
        P(),
        P(("row", "col"), None),
    )
    out_specs = (P(("row", "col"), None), P("col", "row"), P(), P())
    return jax.shard_map(
        on_device, mesh=mesh, in_specs=in_specs, out_specs=out_specs, check_vma=False
    )
```

time: 385 us -> 191 us (0.50)
  the two profiles are of different devices: /device:TPU:14 before, /device:TPU:0 now
where the time goes in v2:
time: 191 us
  waiting for transfers between devices  79.3 us (42%)
  Pallas kernels  56.7 us (30%)
  starting transfers between devices  37.8 us (20%)
  other arithmetic  9.55 us (5%)
  local copies, waits for them, and re-layouts  6.1 us (3%)
    ppermute x38, waiting for transfers between devices, swap(): lax.ppermute(array, axis, [(at, at ^ bit) for at in range(lax.axis_size(a...  79.3 us
    ppermute x38, starting transfers between devices, swap(): lax.ppermute(array, axis, [(at, at ^ bit) for at in range(lax.axis_size(a...  37.8 us
    pallas_call x2, Pallas kernels, forward_blocks(): pl.pallas_call(functools.partial(forward_kernel, count, per_device), in_s...  28.9 us
    pallas_call x2, Pallas kernels, backward_blocks(): pl.pallas_call(functools.partial(backward_kernel, count, per_device, part...  24.1 us
    convert_element_type x10, other arithmetic, add(): return (x.astype(F32) + y.astype(F32)).astype(BF16)  6.91 us
  transfers between devices with their start and end apart: 38, of which 19 were waited for; matrix products, arithmetic and copies ran while one was open for 4% of the time, Pallas kernels for 28%

profile of v2, /device:TPU:0, one launch (start us, length us, event | category | flops | bytes accessed | tf_op | source)
XLA Modules:
  0.0 191.2 jit_solution(18111269232836152732)
XLA Ops:
  0.6 3.0 %collective-permute-start = (bf16[2048,128]{1,0:T(8,128)(2,1)}, bf16[2048,128]{1,0:T(8,128)(2,1)S(1)}, u32[]{:S(2)}, u32[]{:S(2)}) collective-permute-start(bf16[2048,128]{1,0:T(8,128)(2,1)} %param.7), channel_id=1, source_target_pairs={{0,16},{16,0},{1,17},{17,1},{2,18},{18,2},{3,19},{19,3},{4,20},{20... | collective-permute-start | bytes 1572872 | tf_op jit(solution)/shard_map/ppermute | solution.py:251
  4.3 14.3 %forward_blocks.2 = (bf16[64,128,128]{2,1,0:T(8,128)(2,1)}, bf16[64,128,128]{2,1,0:T(8,128)(2,1)}) custom-call(s32[1]{0:T(128)} %bitcast.14.live, s32[1]{0:T(128)} %bitcast.2.me, s32[2,256]{1,0:T(2,128)} %bitcast.26, bf16[256,128,128]{2,1,0:T(8,128)(2,1)} %bitcast.19, bf16[16,128,128]{2,1,0:T(8,128)(2,1)} %bitcast.23), custom_call_target="tpu_custom_call" | custom-call | flops 4294967296 | bytes 16777216 | tf_op jit(solution)/shard_map/forward_blocks/pallas_call | solution.py:115
  18.8 4.4 %collective-permute-done.1 = bf16[64,128,128]{2,1,0:T(8,128)(2,1)S(1)} collective-permute-done((bf16[64,128,128]{2,1,0:T(8,128)(2,1)}, bf16[64,128,128]{2,1,0:T(8,128)(2,1)S(1)}, u32[]{:S(2)}, u32[]{:S(2)}) %collective-permute-start.1) | collective-permute-done | bytes 2097184 | tf_op jit(solution)/shard_map/ppermute | solution.py:251
  23.1 2.3 %add_convert_fusion.5 = (bf16[16,128,128]{2,1,0:T(8,128)(2,1)S(1)}, bf16[16,128,128]{2,1,0:T(8,128)(2,1)S(1)}, bf16[16,128,128]{2,1,0:T(8,128)(2,1)S(1)}, bf16[16,128,128]{2,1,0:T(8,128)(2,1)S(1)}) fusion(bf16[64,128,128]{2,1,0:T(8,128)(2,1)S(1)} %collective-permute-done.1, bf16[64,128,128]{2,1,0:T(8,128)(2,1)} %get-tuple-element.33), kind=kLoop, calls=%fused_computation.9 | loop fusion | flops 4194304 | bytes 6291456 | tf_op jit(solution)/shard_map/convert_element_type | solution.py:259
  26.3 14.5 %forward_blocks.3 = (bf16[64,128,128]{2,1,0:T(8,128)(2,1)}, bf16[64,128,128]{2,1,0:T(8,128)(2,1)}) custom-call(s32[1]{0:T(128)} %bitcast.15.live, s32[1]{0:T(128)} %bitcast.2.me, s32[2,256]{1,0:T(2,128)} %bitcast.27, bf16[256,128,128]{2,1,0:T(8,128)(2,1)} %bitcast.20, bf16[16,128,128]{2,1,0:T(8,128)(2,1)} %bitcast.25), custom_call_target="tpu_custom_call" | custom-call | flops 4294967296 | bytes 16777216 | tf_op jit(solution)/shard_map/forward_blocks/pallas_call | solution.py:115
  41.3 4.4 %collective-permute-done.8 = bf16[64,128,128]{2,1,0:T(8,128)(2,1)S(1)} collective-permute-done((bf16[64,128,128]{2,1,0:T(8,128)(2,1)}, bf16[64,128,128]{2,1,0:T(8,128)(2,1)S(1)}, u32[]{:S(2)}, u32[]{:S(2)}) %collective-permute-start.8) | collective-permute-done | bytes 2097184 | tf_op jit(solution)/shard_map/ppermute | solution.py:251
  50.9 5.3 %collective-permute-done.6 = bf16[8,128,128]{2,1,0:T(8,128)(2,1)S(1)} collective-permute-done((bf16[8,128,128]{2,1,0:T(8,128)(2,1)S(1)}, bf16[8,128,128]{2,1,0:T(8,128)(2,1)S(1)}, u32[]{:S(2)}, u32[]{:S(2)}) %collective-permute-start.6) | collective-permute-done | bytes 262176 | tf_op jit(solution)/shard_map/ppermute | solution.py:251
  56.9 2.9 %collective-permute-start.7 = (bf16[4,128,128]{2,1,0:T(8,128)(2,1)S(1)}, bf16[4,128,128]{2,1,0:T(8,128)(2,1)S(1)}, u32[]{:S(2)}, u32[]{:S(2)}) collective-permute-start(bf16[4,128,128]{2,1,0:T(8,128)(2,1)S(1)} %get-tuple-element.82), channel_id=1, source_target_pairs={{0,8},{1,9},{2,10},{3,11},{4,12},{5,13},{6,14},{7,15},{8,0},{9,1},... | collective-permute-start | bytes 393224 | tf_op jit(solution)/shard_map/ppermute | solution.py:251
  59.8 4.5 %collective-permute-done.12 = bf16[16,128,128]{2,1,0:T(8,128)(2,1)S(1)} collective-permute-done((bf16[16,128,128]{2,1,0:T(8,128)(2,1)S(1)}, bf16[16,128,128]{2,1,0:T(8,128)(2,1)S(1)}, u32[]{:S(2)}, u32[]{:S(2)}) %collective-permute-start.12) | collective-permute-done | bytes 524320 | tf_op jit(solution)/shard_map/ppermute | solution.py:251
  64.6 2.8 %collective-permute-done.9 = bf16[16,128,128]{2,1,0:T(8,128)(2,1)S(1)} collective-permute-done((bf16[16,128,128]{2,1,0:T(8,128)(2,1)S(1)}, bf16[16,128,128]{2,1,0:T(8,128)(2,1)S(1)}, u32[]{:S(2)}, u32[]{:S(2)}) %collective-permute-start.9) | collective-permute-done | bytes 524320 | tf_op jit(solution)/shard_map/ppermute | solution.py:251
  67.6 1.9 collective-permute-start.10
  70.6 2.2 %collective-permute-start.4 = (bf16[4,128,128]{2,1,0:T(8,128)(2,1)S(1)}, bf16[4,128,128]{2,1,0:T(8,128)(2,1)S(1)}, u32[]{:S(2)}, u32[]{:S(2)}) collective-permute-start(bf16[4,128,128]{2,1,0:T(8,128)(2,1)S(1)} %get-tuple-element.84), channel_id=1, source_target_pairs={{0,8},{1,9},{2,10},{3,11},{4,12},{5,13},{6,14},{7,15},{8,0},{9,1},... | collective-permute-start | bytes 393224 | tf_op jit(solution)/shard_map/ppermute | solution.py:251
  73.5 2.2 %collective-permute-start.14 = (bf16[4,128,128]{2,1,0:T(8,128)(2,1)S(1)}, bf16[4,128,128]{2,1,0:T(8,128)(2,1)S(1)}, u32[]{:S(2)}, u32[]{:S(2)}) collective-permute-start(bf16[4,128,128]{2,1,0:T(8,128)(2,1)S(1)} %get-tuple-element.78), channel_id=1, source_target_pairs={{0,8},{1,9},{2,10},{3,11},{4,12},{5,13},{6,14},{7,15},{8,0},{9,1},... | collective-permute-start | bytes 393224 | tf_op jit(solution)/shard_map/ppermute | solution.py:251
  78.1 2.5 %collective-permute-start.11 = (bf16[4,128,128]{2,1,0:T(8,128)(2,1)S(1)}, bf16[4,128,128]{2,1,0:T(8,128)(2,1)S(1)}, u32[]{:S(2)}, u32[]{:S(2)}) collective-permute-start(bf16[4,128,128]{2,1,0:T(8,128)(2,1)S(1)} %get-tuple-element.80), channel_id=1, source_target_pairs={{0,8},{1,9},{2,10},{3,11},{4,12},{5,13},{6,14},{7,15},{8,0},{9,1},... | collective-permute-start | bytes 393224 | tf_op jit(solution)/shard_map/ppermute | solution.py:251
  80.5 5.2 %collective-permute-done.4.refs_1_ = bf16[4,128,128]{2,1,0:T(8,128)(2,1)S(1)} collective-permute-done((bf16[4,128,128]{2,1,0:T(8,128)(2,1)S(1)}, bf16[4,128,128]{2,1,0:T(8,128)(2,1)S(1)}, u32[]{:S(2)}, u32[]{:S(2)}) %collective-permute-start.4) | collective-permute-done | bytes 131104 | tf_op jit(solution)/shard_map/ppermute | solution.py:251
  85.7 2.8 %collective-permute-done.14.refs_7_ = bf16[4,128,128]{2,1,0:T(8,128)(2,1)S(1)} collective-permute-done((bf16[4,128,128]{2,1,0:T(8,128)(2,1)S(1)}, bf16[4,128,128]{2,1,0:T(8,128)(2,1)S(1)}, u32[]{:S(2)}, u32[]{:S(2)}) %collective-permute-start.14) | collective-permute-done | bytes 131104 | tf_op jit(solution)/shard_map/ppermute | solution.py:251
  90.9 3.7 %dense_layer.1 = (bf16[1024,256]{1,0:T(8,128)(2,1)}, bf16[8,128,128]{2,1,0:T(8,128)(2,1)}, bf16[8,128,128]{2,1,0:T(8,128)(2,1)}, f32[288,256]{1,0:T(8,128)}) custom-call(s32[1]{0:T(128)} %bitcast.first, bf16[4,128,128]{2,1,0:T(8,128)(2,1)} %get-tuple-element.85.refs_0_, bf16[4,128,128]{2,1,0:T(8,128)(2,1)} %copy-done.12, ...), custom_call_target="tpu_custom_call" | custom-call | flops 536870912 | bytes 2097152 | tf_op jit(solution)/shard_map/dense_layer/pallas_call | solution.py:232
  95.2 3.3 %collective-permute-start.15 = (bf16[8,128,128]{2,1,0:T(8,128)(2,1)}, bf16[8,128,128]{2,1,0:T(8,128)(2,1)S(1)}, u32[]{:S(2)}, u32[]{:S(2)}) collective-permute-start(bf16[8,128,128]{2,1,0:T(8,128)(2,1)} %get-tuple-element.42), channel_id=1, source_target_pairs={{0,8},{1,9},{2,10},{3,11},{4,12},{5,13},{6,14},{7,15},{8,0},{9,1},... | collective-permute-start | bytes 786440 | tf_op jit(solution)/shard_map/ppermute | solution.py:251
  102.0 2.6 %collective-permute-done.16 = f32[144,256]{1,0:T(8,128)S(1)} collective-permute-done((f32[144,256]{1,0:T(8,128)S(1)}, f32[144,256]{1,0:T(8,128)S(1)}, u32[]{:S(2)}, u32[]{:S(2)}) %collective-permute-start.16) | collective-permute-done | bytes 147488 | tf_op jit(solution)/shard_map/ppermute | solution.py:251
  104.6 5.0 %collective-permute-done.15 = bf16[8,128,128]{2,1,0:T(8,128)(2,1)S(1)} collective-permute-done((bf16[8,128,128]{2,1,0:T(8,128)(2,1)}, bf16[8,128,128]{2,1,0:T(8,128)(2,1)S(1)}, u32[]{:S(2)}, u32[]{:S(2)}) %collective-permute-start.15) | collective-permute-done | bytes 262176 | tf_op jit(solution)/shard_map/ppermute | solution.py:251
  111.2 2.7 %collective-permute-start.18 = (bf16[8,128,128]{2,1,0:T(8,128)(2,1)S(1)}, bf16[8,128,128]{2,1,0:T(8,128)(2,1)S(1)}, u32[]{:S(2)}, u32[]{:S(2)}) collective-permute-start(bf16[8,128,128]{2,1,0:T(8,128)(2,1)S(1)} %copy-done.4), channel_id=1, source_target_pairs={{0,8},{1,9},{2,10},{3,11},{4,12},{5,13},{6,14},{7,15},{8,0},{9,1},... | collective-permute-start | bytes 786440 | tf_op jit(solution)/shard_map/ppermute | solution.py:251
  113.9 5.3 %collective-permute-done.21 = bf16[8,128,128]{2,1,0:T(8,128)(2,1)S(1)} collective-permute-done((bf16[8,128,128]{2,1,0:T(8,128)(2,1)S(1)}, bf16[8,128,128]{2,1,0:T(8,128)(2,1)S(1)}, u32[]{:S(2)}, u32[]{:S(2)}) %collective-permute-start.21) | collective-permute-done | bytes 262176 | tf_op jit(solution)/shard_map/ppermute | solution.py:251
  120.1 4.2 %collective-permute-done.18 = bf16[8,128,128]{2,1,0:T(8,128)(2,1)S(1)} collective-permute-done((bf16[8,128,128]{2,1,0:T(8,128)(2,1)S(1)}, bf16[8,128,128]{2,1,0:T(8,128)(2,1)S(1)}, u32[]{:S(2)}, u32[]{:S(2)}) %collective-permute-start.18) | collective-permute-done | bytes 262176 | tf_op jit(solution)/shard_map/ppermute | solution.py:251
  124.3 2.0 %collective-permute-start.23 = (bf16[8,128,128]{2,1,0:T(8,128)(2,1)S(1)}, bf16[8,128,128]{2,1,0:T(8,128)(2,1)S(1)}, u32[]{:S(2)}, u32[]{:S(2)}) collective-permute-start(bf16[8,128,128]{2,1,0:T(8,128)(2,1)S(1)} %collective-permute-done.18), channel_id=1, source_target_pairs={{0,4},{1,5},{2,6},{3,7},{4,0},{5,1},{6,2},{7,3},{8,12},{9,13},{10,... | collective-permute-start | bytes 786440 | tf_op jit(solution)/shard_map/ppermute | solution.py:251
  128.6 13.7 %collective-permute-done.23 = bf16[8,128,128]{2,1,0:T(8,128)(2,1)S(1)} collective-permute-done((bf16[8,128,128]{2,1,0:T(8,128)(2,1)S(1)}, bf16[8,128,128]{2,1,0:T(8,128)(2,1)S(1)}, u32[]{:S(2)}, u32[]{:S(2)}) %collective-permute-start.23) | collective-permute-done | bytes 262176 | tf_op jit(solution)/shard_map/ppermute | solution.py:251
  143.5 3.9 %collective-permute-done.24 = f32[144,256]{1,0:T(8,128)S(1)} collective-permute-done((f32[144,256]{1,0:T(8,128)S(1)}, f32[144,256]{1,0:T(8,128)S(1)}, u32[]{:S(2)}, u32[]{:S(2)}) %collective-permute-start.24) | collective-permute-done | bytes 147488 | tf_op jit(solution)/shard_map/ppermute | solution.py:251
  149.5 5.0 %collective-permute-done.30 = f32[144,256]{1,0:T(8,128)S(1)} collective-permute-done((f32[144,256]{1,0:T(8,128)S(1)}, f32[144,256]{1,0:T(8,128)S(1)}, u32[]{:S(2)}, u32[]{:S(2)}) %collective-permute-start.30) | collective-permute-done | bytes 147488 | tf_op jit(solution)/shard_map/ppermute | solution.py:251
  155.9 12.0 %backward_blocks.2 = bf16[16,128,128]{2,1,0:T(8,128)(2,1)} custom-call(s32[1]{0:T(128)} %bitcast.16.live, s32[1]{0:T(128)} %bitcast.2.me, s32[2,256]{1,0:T(2,128)} %bitcast.28, bf16[256,128,128]{2,1,0:T(8,128)(2,1)} %bitcast.21, bf16[32,128,128]{2,1,0:T(8,128)(2,1)} %copy-done.1, bf16[32,128,128]{2,1,0:T(8,128)(2,1)} %copy-done.7, ...), custom_call_target="tpu_custom_call" | custom-call | flops 4294967296 | bytes 16777216 | tf_op jit(solution)/shard_map/backward_blocks/pallas_call | solution.py:173
  168.1 2.0 %collective-permute-start.35 = (bf16[2048,128]{1,0:T(8,128)(2,1)}, bf16[2048,128]{1,0:T(8,128)(2,1)S(1)}, u32[]{:S(2)}, u32[]{:S(2)}) collective-permute-start(bf16[2048,128]{1,0:T(8,128)(2,1)} %bitcast.24), channel_id=1, source_target_pairs={{0,16},{16,0},{1,17},{17,1},{2,18},{18,2},{3,19},{19,3},{4,20},{20... | collective-permute-start | bytes 1572872 | tf_op jit(solution)/shard_map/ppermute | solution.py:251
  170.1 4.7 %collective-permute-done.37 = f32[144,256]{1,0:T(8,128)S(1)} collective-permute-done((f32[144,256]{1,0:T(8,128)S(1)}, f32[144,256]{1,0:T(8,128)S(1)}, u32[]{:S(2)}, u32[]{:S(2)}) %collective-permute-start.37) | collective-permute-done | bytes 147488 | tf_op jit(solution)/shard_map/ppermute | solution.py:251
  176.9 12.1 %backward_blocks.3 = f32[16,128,128]{2,1,0:T(8,128)} custom-call(s32[1]{0:T(128)} %bitcast.17.live, s32[1]{0:T(128)} %bitcast.2.me, s32[2,256]{1,0:T(2,128)} %bitcast.29, bf16[256,128,128]{2,1,0:T(8,128)(2,1)} %bitcast.22, bf16[56,128,128]{2,1,0:T(8,128)(2,1)} %copy-done.5, bf16[8,128,128]{2,1,0:T(8,128)(2,1)} %copy-done.9, ...), custom_call_target="tpu_custom_call" | custom-call | flops 4294967296 | bytes 16777216 | tf_op jit(solution)/shard_map/backward_blocks/pallas_call | solution.py:173
  189.0 2.1 %fusion = bf16[2048,128]{1,0:T(8,128)(2,1)} fusion(f32[16,128,128]{2,1,0:T(8,128)} %backward_blocks.3, bf16[2048,128]{1,0:T(8,128)(2,1)S(1)} %collective-permute-done.35), kind=kLoop, calls=%fused_computation.3 | loop fusion | flops 786432 | bytes 2097152 | tf_op jit(solution)/shard_map/convert_element_type | solution.py:389
  (115 shorter events, 29.8 us)
Async XLA Ops:
  0.6 18.0 %collective-permute-start = (bf16[2048,128]{1,0:T(8,128)(2,1)}, bf16[2048,128]{1,0:T(8,128)(2,1)S(1)}, u32[]{:S(2)}, u32[]{:S(2)}) collective-permute-start(bf16[2048,128]{1,0:T(8,128)(2,1)} %param.7), channel_id=1, source_target_pairs={{0,16},{16,0},{1,17},{17,1},{2,18},{18,2},{3,19},{19,3},{4,20},{20... | collective-permute-start | bytes 1572872 | tf_op jit(solution)/shard_map/ppermute | solution.py:251
  25.5 15.4 %collective-permute-start.5 = (bf16[16,128,128]{2,1,0:T(8,128)(2,1)S(1)}, bf16[16,128,128]{2,1,0:T(8,128)(2,1)S(1)}, u32[]{:S(2)}, u32[]{:S(2)}) collective-permute-start(bf16[16,128,128]{2,1,0:T(8,128)(2,1)S(1)} %get-tuple-element.67), channel_id=1, source_target_pairs={{0,4},{1,5},{2,6},{3,7},{4,0},{5,1},{6,2},{7,3},{8,12},{9,13},{10,... | collective-permute-start | bytes 1572872 | tf_op jit(solution)/shard_map/ppermute | solution.py:251
  25.6 15.5 %collective-permute-start.2 = (bf16[16,128,128]{2,1,0:T(8,128)(2,1)S(1)}, bf16[16,128,128]{2,1,0:T(8,128)(2,1)S(1)}, u32[]{:S(2)}, u32[]{:S(2)}) collective-permute-start(bf16[16,128,128]{2,1,0:T(8,128)(2,1)S(1)} %get-tuple-element.68), channel_id=1, source_target_pairs={{0,2},{1,3},{2,0},{3,1},{4,6},{5,7},{6,4},{7,5},{8,10},{9,11},{10,... | collective-permute-start | bytes 1572872 | tf_op jit(solution)/shard_map/ppermute | solution.py:251
  46.7 17.6 %collective-permute-start.12 = (bf16[16,128,128]{2,1,0:T(8,128)(2,1)S(1)}, bf16[16,128,128]{2,1,0:T(8,128)(2,1)S(1)}, u32[]{:S(2)}, u32[]{:S(2)}) collective-permute-start(bf16[16,128,128]{2,1,0:T(8,128)(2,1)S(1)} %get-tuple-element.63), channel_id=1, source_target_pairs={{0,4},{1,5},{2,6},{3,7},{4,0},{5,1},{6,2},{7,3},{8,12},{9,13},{10,... | collective-permute-start | bytes 1572872 | tf_op jit(solution)/shard_map/ppermute | solution.py:251
  47.0 9.2 %collective-permute-start.6 = (bf16[8,128,128]{2,1,0:T(8,128)(2,1)S(1)}, bf16[8,128,128]{2,1,0:T(8,128)(2,1)S(1)}, u32[]{:S(2)}, u32[]{:S(2)}) collective-permute-start(bf16[8,128,128]{2,1,0:T(8,128)(2,1)S(1)} %get-tuple-element.75), channel_id=1, source_target_pairs={{0,2},{1,3},{2,0},{3,1},{4,6},{5,7},{6,4},{7,5},{8,10},{9,11},{10,... | collective-permute-start | bytes 786440 | tf_op jit(solution)/shard_map/ppermute | solution.py:251
  47.8 19.6 %collective-permute-start.9 = (bf16[16,128,128]{2,1,0:T(8,128)(2,1)S(1)}, bf16[16,128,128]{2,1,0:T(8,128)(2,1)S(1)}, u32[]{:S(2)}, u32[]{:S(2)}) collective-permute-start(bf16[16,128,128]{2,1,0:T(8,128)(2,1)S(1)} %get-tuple-element.64), channel_id=1, source_target_pairs={{0,2},{1,3},{2,0},{3,1},{4,6},{5,7},{6,4},{7,5},{8,10},{9,11},{10,... | collective-permute-start | bytes 1572872 | tf_op jit(solution)/shard_map/ppermute | solution.py:251
  49.0 20.9 %collective-permute-start.3 = (bf16[8,128,128]{2,1,0:T(8,128)(2,1)S(1)}, bf16[8,128,128]{2,1,0:T(8,128)(2,1)S(1)}, u32[]{:S(2)}, u32[]{:S(2)}) collective-permute-start(bf16[8,128,128]{2,1,0:T(8,128)(2,1)S(1)} %get-tuple-element.77), channel_id=1, source_target_pairs={{0,4},{1,5},{2,6},{3,7},{4,0},{5,1},{6,2},{7,3},{8,12},{9,13},{10,... | collective-permute-start | bytes 786440 | tf_op jit(solution)/shard_map/ppermute | solution.py:251
  56.9 23.6 %collective-permute-start.7 = (bf16[4,128,128]{2,1,0:T(8,128)(2,1)S(1)}, bf16[4,128,128]{2,1,0:T(8,128)(2,1)S(1)}, u32[]{:S(2)}, u32[]{:S(2)}) collective-permute-start(bf16[4,128,128]{2,1,0:T(8,128)(2,1)S(1)} %get-tuple-element.82), channel_id=1, source_target_pairs={{0,8},{1,9},{2,10},{3,11},{4,12},{5,13},{6,14},{7,15},{8,0},{9,1},... | collective-permute-start | bytes 393224 | tf_op jit(solution)/shard_map/ppermute | solution.py:251
  64.5 8.3 %collective-permute-start.13 = (bf16[8,128,128]{2,1,0:T(8,128)(2,1)S(1)}, bf16[8,128,128]{2,1,0:T(8,128)(2,1)S(1)}, u32[]{:S(2)}, u32[]{:S(2)}) collective-permute-start(bf16[8,128,128]{2,1,0:T(8,128)(2,1)S(1)} %get-tuple-element.71), channel_id=1, source_target_pairs={{0,2},{1,3},{2,0},{3,1},{4,6},{5,7},{6,4},{7,5},{8,10},{9,11},{10,... | collective-permute-start | bytes 786440 | tf_op jit(solution)/shard_map/ppermute | solution.py:251
  67.6 9.8 %collective-permute-start.10 = (bf16[8,128,128]{2,1,0:T(8,128)(2,1)S(1)}, bf16[8,128,128]{2,1,0:T(8,128)(2,1)S(1)}, u32[]{:S(2)}, u32[]{:S(2)}) collective-permute-start(bf16[8,128,128]{2,1,0:T(8,128)(2,1)S(1)} %get-tuple-element.73), channel_id=1, source_target_pairs={{0,4},{1,5},{2,6},{3,7},{4,0},{5,1},{6,2},{7,3},{8,12},{9,13},{10,... | collective-permute-start | bytes 786440 | tf_op jit(solution)/shard_map/ppermute | solution.py:251
  70.6 15.1 %collective-permute-start.4 = (bf16[4,128,128]{2,1,0:T(8,128)(2,1)S(1)}, bf16[4,128,128]{2,1,0:T(8,128)(2,1)S(1)}, u32[]{:S(2)}, u32[]{:S(2)}) collective-permute-start(bf16[4,128,128]{2,1,0:T(8,128)(2,1)S(1)} %get-tuple-element.84), channel_id=1, source_target_pairs={{0,8},{1,9},{2,10},{3,11},{4,12},{5,13},{6,14},{7,15},{8,0},{9,1},... | collective-permute-start | bytes 393224 | tf_op jit(solution)/shard_map/ppermute | solution.py:251
  73.5 15.0 %collective-permute-start.14 = (bf16[4,128,128]{2,1,0:T(8,128)(2,1)S(1)}, bf16[4,128,128]{2,1,0:T(8,128)(2,1)S(1)}, u32[]{:S(2)}, u32[]{:S(2)}) collective-permute-start(bf16[4,128,128]{2,1,0:T(8,128)(2,1)S(1)} %get-tuple-element.78), channel_id=1, source_target_pairs={{0,8},{1,9},{2,10},{3,11},{4,12},{5,13},{6,14},{7,15},{8,0},{9,1},... | collective-permute-start | bytes 393224 | tf_op jit(solution)/shard_map/ppermute | solution.py:251
  78.1 12.1 %collective-permute-start.11 = (bf16[4,128,128]{2,1,0:T(8,128)(2,1)S(1)}, bf16[4,128,128]{2,1,0:T(8,128)(2,1)S(1)}, u32[]{:S(2)}, u32[]{:S(2)}) collective-permute-start(bf16[4,128,128]{2,1,0:T(8,128)(2,1)S(1)} %get-tuple-element.80), channel_id=1, source_target_pairs={{0,8},{1,9},{2,10},{3,11},{4,12},{5,13},{6,14},{7,15},{8,0},{9,1},... | collective-permute-start | bytes 393224 | tf_op jit(solution)/shard_map/ppermute | solution.py:251
  94.6 7.5 %collective-permute-start.17 = (bf16[8,128,128]{2,1,0:T(8,128)(2,1)}, bf16[8,128,128]{2,1,0:T(8,128)(2,1)S(1)}, u32[]{:S(2)}, u32[]{:S(2)}) collective-permute-start(bf16[8,128,128]{2,1,0:T(8,128)(2,1)} %get-tuple-element.47), channel_id=1, source_target_pairs={{0,2},{1,3},{2,0},{3,1},{4,6},{5,7},{6,4},{7,5},{8,10},{9,11},{10,... | collective-permute-start | bytes 786440 | tf_op jit(solution)/shard_map/ppermute | solution.py:251
  95.2 31.2 %collective-permute-start.22 = (bf16[8,128,128]{2,1,0:T(8,128)(2,1)}, bf16[8,128,128]{2,1,0:T(8,128)(2,1)S(1)}, u32[]{:S(2)}, u32[]{:S(2)}) collective-permute-start(bf16[8,128,128]{2,1,0:T(8,128)(2,1)} %get-tuple-element.47), channel_id=1, source_target_pairs={{0,4},{1,5},{2,6},{3,7},{4,0},{5,1},{6,2},{7,3},{8,12},{9,13},{10,... | collective-permute-start | bytes 786440 | tf_op jit(solution)/shard_map/ppermute | solution.py:251
  95.2 14.4 %collective-permute-start.15 = (bf16[8,128,128]{2,1,0:T(8,128)(2,1)}, bf16[8,128,128]{2,1,0:T(8,128)(2,1)S(1)}, u32[]{:S(2)}, u32[]{:S(2)}) collective-permute-start(bf16[8,128,128]{2,1,0:T(8,128)(2,1)} %get-tuple-element.42), channel_id=1, source_target_pairs={{0,8},{1,9},{2,10},{3,11},{4,12},{5,13},{6,14},{7,15},{8,0},{9,1},... | collective-permute-start | bytes 786440 | tf_op jit(solution)/shard_map/ppermute | solution.py:251
  109.7 9.5 %collective-permute-start.21 = (bf16[8,128,128]{2,1,0:T(8,128)(2,1)S(1)}, bf16[8,128,128]{2,1,0:T(8,128)(2,1)S(1)}, u32[]{:S(2)}, u32[]{:S(2)}) collective-permute-start(bf16[8,128,128]{2,1,0:T(8,128)(2,1)S(1)} %pad_maximum_fusion.5), channel_id=1, source_target_pairs={{0,4},{1,5},{2,6},{3,7},{4,0},{5,1},{6,2},{7,3},{8,12},{9,13},{10,... | collective-permute-start | bytes 786440 | tf_op jit(solution)/shard_map/ppermute | solution.py:251
  109.8 10.2 %collective-permute-start.20 = (bf16[8,128,128]{2,1,0:T(8,128)(2,1)S(1)}, bf16[8,128,128]{2,1,0:T(8,128)(2,1)S(1)}, u32[]{:S(2)}, u32[]{:S(2)}) collective-permute-start(bf16[8,128,128]{2,1,0:T(8,128)(2,1)S(1)} %pad_maximum_fusion.4), channel_id=1, source_target_pairs={{0,2},{1,3},{2,0},{3,1},{4,6},{5,7},{6,4},{7,5},{8,10},{9,11},{10,... | collective-permute-start | bytes 786440 | tf_op jit(solution)/shard_map/ppermute | solution.py:251
  111.2 13.2 %collective-permute-start.18 = (bf16[8,128,128]{2,1,0:T(8,128)(2,1)S(1)}, bf16[8,128,128]{2,1,0:T(8,128)(2,1)S(1)}, u32[]{:S(2)}, u32[]{:S(2)}) collective-permute-start(bf16[8,128,128]{2,1,0:T(8,128)(2,1)S(1)} %copy-done.4), channel_id=1, source_target_pairs={{0,8},{1,9},{2,10},{3,11},{4,12},{5,13},{6,14},{7,15},{8,0},{9,1},... | collective-permute-start | bytes 786440 | tf_op jit(solution)/shard_map/ppermute | solution.py:251
  119.2 24.0 %collective-permute-start.26 = (bf16[16,128,128]{2,1,0:T(8,128)(2,1)S(1)}, bf16[16,128,128]{2,1,0:T(8,128)(2,1)S(1)}, u32[]{:S(2)}, u32[]{:S(2)}) collective-permute-start(bf16[16,128,128]{2,1,0:T(8,128)(2,1)S(1)} %pad_maximum_fusion.3), channel_id=1, source_target_pairs={{0,2},{1,3},{2,0},{3,1},{4,6},{5,7},{6,4},{7,5},{8,10},{9,11},{10,... | collective-permute-start | bytes 1572872 | tf_op jit(solution)/shard_map/ppermute | solution.py:251
  124.3 19.1 %collective-permute-start.25 = (bf16[16,128,128]{2,1,0:T(8,128)(2,1)S(1)}, bf16[16,128,128]{2,1,0:T(8,128)(2,1)S(1)}, u32[]{:S(2)}, u32[]{:S(2)}) collective-permute-start(bf16[16,128,128]{2,1,0:T(8,128)(2,1)S(1)} %pad_maximum_fusion.2), channel_id=1, source_target_pairs={{0,4},{1,5},{2,6},{3,7},{4,0},{5,1},{6,2},{7,3},{8,12},{9,13},{10,... | collective-permute-start | bytes 1572872 | tf_op jit(solution)/shard_map/ppermute | solution.py:251
  124.3 18.0 %collective-permute-start.23 = (bf16[8,128,128]{2,1,0:T(8,128)(2,1)S(1)}, bf16[8,128,128]{2,1,0:T(8,128)(2,1)S(1)}, u32[]{:S(2)}, u32[]{:S(2)}) collective-permute-start(bf16[8,128,128]{2,1,0:T(8,128)(2,1)S(1)} %collective-permute-done.18), channel_id=1, source_target_pairs={{0,4},{1,5},{2,6},{3,7},{4,0},{5,1},{6,2},{7,3},{8,12},{9,13},{10,... | collective-permute-start | bytes 786440 | tf_op jit(solution)/shard_map/ppermute | solution.py:251
  126.4 21.7 %collective-permute-start.28 = (bf16[8,128,128]{2,1,0:T(8,128)(2,1)S(1)}, bf16[8,128,128]{2,1,0:T(8,128)(2,1)S(1)}, u32[]{:S(2)}, u32[]{:S(2)}) collective-permute-start(bf16[8,128,128]{2,1,0:T(8,128)(2,1)S(1)} %collective-permute-done.22), channel_id=1, source_target_pairs={{0,2},{1,3},{2,0},{3,1},{4,6},{5,7},{6,4},{7,5},{8,10},{9,11},{10,... | collective-permute-start | bytes 786440 | tf_op jit(solution)/shard_map/ppermute | solution.py:251
  126.9 20.6 %collective-permute-start.27 = (bf16[8,128,128]{2,1,0:T(8,128)(2,1)S(1)}, bf16[8,128,128]{2,1,0:T(8,128)(2,1)S(1)}, u32[]{:S(2)}, u32[]{:S(2)}) collective-permute-start(bf16[8,128,128]{2,1,0:T(8,128)(2,1)S(1)} %collective-permute-done.18), channel_id=1, source_target_pairs={{0,2},{1,3},{2,0},{3,1},{4,6},{5,7},{6,4},{7,5},{8,10},{9,11},{10,... | collective-permute-start | bytes 786440 | tf_op jit(solution)/shard_map/ppermute | solution.py:251
  147.4 7.2 %collective-permute-start.32 = (bf16[32,128,128]{2,1,0:T(8,128)(2,1)S(1)}, bf16[32,128,128]{2,1,0:T(8,128)(2,1)S(1)}, u32[]{:S(2)}, u32[]{:S(2)}) collective-permute-start(bf16[32,128,128]{2,1,0:T(8,128)(2,1)S(1)} %pad_maximum_fusion.1.refs_2_), channel_id=1, source_target_pairs={{0,1},{1,0},{2,3},{3,2},{4,5},{5,4},{6,7},{7,6},{8,9},{9,8},{10,11... | collective-permute-start | bytes 3145736 | tf_op jit(solution)/shard_map/ppermute | solution.py:251
  147.4 7.2 %collective-permute-start.31 = (bf16[32,128,128]{2,1,0:T(8,128)(2,1)S(1)}, bf16[32,128,128]{2,1,0:T(8,128)(2,1)S(1)}, u32[]{:S(2)}, u32[]{:S(2)}) collective-permute-start(bf16[32,128,128]{2,1,0:T(8,128)(2,1)S(1)} %pad_maximum_fusion.refs_0_), channel_id=1, source_target_pairs={{0,1},{1,0},{2,3},{3,2},{4,5},{5,4},{6,7},{7,6},{8,9},{9,8},{10,11... | collective-permute-start | bytes 3145736 | tf_op jit(solution)/shard_map/ppermute | solution.py:251
  148.1 28.1 %collective-permute-start.33 = (bf16[56,128,128]{2,1,0:T(8,128)(2,1)S(1)}, bf16[56,128,128]{2,1,0:T(8,128)(2,1)}, u32[]{:S(2)}, u32[]{:S(2)}) collective-permute-start(bf16[56,128,128]{2,1,0:T(8,128)(2,1)S(1)} %constant_dynamic-update-slice_fusion.refs_0_), channel_id=1, source_target_pairs={{0,1},{1,0},{2,3},{3,2},{4,5},{5,4},{6,7},{7,6},{8,9},{9,8},{10,11... | collective-permute-start | bytes 5505032 | tf_op jit(solution)/shard_map/ppermute | solution.py:251
  148.2 6.3 %collective-permute-start.30 = (f32[144,256]{1,0:T(8,128)S(1)}, f32[144,256]{1,0:T(8,128)S(1)}, u32[]{:S(2)}, u32[]{:S(2)}) collective-permute-start(f32[144,256]{1,0:T(8,128)S(1)} %add.124), channel_id=1, source_target_pairs={{0,4},{1,5},{2,6},{3,7},{4,0},{5,1},{6,2},{7,3},{8,12},{9,13},{10,... | collective-permute-start | bytes 442376 | tf_op jit(solution)/shard_map/ppermute | solution.py:251
  148.6 21.6 %collective-permute-start.29 = (bf16[8,128,128]{2,1,0:T(8,128)(2,1)S(1)}, bf16[8,128,128]{2,1,0:T(8,128)(2,1)S(1)}, u32[]{:S(2)}, u32[]{:S(2)}) collective-permute-start(bf16[8,128,128]{2,1,0:T(8,128)(2,1)S(1)} %collective-permute-done.23), channel_id=1, source_target_pairs={{0,2},{1,3},{2,0},{3,1},{4,6},{5,7},{6,4},{7,5},{8,10},{9,11},{10,... | collective-permute-start | bytes 786440 | tf_op jit(solution)/shard_map/ppermute | solution.py:251
  154.5 13.4 %collective-permute-start.36 = (f32[144,256]{1,0:T(8,128)S(1)}, f32[144,256]{1,0:T(8,128)S(1)}, u32[]{:S(2)}, u32[]{:S(2)}) collective-permute-start(f32[144,256]{1,0:T(8,128)S(1)} %add.126), channel_id=1, source_target_pairs={{0,8},{1,9},{2,10},{3,11},{4,12},{5,13},{6,14},{7,15},{8,0},{9,1},... | collective-permute-start | bytes 442376 | tf_op jit(solution)/shard_map/ppermute | solution.py:251
  168.0 6.9 %collective-permute-start.37 = (f32[144,256]{1,0:T(8,128)S(1)}, f32[144,256]{1,0:T(8,128)S(1)}, u32[]{:S(2)}, u32[]{:S(2)}) collective-permute-start(f32[144,256]{1,0:T(8,128)S(1)} %add.127), channel_id=1, source_target_pairs={{0,16},{16,0},{1,17},{17,1},{2,18},{18,2},{3,19},{19,3},{4,20},{20... | collective-permute-start | bytes 442376 | tf_op jit(solution)/shard_map/ppermute | solution.py:251
  168.1 20.9 %collective-permute-start.35 = (bf16[2048,128]{1,0:T(8,128)(2,1)}, bf16[2048,128]{1,0:T(8,128)(2,1)S(1)}, u32[]{:S(2)}, u32[]{:S(2)}) collective-permute-start(bf16[2048,128]{1,0:T(8,128)(2,1)} %bitcast.24), channel_id=1, source_target_pairs={{0,16},{16,0},{1,17},{17,1},{2,18},{18,2},{3,19},{19,3},{4,20},{20... | collective-permute-start | bytes 1572872 | tf_op jit(solution)/shard_map/ppermute | solution.py:251
  (21 other events, 140.5 us)

commit v3 on v2

v3 whole, which is shorter than its diff:
```python
import functools
import math

import jax
import jax.numpy as jnp
from jax import lax
from jax.experimental import pallas as pl
from jax.experimental.pallas import tpu as pltpu
from jax.sharding import PartitionSpec as P

BF16 = jnp.bfloat16
F32 = jnp.float32
GROUP = 32
EARLY = 2
PARTS = 2
VMEM_LIMIT = 56 * 1024 * 1024


def orders(count):
    bits = [1 << k for k in range(count.bit_length() - 1)]
    swapped = list(bits)
    swapped[1], swapped[2] = bits[2], bits[1]
    return bits, swapped


def spot_of(apart, order):
    spot = apart * 0
    for k, bit in enumerate(reversed(order)):
        spot = spot + jnp.where((apart & bit) != 0, 1 << k, 0)
    return spot


def split_row(row, me, per_device, plan):
    run = per_device // len(plan)
    apart, at = (row // per_device) ^ me, row % per_device
    part = at // run
    spot = spot_of(apart, plan[0])
    for number, order in enumerate(plan[1:], 1):
        spot = jnp.where(part == number, spot_of(apart, order), spot)
    return spot, part, at % run


def clear(totals, count):
    steps = math.gcd(count, 16)
    height = count // steps

    def one(at, _):
        totals[pl.ds(at * height, height)] = jnp.zeros((height,) + totals.shape[1:], F32)
        return 0

    lax.fori_loop(0, steps, one, 0)


def start_table(sources, targets, table, scalars, sem):
    table[0:1, :] = sources
    table[1:2, :] = targets
    copy = pltpu.make_async_copy(table, scalars, sem)
    copy.start()
    return copy


def alive_slots(live, slots):
    return lax.broadcasted_iota(jnp.int32, (1, slots), 1) < live[0]


def block_copies(vals, held, sems):
    groups = held.shape[0] // GROUP
    part = lambda at: pl.ds(at * GROUP, GROUP)
    return [pltpu.make_async_copy(vals.at[part(at)], held.at[part(at)], sems.at[at]) for at in range(groups)]


def over_blocks(live, copies, body):
    for at, copy in enumerate(copies):

        @pl.when(at * GROUP < live[0])
        def _(at=at, copy=copy):
            copy.wait()
            for u in range(GROUP):
                body(at * GROUP + u)


def start_blocks(live, copies, first=0, last=None):
    for at, copy in list(enumerate(copies))[first:last]:

        @pl.when(at * GROUP < live[0])
        def _(copy=copy):
            copy.start()


def forward_kernel(
    plan, per_device, live, me, coords, vals, feats, keep, send, held, totals, rounded, table, scalars, sems, out_sems
):
    parts = len(plan)
    half, run = keep.shape[0], per_device // parts
    rows, below = 2 * half, half // per_device
    copies = block_copies(vals, held, sems)
    start_blocks(live, copies)
    spot, part, at = split_row(coords[0:1, :], me[0], per_device, plan)
    to = (((spot // below) * parts + part) * below + spot % below) * run + at
    to = jnp.where(alive_slots(live, to.shape[1]), to, rows)
    filled = start_table(coords[1:2, :], to, table, scalars, out_sems.at[0])
    clear(totals, rows)
    filled.wait()

    def one_slot(slot):
        to = scalars[1, slot]
        totals[to] += jnp.dot(held[slot], feats[scalars[0, slot]], preferred_element_type=F32)

    over_blocks(live, copies, one_slot)
    outs = []
    for at, out in ((1, send), (0, keep)):

        height = math.gcd(half, 8)

        def write(k, _, at=at):
            here = pl.ds(at * half + k * height, height)
            rounded[here] = totals[here].astype(BF16)
            return 0

        lax.fori_loop(0, half // height, write, 0)
        outs.append(pltpu.make_async_copy(rounded.at[pl.ds(at * half, half)], out, out_sems.at[at]))
        outs[-1].start()
    for out in outs:
        out.wait()


def forward_blocks(live, me, coords, vals, feats, plan, per_device):
    slots, size = vals.shape[0], vals.shape[1]
    width = feats.shape[2]
    rows = (1 << len(plan[0])) * per_device
    part = jax.ShapeDtypeStruct((rows // 2, size, width), BF16)
    smem, hbm = pl.BlockSpec(memory_space=pltpu.SMEM), pl.BlockSpec(memory_space=pl.ANY)
    vmem = pl.BlockSpec(memory_space=pltpu.VMEM)
    return pl.pallas_call(
        functools.partial(forward_kernel, plan, per_device),
        in_specs=[smem, smem, vmem, hbm, vmem],
        out_specs=[hbm, hbm],
        scratch_shapes=[
            pltpu.VMEM(vals.shape, BF16),
            pltpu.VMEM((rows + 1, size, width), F32),
            pltpu.VMEM((rows, size, width), BF16),
            pltpu.VMEM((2, slots), jnp.int32),
            pltpu.SMEM((2, slots), jnp.int32),
            pltpu.SemaphoreType.DMA((slots // GROUP,)),
            pltpu.SemaphoreType.DMA((2,)),
        ],
        out_shape=[part, part],
        compiler_params=pltpu.CompilerParams(vmem_limit_bytes=VMEM_LIMIT),
        cost_estimate=pl.CostEstimate(
            flops=8 * slots * size * size * width, bytes_accessed=4 * vals.size, transcendentals=0
        ),
        name="forward_blocks",
    )(live, me, coords, vals, feats)


def backward_kernel(plan, per_device, lengths, live, me, coords, vals, *refs):
    pieces, (out, held, grads, totals, table, scalars, sems, piece_sems) = refs[:-8], refs[-8:]
    run, cols, count = per_device // len(plan), out.shape[0], 1 << len(plan[0])
    copies = block_copies(vals, held, sems)
    fetches, start = [], 0
    for at, (piece, length) in enumerate(zip(pieces, lengths)):
        fetches.append(pltpu.make_async_copy(piece, grads.at[pl.ds(start, length)], piece_sems.at[at]))
        fetches[-1].start()
        start += length
    start_blocks(live, copies, last=EARLY)
    spot, part, at = split_row(coords[0:1, :], me[0], per_device, plan)
    alive = alive_slots(live, spot.shape[1])
    to = jnp.where(alive, coords[1:2, :], cols)
    filled = start_table((part * count + spot) * run + at, to, table, scalars, piece_sems.at[len(pieces)])
    clear(totals, cols)
    filled.wait()
    for fetch in fetches:
        fetch.wait()
    start_blocks(live, copies, first=EARLY)

    def one_slot(slot):
        to = scalars[1, slot]
        totals[to] += jnp.dot(grads[scalars[0, slot]], held[slot], preferred_element_type=F32)

    over_blocks(live, copies, one_slot)

    def write(at, _):
        out[at] = totals[at].T.astype(out.dtype)
        return 0

    lax.fori_loop(0, cols, write, 0)


def backward_blocks(live, me, coords, vals, pieces, cols, kind, plan, per_device):
    slots, size = vals.shape[0], vals.shape[1]
    width = pieces[0].shape[1]
    lengths = tuple(piece.shape[0] for piece in pieces)
    smem, hbm = pl.BlockSpec(memory_space=pltpu.SMEM), pl.BlockSpec(memory_space=pl.ANY)
    vmem = pl.BlockSpec(memory_space=pltpu.VMEM)
    return pl.pallas_call(
        functools.partial(backward_kernel, plan, per_device, lengths),
        in_specs=[smem, smem, vmem, hbm] + [hbm] * len(pieces),
        out_specs=pl.BlockSpec(memory_space=pltpu.VMEM),
        scratch_shapes=[
            pltpu.VMEM(vals.shape, BF16),
            pltpu.VMEM((sum(lengths), width, size), BF16),
            pltpu.VMEM((cols + 1, width, size), F32),
            pltpu.VMEM((2, slots), jnp.int32),
            pltpu.SMEM((2, slots), jnp.int32),
            pltpu.SemaphoreType.DMA((slots // GROUP,)),
            pltpu.SemaphoreType.DMA((len(pieces) + 1,)),
        ],
        out_shape=jax.ShapeDtypeStruct((cols, size, width), kind),
        compiler_params=pltpu.CompilerParams(vmem_limit_bytes=VMEM_LIMIT),
        cost_estimate=pl.CostEstimate(
            flops=8 * slots * size * size * width, bytes_accessed=4 * vals.size, transcendentals=0
        ),
        name="backward_blocks",
    )(live, me, coords, vals, *pieces)


def dense_kernel(first, *refs):
    terms_a, terms_b, (cot, weight, bias, out, grad_a, grad_b, terms) = refs[:4], refs[4:8], refs[8:]
    half = weight.shape[0] // 2
    size = grad_a.shape[2]
    at_a = pl.multiple_of(first[0] * half, half)
    at_b = pl.multiple_of((1 - first[0]) * half, half)

    def total(keep_0, got_0, keep_1, got_1):
        add_up = lambda x, y: (x[...].astype(F32) + y[...].astype(F32)).astype(BF16).reshape(-1, half)
        return jnp.concatenate([add_up(keep_0, got_0), add_up(keep_1, got_1)])

    agg_a, agg_b = total(*terms_a), total(*terms_b)
    weight_a, weight_b = weight[pl.ds(at_a, half), :], weight[pl.ds(at_b, half), :]
    preact = jnp.dot(agg_a, weight_a, preferred_element_type=F32)
    preact += jnp.dot(agg_b, weight_b, preferred_element_type=F32)
    preact += bias[...]
    gate = jax.nn.sigmoid(preact)
    out[...] = (preact * gate).astype(BF16)
    slope = gate * (1.0 + preact * (1.0 - gate))
    grad_pre = (cot[...].astype(F32) * slope).astype(BF16)
    over_rows = (((0,), (0,)), ((), ()))
    over_outputs = (((1,), (1,)), ((), ()))
    turned_a = lax.dot_general(weight_a, grad_pre, over_outputs, preferred_element_type=F32).astype(BF16)
    turned_b = lax.dot_general(weight_b, grad_pre, over_outputs, preferred_element_type=F32).astype(BF16)
    for at in range(grad_a.shape[0]):
        grad_a[at] = turned_a[:, at * size : (at + 1) * size]
        grad_b[at] = turned_b[:, at * size : (at + 1) * size]
    terms[pl.ds(at_a, half), :] = lax.dot_general(agg_a, grad_pre, over_rows, preferred_element_type=F32)
    terms[pl.ds(at_b, half), :] = lax.dot_general(agg_b, grad_pre, over_rows, preferred_element_type=F32)
    sums = jnp.sum(grad_pre.astype(F32), axis=0, keepdims=True)
    terms[2 * half :, :] = jnp.broadcast_to(sums, (terms.shape[0] - 2 * half, sums.shape[1]))


def dense(first, terms_a, terms_b, cot, weight, bias):
    run, size, half = terms_b[0].shape
    rows, width = cot.shape
    vmem = pl.BlockSpec(memory_space=pltpu.VMEM)
    turned = jax.ShapeDtypeStruct((rows // size, half, size), BF16)
    return pl.pallas_call(
        dense_kernel,
        in_specs=[pl.BlockSpec(memory_space=pltpu.SMEM)] + [vmem] * 11,
        out_specs=[vmem] * 4,
        out_shape=[
            jax.ShapeDtypeStruct((rows, width), BF16),
            turned,
            turned,
            jax.ShapeDtypeStruct((2 * half + 32, width), F32),
        ],
        compiler_params=pltpu.CompilerParams(vmem_limit_bytes=VMEM_LIMIT),
        cost_estimate=pl.CostEstimate(
            flops=8 * rows * width * width, bytes_accessed=8 * rows * width, transcendentals=rows * width
        ),
        name="dense_layer",
    )(first, *terms_a, *terms_b, cot, weight, bias)


def swap(array, axis, bit):
    return lax.ppermute(array, axis, [(at, at ^ bit) for at in range(lax.axis_size(axis))])


def after(array, *others):
    return lax.optimization_barrier((array, *others))[0]


def add(x, y):
    return (x.astype(F32) + y.astype(F32)).astype(BF16)


def halves(keep, got):
    half = keep.shape[0] // 2
    send = add(keep[half:], got[half:])
    return add(keep[:half], got[:half]), send


class SumOverAll:
    def __init__(self, terms):
        self.terms = self.got = terms
        self.bits = [1 << k for k in range(1, lax.axis_size("col").bit_length() - 1)]
        self.row_bits = [1]
        if lax.axis_size("row") == 2:
            half = terms.shape[0] // 2
            self.mine = lax.axis_index("col") % 2
            self.part = lax.dynamic_slice_in_dim(terms, self.mine * half, half)
            self.got = swap(lax.dynamic_slice_in_dim(terms, (1 - self.mine) * half, half), "col", 1)

    def step(self, take=lambda got: got):
        if lax.axis_size("row") == 2 and self.bits:
            self.part = self.part + take(self.got)
            if self.row_bits:
                self.got = swap(self.part, "row", self.row_bits.pop())
            else:
                self.got = swap(self.part, "col", self.bits.pop(0))

    def finish(self):
        if lax.axis_size("row") != 2:
            return lax.psum(self.terms, ("row", "col"))
        while self.bits:
            self.step()
        part = self.part + self.got
        other = swap(part, "col", 1)
        first, second = jnp.where(self.mine == 0, part, other), jnp.where(self.mine == 0, other, part)
        return jnp.concatenate([first, second])


def on_device(features, block_values, block_coords, live_blocks, weight, bias, cotangent):
    vals, coords, live = block_values[0, 0], block_coords[0, 0], live_blocks[0]
    size = vals.shape[1]
    row_count, count = lax.axis_size("row"), lax.axis_size("col")
    me = lax.axis_index("col").reshape(1)
    width = weight.shape[0]
    half = width // 2
    per_device = cotangent.shape[0] // size
    cols = features.shape[0] // size
    order_0, order_1 = orders(count)

    if row_count == 2:
        first = lax.axis_index("row").reshape(1)
        feats_a, feats_b = features, swap(features, "row", 1)
    else:
        first = jnp.zeros((1,), jnp.int32)
        feats = lax.all_gather(features, "row", axis=1, tiled=True)
        feats_a, feats_b = feats[:, :half], feats[:, half:]

    def products(feats, plan):
        keep, send = forward_blocks(live, me, coords, vals, feats.reshape(cols, size, half), plan, per_device)
        return keep, send, swap(send, "col", 1)

    def core_sums(keep, got):
        part = keep.shape[0] // 2
        return halves(keep[:part], got[:part]), halves(keep[part:], got[part:])

    plan_a, plan_b = (order_0, order_0), (order_0, order_1)
    keep_a, send_a, got_a = products(feats_a, plan_a)
    keep_b, send_b, got_b = products(after(feats_b, send_a), plan_b)
    parts = [*core_sums(keep_a, after(got_a, send_b)), *core_sums(keep_b, got_b)]
    plans = [*plan_a, *plan_b]
    taken, got = [got_b], {}

    def take(got):
        taken[0] = after(got, taken[0])
        return taken[0]

    steps = len(order_0) - 1
    turns = [(1, 0), (1, 3), (1, 1), (2, 0), (2, 1)]
    turns += [(step, part) for step in range(3, steps) for part in (0, 1)]
    turns += [(steps, 0), (1, 2), (2, 3), (2, 2), (steps, 1)]
    turns += [(step, part) for step in range(3, steps) for part in (3, 2)]
    turns += [(steps, 3), (steps, 2)]
    sent = {part: swap(parts[part][1], "col", plans[part][1]) for part in range(4)}
    for step, part in turns:
        sent[part] = take(sent[part])
        if step < steps:
            parts[part] = halves(parts[part][0], sent[part])
            sent[part] = swap(parts[part][1], "col", plans[part][step + 1])
    terms = []
    for part in range(4):
        terms += [parts[part][0], sent[part]]
    terms_a, terms_b = terms[:4], terms[4:]
    out, grad_a, grad_b, terms = dense(first, terms_a, terms_b, cotangent, weight, bias.reshape(1, -1))
    run = per_device // PARTS

    def input_grad(pieces, plan, kind):
        result = backward_blocks(live, me, coords, vals, pieces, cols, kind, plan, per_device)
        return result.reshape(-1, half)

    taken[0] = grad_b
    totals = SumOverAll(terms)
    outer, inner = list(reversed(order_0[2:])), order_0[1]
    steps_b = list(zip(reversed(order_0[1:-1]), reversed(order_1[1:-1])))
    cross = lambda piece: swap(piece, "col", inner)

    got_b = swap(grad_b, "col", outer[0])
    masks = [0]
    for bit in outer:
        masks = masks + [mask ^ bit for mask in masks]
    soon = [mask for mask in masks if not mask & outer[0]]
    pieces, crossed = {0: grad_a}, {0: cross(grad_a)}
    for mask in soon[1:]:
        pieces[mask] = swap(grad_a, "col", mask)
    crossed[0] = take(crossed[0])
    for mask in soon[1:]:
        pieces[mask] = take(pieces[mask])
        crossed[mask] = cross(pieces[mask])
    totals.step(take)
    got_b = take(got_b)
    for mask in masks:
        if mask not in pieces:
            pieces[mask] = swap(after(grad_a, got_b), "col", mask)
    parts_b = [jnp.concatenate([grad_b[at : at + run], got_b[at : at + run]]) for at in (0, run)]
    taken[0] = after(taken[0], *parts_b)
    late = [mask for mask in masks if mask not in soon]
    for at, bits in enumerate(steps_b):
        got = [swap(part, "col", bit) for part, bit in zip(parts_b, bits)]
        if at == 0:
            crossed.update({mask: take(crossed[mask]) for mask in soon[1:]})
        got[0] = take(got[0])
        if at == 1:
            core = {mask: [swap(piece[mask], "col", 1) for piece in (pieces, crossed)] for mask in soon}
            for mask in soon:
                core[mask] = [take(piece) for piece in core[mask]]
            totals.step(take)
        got[1] = take(got[1])
        parts_b = [jnp.concatenate([part, more]) for part, more in zip(parts_b, got)]
        taken[0] = after(taken[0], *parts_b)
        totals.step(take)
        if at == 0:
            for mask in late:
                pieces[mask] = take(pieces[mask])
                crossed[mask] = cross(pieces[mask])
    core_b = [take(swap(part, "col", 1)) for part in parts_b]
    pieces_b = [after(parts_b[0], *taken), core_b[0], parts_b[1], core_b[1]]

    part_b = input_grad(pieces_b, (order_0, order_1), BF16 if row_count == 2 else F32)
    for mask in late:
        crossed[mask] = after(crossed[mask], part_b)
        core[mask] = [swap(piece[mask], "col", 1) for piece in (pieces, crossed)]
    pieces_a = [pieces[mask] for mask in masks] + [crossed[mask] for mask in masks]
    pieces_a = pieces_a + [core[mask][0] for mask in masks] + [core[mask][1] for mask in masks]
    part_a = input_grad(pieces_a, (order_0,), F32)
    if row_count == 2:
        theirs = swap(part_b, "row", 1)
        grad_x = (part_a + theirs.astype(F32)).astype(BF16)
    else:
        partial_x = jnp.concatenate([part_a, part_b], axis=1)
        grad_x = lax.psum_scatter(partial_x, "row", scatter_dimension=1, tiled=True).astype(BF16)
    totals.got = after(totals.got, part_b)
    sums = totals.finish() * (cols * size * count) ** (-0.5)
    return out, grad_x, sums[:width], sums[width]


def solution(mesh):
    in_specs = (
        P("col", "row"),
        P("row", "col", None, None, None),
        P("row", "col", None, None),
        P("row", "col"),
        P(),
        P(),
        P(("row", "col"), None),
    )
    out_specs = (P(("row", "col"), None), P("col", "row"), P(), P())
    return jax.shard_map(
        on_device, mesh=mesh, in_specs=in_specs, out_specs=out_specs, check_vma=False
    )
```

time: 191 us -> 175 us (0.916)
  Pallas kernels: 56.7 us -> 32.8 us
  starting transfers between devices: 37.8 us -> 52.1 us
  waiting for transfers between devices: 79.3 us -> 73.4 us
    pallas_call x4, Pallas kernels: 53 us -> 29.2 us  [the longest x2 15.7 us: backward_blocks(): pl.pallas_call(functools.partial(backward_kernel, plan, per_device, lengt...]
    ppermute x38 -> x44, starting transfers between devices: 37.8 us -> 52.1 us  [swap(): lax.ppermute(array, axis, [(at, at ^ bit) for at in range(lax.axis_size(a...]
    ppermute x38 -> x44, waiting for transfers between devices: 79.3 us -> 73.4 us  [swap(): lax.ppermute(array, axis, [(at, at ^ bit) for at in range(lax.axis_size(a...]
  transfers between devices with their start and end apart: 38 -> 44, of which waited for: 19 -> 21; matrix products, arithmetic and copies ran while one was open for 4% -> 5% of each run, Pallas kernels for 28% -> 17%
where the time goes in v3:
time: 175 us
  waiting for transfers between devices  73.4 us (42%)
  starting transfers between devices  52.1 us (30%)
  Pallas kernels  32.8 us (19%)
  other arithmetic  7.98 us (5%)
  local copies, waits for them, and re-layouts  6.94 us (4%)
  between operations  1.83 us (1%)
    ppermute x44, waiting for transfers between devices, swap(): lax.ppermute(array, axis, [(at, at ^ bit) for at in range(lax.axis_size(a...  73.4 us
    ppermute x44, starting transfers between devices, swap(): lax.ppermute(array, axis, [(at, at ^ bit) for at in range(lax.axis_size(a...  52.1 us
    pallas_call x2, Pallas kernels, backward_blocks(): pl.pallas_call(functools.partial(backward_kernel, plan, per_device, lengt...  15.7 us
    pallas_call x2, Pallas kernels, forward_blocks(): pl.pallas_call(functools.partial(forward_kernel, plan, per_device), in_sp...  13.5 us
    convert_element_type x10, other arithmetic, add(): return (x.astype(F32) + y.astype(F32)).astype(BF16)  5.35 us
    unnamed x54, local copies, waits for them, and re-layouts  3.73 us
    pallas_call x1, Pallas kernels, dense(): pl.pallas_call(dense_kernel, in_specs=[pl.BlockSpec(memory_space=pltpu.SM...  3.67 us
  transfers between devices with their start and end apart: 44, of which 21 were waited for; matrix products, arithmetic and copies ran while one was open for 5% of the time, Pallas kernels for 17%

profile of v3, /device:TPU:0, one launch (start us, length us, event | category | flops | bytes accessed | tf_op | source)
XLA Modules:
  0.0 175.0 jit_solution(4941149549892907733)
XLA Ops:
  0.6 3.0 %collective-permute-start.1 = (bf16[2048,128]{1,0:T(8,128)(2,1)}, bf16[2048,128]{1,0:T(8,128)(2,1)S(1)}, u32[]{:S(2)}, u32[]{:S(2)}) collective-permute-start(bf16[2048,128]{1,0:T(8,128)(2,1)} %param.7), channel_id=1, source_target_pairs={{0,16},{16,0},{1,17},{17,1},{2,18},{18,2},{3,19},{19,3},{4,20},{20... | collective-permute-start | bytes 1572872 | tf_op jit(solution)/shard_map/ppermute | solution.py:274
  4.3 6.6 %forward_blocks.2 = (bf16[64,128,128]{2,1,0:T(8,128)(2,1)}, bf16[64,128,128]{2,1,0:T(8,128)(2,1)}) custom-call(s32[1]{0:T(128)} %bitcast.14.live, s32[1]{0:T(128)} %bitcast.2.me, s32[2,256]{1,0:T(2,128)} %bitcast.26, bf16[256,128,128]{2,1,0:T(8,128)(2,1)} %bitcast.19, bf16[16,128,128]{2,1,0:T(8,128)(2,1)} %bitcast.23), custom_call_target="tpu_custom_call" | custom-call | flops 4294967296 | bytes 16777216 | tf_op jit(solution)/shard_map/forward_blocks/pallas_call | solution.py:134
  11.0 4.8 %collective-permute-done.1 = bf16[2048,128]{1,0:T(8,128)(2,1)S(1)} collective-permute-done((bf16[2048,128]{1,0:T(8,128)(2,1)}, bf16[2048,128]{1,0:T(8,128)(2,1)S(1)}, u32[]{:S(2)}, u32[]{:S(2)}) %collective-permute-start.1) | collective-permute-done | bytes 524320 | tf_op jit(solution)/shard_map/ppermute | solution.py:274
  16.6 6.9 %forward_blocks.3 = (bf16[64,128,128]{2,1,0:T(8,128)(2,1)}, bf16[64,128,128]{2,1,0:T(8,128)(2,1)}) custom-call(s32[1]{0:T(128)} %bitcast.15.live, s32[1]{0:T(128)} %bitcast.2.me, s32[2,256]{1,0:T(2,128)} %bitcast.27, bf16[256,128,128]{2,1,0:T(8,128)(2,1)} %bitcast.20, bf16[16,128,128]{2,1,0:T(8,128)(2,1)} %bitcast.25), custom_call_target="tpu_custom_call" | custom-call | flops 4294967296 | bytes 16777216 | tf_op jit(solution)/shard_map/forward_blocks/pallas_call | solution.py:134
  24.4 3.7 %collective-permute-start.2 = (bf16[16,128,128]{2,1,0:T(8,128)(2,1)S(1)}, bf16[16,128,128]{2,1,0:T(8,128)(2,1)S(1)}, u32[]{:S(2)}, u32[]{:S(2)}) collective-permute-start(bf16[16,128,128]{2,1,0:T(8,128)(2,1)S(1)} %get-tuple-element.98), channel_id=1, source_target_pairs={{0,2},{1,3},{2,0},{3,1},{4,6},{5,7},{6,4},{7,5},{8,10},{9,11},{10,... | collective-permute-start | bytes 1572872 | tf_op jit(solution)/shard_map/ppermute | solution.py:274
  30.8 3.5 %collective-permute-start.5 = (bf16[16,128,128]{2,1,0:T(8,128)(2,1)S(1)}, bf16[16,128,128]{2,1,0:T(8,128)(2,1)S(1)}, u32[]{:S(2)}, u32[]{:S(2)}) collective-permute-start(bf16[16,128,128]{2,1,0:T(8,128)(2,1)S(1)} %get-tuple-element.97), channel_id=1, source_target_pairs={{0,2},{1,3},{2,0},{3,1},{4,6},{5,7},{6,4},{7,5},{8,10},{9,11},{10,... | collective-permute-start | bytes 1572872 | tf_op jit(solution)/shard_map/ppermute | solution.py:274
  34.3 6.6 %collective-permute-done.2 = bf16[16,128,128]{2,1,0:T(8,128)(2,1)S(1)} collective-permute-done((bf16[16,128,128]{2,1,0:T(8,128)(2,1)S(1)}, bf16[16,128,128]{2,1,0:T(8,128)(2,1)S(1)}, u32[]{:S(2)}, u32[]{:S(2)}) %collective-permute-start.2) | collective-permute-done | bytes 524320 | tf_op jit(solution)/shard_map/ppermute | solution.py:274
  44.6 7.5 %collective-permute-done.5 = bf16[16,128,128]{2,1,0:T(8,128)(2,1)S(1)} collective-permute-done((bf16[16,128,128]{2,1,0:T(8,128)(2,1)S(1)}, bf16[16,128,128]{2,1,0:T(8,128)(2,1)S(1)}, u32[]{:S(2)}, u32[]{:S(2)}) %collective-permute-start.5) | collective-permute-done | bytes 524320 | tf_op jit(solution)/shard_map/ppermute | solution.py:274
  54.6 2.6 %collective-permute-start.7 = (bf16[4,128,128]{2,1,0:T(8,128)(2,1)S(1)}, bf16[4,128,128]{2,1,0:T(8,128)(2,1)S(1)}, u32[]{:S(2)}, u32[]{:S(2)}) collective-permute-start(bf16[4,128,128]{2,1,0:T(8,128)(2,1)S(1)} %get-tuple-element.114), channel_id=1, source_target_pairs={{0,8},{1,9},{2,10},{3,11},{4,12},{5,13},{6,14},{7,15},{8,0},{9,1},... | collective-permute-start | bytes 393224 | tf_op jit(solution)/shard_map/ppermute | solution.py:274
  59.3 3.6 %collective-permute-done.8 = bf16[8,128,128]{2,1,0:T(8,128)(2,1)S(1)} collective-permute-done((bf16[8,128,128]{2,1,0:T(8,128)(2,1)S(1)}, bf16[8,128,128]{2,1,0:T(8,128)(2,1)S(1)}, u32[]{:S(2)}, u32[]{:S(2)}) %collective-permute-start.8) | collective-permute-done | bytes 262176 | tf_op jit(solution)/shard_map/ppermute | solution.py:274
  63.4 2.2 %collective-permute-start.11 = (bf16[8,128,128]{2,1,0:T(8,128)(2,1)S(1)}, bf16[8,128,128]{2,1,0:T(8,128)(2,1)S(1)}, u32[]{:S(2)}, u32[]{:S(2)}) collective-permute-start(bf16[8,128,128]{2,1,0:T(8,128)(2,1)S(1)} %get-tuple-element.103), channel_id=1, source_target_pairs={{0,4},{1,5},{2,6},{3,7},{4,0},{5,1},{6,2},{7,3},{8,12},{9,13},{10,... | collective-permute-start | bytes 786440 | tf_op jit(solution)/shard_map/ppermute | solution.py:274
  66.4 2.0 %collective-permute-start.9 = (bf16[4,128,128]{2,1,0:T(8,128)(2,1)S(1)}, bf16[4,128,128]{2,1,0:T(8,128)(2,1)S(1)}, u32[]{:S(2)}, u32[]{:S(2)}) collective-permute-start(bf16[4,128,128]{2,1,0:T(8,128)(2,1)S(1)} %get-tuple-element.112), channel_id=1, source_target_pairs={{0,8},{1,9},{2,10},{3,11},{4,12},{5,13},{6,14},{7,15},{8,0},{9,1},... | collective-permute-start | bytes 393224 | tf_op jit(solution)/shard_map/ppermute | solution.py:274
  70.8 4.3 %collective-permute-done.11 = bf16[8,128,128]{2,1,0:T(8,128)(2,1)S(1)} collective-permute-done((bf16[8,128,128]{2,1,0:T(8,128)(2,1)S(1)}, bf16[8,128,128]{2,1,0:T(8,128)(2,1)S(1)}, u32[]{:S(2)}, u32[]{:S(2)}) %collective-permute-start.11) | collective-permute-done | bytes 262176 | tf_op jit(solution)/shard_map/ppermute | solution.py:274
  76.9 7.4 %collective-permute-done.14.refs_7_ = bf16[4,128,128]{2,1,0:T(8,128)(2,1)S(1)} collective-permute-done((bf16[4,128,128]{2,1,0:T(8,128)(2,1)S(1)}, bf16[4,128,128]{2,1,0:T(8,128)(2,1)S(1)}, u32[]{:S(2)}, u32[]{:S(2)}) %collective-permute-start.14) | collective-permute-done | bytes 131104 | tf_op jit(solution)/shard_map/ppermute | solution.py:274
  84.3 2.3 %collective-permute-done.13.refs_5_ = bf16[4,128,128]{2,1,0:T(8,128)(2,1)S(1)} collective-permute-done((bf16[4,128,128]{2,1,0:T(8,128)(2,1)S(1)}, bf16[4,128,128]{2,1,0:T(8,128)(2,1)S(1)}, u32[]{:S(2)}, u32[]{:S(2)}) %collective-permute-start.13) | collective-permute-done | bytes 131104 | tf_op jit(solution)/shard_map/ppermute | solution.py:274
  87.2 3.7 %dense_layer.1 = (bf16[1024,256]{1,0:T(8,128)(2,1)}, bf16[8,128,128]{2,1,0:T(8,128)(2,1)}, bf16[8,128,128]{2,1,0:T(8,128)(2,1)}, f32[288,256]{1,0:T(8,128)}) custom-call(s32[1]{0:T(128)} %bitcast.first, bf16[4,128,128]{2,1,0:T(8,128)(2,1)} %get-tuple-element.115.refs_0_, bf16[4,128,128]{2,1,0:T(8,128)(2,1)} %copy-done.23, ...), custom_call_target="tpu_custom_call" | custom-call | flops 536870912 | bytes 2097152 | tf_op jit(solution)/shard_map/dense_layer/pallas_call | solution.py:255
  92.3 2.8 %collective-permute-start.15 = (bf16[8,128,128]{2,1,0:T(8,128)(2,1)}, bf16[8,128,128]{2,1,0:T(8,128)(2,1)S(1)}, u32[]{:S(2)}, u32[]{:S(2)}) collective-permute-start(bf16[8,128,128]{2,1,0:T(8,128)(2,1)} %get-tuple-element.68), channel_id=1, source_target_pairs={{0,8},{1,9},{2,10},{3,11},{4,12},{5,13},{6,14},{7,15},{8,0},{9,1},... | collective-permute-start | bytes 786440 | tf_op jit(solution)/shard_map/ppermute | solution.py:274
  99.0 4.1 %collective-permute-done.17.refs_2_ = bf16[8,128,128]{2,1,0:T(8,128)(2,1)S(1)} collective-permute-done((bf16[8,128,128]{2,1,0:T(8,128)(2,1)}, bf16[8,128,128]{2,1,0:T(8,128)(2,1)S(1)}, u32[]{:S(2)}, u32[]{:S(2)}) %collective-permute-start.17) | collective-permute-done | bytes 262176 | tf_op jit(solution)/shard_map/ppermute | solution.py:274
  103.0 2.2 %collective-permute-start.24 = (bf16[8,128,128]{2,1,0:T(8,128)(2,1)S(1)}, bf16[8,128,128]{2,1,0:T(8,128)(2,1)S(1)}, u32[]{:S(2)}, u32[]{:S(2)}) collective-permute-start(bf16[8,128,128]{2,1,0:T(8,128)(2,1)S(1)} %collective-permute-done.17.refs_2_), channel_id=1, source_target_pairs={{0,2},{1,3},{2,0},{3,1},{4,6},{5,7},{6,4},{7,5},{8,10},{9,11},{10,... | collective-permute-start | bytes 786440 | tf_op jit(solution)/shard_map/ppermute | solution.py:274
  107.1 2.8 %collective-permute-start.19 = (bf16[8,128,128]{2,1,0:T(8,128)(2,1)}, bf16[8,128,128]{2,1,0:T(8,128)(2,1)S(1)}, u32[]{:S(2)}, u32[]{:S(2)}) collective-permute-start(bf16[8,128,128]{2,1,0:T(8,128)(2,1)} %get-tuple-element.74.refs_0_), channel_id=1, source_target_pairs={{0,8},{1,9},{2,10},{3,11},{4,12},{5,13},{6,14},{7,15},{8,0},{9,1},... | collective-permute-start | bytes 786440 | tf_op jit(solution)/shard_map/ppermute | solution.py:274
  112.0 4.4 %collective-permute-done.23 = bf16[8,128,128]{2,1,0:T(8,128)(2,1)S(1)} collective-permute-done((bf16[8,128,128]{2,1,0:T(8,128)(2,1)S(1)}, bf16[8,128,128]{2,1,0:T(8,128)(2,1)S(1)}, u32[]{:S(2)}, u32[]{:S(2)}) %collective-permute-start.23) | collective-permute-done | bytes 262176 | tf_op jit(solution)/shard_map/ppermute | solution.py:274
  116.8 3.8 %collective-permute-done.26 = bf16[8,128,128]{2,1,0:T(8,128)(2,1)S(1)} collective-permute-done((bf16[8,128,128]{2,1,0:T(8,128)(2,1)S(1)}, bf16[8,128,128]{2,1,0:T(8,128)(2,1)S(1)}, u32[]{:S(2)}, u32[]{:S(2)}) %collective-permute-start.26) | collective-permute-done | bytes 262176 | tf_op jit(solution)/shard_map/ppermute | solution.py:274
  122.4 3.4 %collective-permute-done.20 = f32[144,256]{1,0:T(8,128)S(1)} collective-permute-done((f32[144,256]{1,0:T(8,128)S(1)}, f32[144,256]{1,0:T(8,128)S(1)}, u32[]{:S(2)}, u32[]{:S(2)}) %collective-permute-start.20) | collective-permute-done | bytes 147488 | tf_op jit(solution)/shard_map/ppermute | solution.py:274
  125.8 3.0 %collective-permute-done.19.refs_1_ = bf16[8,128,128]{2,1,0:T(8,128)(2,1)S(1)} collective-permute-done((bf16[8,128,128]{2,1,0:T(8,128)(2,1)}, bf16[8,128,128]{2,1,0:T(8,128)(2,1)S(1)}, u32[]{:S(2)}, u32[]{:S(2)}) %collective-permute-start.19) | collective-permute-done | bytes 262176 | tf_op jit(solution)/shard_map/ppermute | solution.py:274
  131.3 4.7 %collective-permute-done.28 = f32[144,256]{1,0:T(8,128)S(1)} collective-permute-done((f32[144,256]{1,0:T(8,128)S(1)}, f32[144,256]{1,0:T(8,128)S(1)}, u32[]{:S(2)}, u32[]{:S(2)}) %collective-permute-start.28) | collective-permute-done | bytes 147488 | tf_op jit(solution)/shard_map/ppermute | solution.py:274
  136.1 3.5 %collective-permute-done.27 = bf16[16,128,128]{2,1,0:T(8,128)(2,1)S(1)} collective-permute-done((bf16[16,128,128]{2,1,0:T(8,128)(2,1)S(1)}, bf16[16,128,128]{2,1,0:T(8,128)(2,1)S(1)}, u32[]{:S(2)}, u32[]{:S(2)}) %collective-permute-start.27) | collective-permute-done | bytes 524320 | tf_op jit(solution)/shard_map/ppermute | solution.py:274
  144.0 2.2 %collective-permute-done.35 = f32[144,256]{1,0:T(8,128)S(1)} collective-permute-done((f32[144,256]{1,0:T(8,128)S(1)}, f32[144,256]{1,0:T(8,128)S(1)}, u32[]{:S(2)}, u32[]{:S(2)}) %collective-permute-start.35) | collective-permute-done | bytes 147488 | tf_op jit(solution)/shard_map/ppermute | solution.py:274
  146.2 2.4 %collective-permute-start.42 = (f32[144,256]{1,0:T(8,128)S(1)}, f32[144,256]{1,0:T(8,128)S(1)}, u32[]{:S(2)}, u32[]{:S(2)}) collective-permute-start(f32[144,256]{1,0:T(8,128)S(1)} %add.131), channel_id=1, source_target_pairs={{0,8},{1,9},{2,10},{3,11},{4,12},{5,13},{6,14},{7,15},{8,0},{9,1},... | collective-permute-start | bytes 442376 | tf_op jit(solution)/shard_map/ppermute | solution.py:274
  149.9 7.7 %backward_blocks.2 = bf16[16,128,128]{2,1,0:T(8,128)(2,1)} custom-call(s32[1]{0:T(128)} %bitcast.16.live, s32[1]{0:T(128)} %bitcast.2.me, s32[2,256]{1,0:T(2,128)} %bitcast.28, bf16[256,128,128]{2,1,0:T(8,128)(2,1)} %bitcast.21, bf16[32,128,128]{2,1,0:T(8,128)(2,1)} %copy-done.2, bf16[32,128,128]{2,1,0:T(8,128)(2,1)} %copy-done.5, ...), custom_call_target="tpu_custom_call" | custom-call | flops 4294967296 | bytes 16777216 | tf_op jit(solution)/shard_map/backward_blocks/pallas_call | solution.py:195
  162.7 8.0 %backward_blocks.3 = f32[16,128,128]{2,1,0:T(8,128)} custom-call(s32[1]{0:T(128)} %bitcast.17.live, s32[1]{0:T(128)} %bitcast.2.me, s32[2,256]{1,0:T(2,128)} %bitcast.29, bf16[256,128,128]{2,1,0:T(8,128)(2,1)} %bitcast.22, bf16[8,128,128]{2,1,0:T(8,128)(2,1)} %get-tuple-element.74.refs_0_, bf16[8,128,128]{2,1,0:T(8,128)(2,1)} %copy-done.12, ...), custom_call_target="tpu_custom_call" | custom-call | flops 4294967296 | bytes 16777216 | tf_op jit(solution)/shard_map/backward_blocks/pallas_call | solution.py:195
  170.7 2.2 %collective-permute-done.41 = bf16[2048,128]{1,0:T(8,128)(2,1)S(1)} collective-permute-done((bf16[2048,128]{1,0:T(8,128)(2,1)}, bf16[2048,128]{1,0:T(8,128)(2,1)S(1)}, u32[]{:S(2)}, u32[]{:S(2)}) %collective-permute-start.41) | collective-permute-done | bytes 524320 | tf_op jit(solution)/shard_map/ppermute | solution.py:274
  172.9 2.1 %fusion = bf16[2048,128]{1,0:T(8,128)(2,1)} fusion(f32[16,128,128]{2,1,0:T(8,128)} %backward_blocks.3, bf16[2048,128]{1,0:T(8,128)(2,1)S(1)} %collective-permute-done.41), kind=kLoop, calls=%fused_computation.3 | loop fusion | flops 786432 | bytes 2097152 | tf_op jit(solution)/shard_map/convert_element_type | solution.py:438
  (144 shorter events, 43.3 us)
Async XLA Ops:
  0.6 15.2 %collective-permute-start.1 = (bf16[2048,128]{1,0:T(8,128)(2,1)}, bf16[2048,128]{1,0:T(8,128)(2,1)S(1)}, u32[]{:S(2)}, u32[]{:S(2)}) collective-permute-start(bf16[2048,128]{1,0:T(8,128)(2,1)} %param.7), channel_id=1, source_target_pairs={{0,16},{16,0},{1,17},{17,1},{2,18},{18,2},{3,19},{19,3},{4,20},{20... | collective-permute-start | bytes 1572872 | tf_op jit(solution)/shard_map/ppermute | solution.py:274
  10.9 12.7 %collective-permute-start = (bf16[64,128,128]{2,1,0:T(8,128)(2,1)}, bf16[64,128,128]{2,1,0:T(8,128)(2,1)S(1)}, u32[]{:S(2)}, u32[]{:S(2)}) collective-permute-start(bf16[64,128,128]{2,1,0:T(8,128)(2,1)} %get-tuple-element.49), channel_id=1, source_target_pairs={{0,1},{1,0},{2,3},{3,2},{4,5},{5,4},{6,7},{7,6},{8,9},{9,8},{10,11... | collective-permute-start | bytes 6291464 | tf_op jit(solution)/shard_map/ppermute | solution.py:274
  24.4 16.4 %collective-permute-start.2 = (bf16[16,128,128]{2,1,0:T(8,128)(2,1)S(1)}, bf16[16,128,128]{2,1,0:T(8,128)(2,1)S(1)}, u32[]{:S(2)}, u32[]{:S(2)}) collective-permute-start(bf16[16,128,128]{2,1,0:T(8,128)(2,1)S(1)} %get-tuple-element.98), channel_id=1, source_target_pairs={{0,2},{1,3},{2,0},{3,1},{4,6},{5,7},{6,4},{7,5},{8,10},{9,11},{10,... | collective-permute-start | bytes 1572872 | tf_op jit(solution)/shard_map/ppermute | solution.py:274
  29.2 15.4 %collective-permute-start.6 = (bf16[16,128,128]{2,1,0:T(8,128)(2,1)S(1)}, bf16[16,128,128]{2,1,0:T(8,128)(2,1)S(1)}, u32[]{:S(2)}, u32[]{:S(2)}) collective-permute-start(bf16[16,128,128]{2,1,0:T(8,128)(2,1)S(1)} %get-tuple-element.95), channel_id=1, source_target_pairs={{0,4},{1,5},{2,6},{3,7},{4,0},{5,1},{6,2},{7,3},{8,12},{9,13},{10,... | collective-permute-start | bytes 1572872 | tf_op jit(solution)/shard_map/ppermute | solution.py:274
  30.8 21.3 %collective-permute-start.5 = (bf16[16,128,128]{2,1,0:T(8,128)(2,1)S(1)}, bf16[16,128,128]{2,1,0:T(8,128)(2,1)S(1)}, u32[]{:S(2)}, u32[]{:S(2)}) collective-permute-start(bf16[16,128,128]{2,1,0:T(8,128)(2,1)S(1)} %get-tuple-element.97), channel_id=1, source_target_pairs={{0,2},{1,3},{2,0},{3,1},{4,6},{5,7},{6,4},{7,5},{8,10},{9,11},{10,... | collective-permute-start | bytes 1572872 | tf_op jit(solution)/shard_map/ppermute | solution.py:274
  41.0 11.2 %collective-permute-start.4 = (bf16[8,128,128]{2,1,0:T(8,128)(2,1)S(1)}, bf16[8,128,128]{2,1,0:T(8,128)(2,1)S(1)}, u32[]{:S(2)}, u32[]{:S(2)}) collective-permute-start(bf16[8,128,128]{2,1,0:T(8,128)(2,1)S(1)} %get-tuple-element.106), channel_id=1, source_target_pairs={{0,4},{1,5},{2,6},{3,7},{4,0},{5,1},{6,2},{7,3},{8,12},{9,13},{10,... | collective-permute-start | bytes 786440 | tf_op jit(solution)/shard_map/ppermute | solution.py:274
  42.6 20.7 %collective-permute-start.10 = (bf16[16,128,128]{2,1,0:T(8,128)(2,1)S(1)}, bf16[16,128,128]{2,1,0:T(8,128)(2,1)S(1)}, u32[]{:S(2)}, u32[]{:S(2)}) collective-permute-start(bf16[16,128,128]{2,1,0:T(8,128)(2,1)S(1)} %get-tuple-element.93), channel_id=1, source_target_pairs={{0,2},{1,3},{2,0},{3,1},{4,6},{5,7},{6,4},{7,5},{8,10},{9,11},{10,... | collective-permute-start | bytes 1572872 | tf_op jit(solution)/shard_map/ppermute | solution.py:274
  52.2 10.8 %collective-permute-start.8 = (bf16[8,128,128]{2,1,0:T(8,128)(2,1)S(1)}, bf16[8,128,128]{2,1,0:T(8,128)(2,1)S(1)}, u32[]{:S(2)}, u32[]{:S(2)}) collective-permute-start(bf16[8,128,128]{2,1,0:T(8,128)(2,1)S(1)} %get-tuple-element.105), channel_id=1, source_target_pairs={{0,4},{1,5},{2,6},{3,7},{4,0},{5,1},{6,2},{7,3},{8,12},{9,13},{10,... | collective-permute-start | bytes 786440 | tf_op jit(solution)/shard_map/ppermute | solution.py:274
  54.6 8.4 %collective-permute-start.7 = (bf16[4,128,128]{2,1,0:T(8,128)(2,1)S(1)}, bf16[4,128,128]{2,1,0:T(8,128)(2,1)S(1)}, u32[]{:S(2)}, u32[]{:S(2)}) collective-permute-start(bf16[4,128,128]{2,1,0:T(8,128)(2,1)S(1)} %get-tuple-element.114), channel_id=1, source_target_pairs={{0,8},{1,9},{2,10},{3,11},{4,12},{5,13},{6,14},{7,15},{8,0},{9,1},... | collective-permute-start | bytes 393224 | tf_op jit(solution)/shard_map/ppermute | solution.py:274
  57.3 11.4 %collective-permute-start.12 = (bf16[8,128,128]{2,1,0:T(8,128)(2,1)S(1)}, bf16[8,128,128]{2,1,0:T(8,128)(2,1)S(1)}, u32[]{:S(2)}, u32[]{:S(2)}) collective-permute-start(bf16[8,128,128]{2,1,0:T(8,128)(2,1)S(1)} %get-tuple-element.101), channel_id=1, source_target_pairs={{0,2},{1,3},{2,0},{3,1},{4,6},{5,7},{6,4},{7,5},{8,10},{9,11},{10,... | collective-permute-start | bytes 786440 | tf_op jit(solution)/shard_map/ppermute | solution.py:274
  63.4 11.6 %collective-permute-start.11 = (bf16[8,128,128]{2,1,0:T(8,128)(2,1)S(1)}, bf16[8,128,128]{2,1,0:T(8,128)(2,1)S(1)}, u32[]{:S(2)}, u32[]{:S(2)}) collective-permute-start(bf16[8,128,128]{2,1,0:T(8,128)(2,1)S(1)} %get-tuple-element.103), channel_id=1, source_target_pairs={{0,4},{1,5},{2,6},{3,7},{4,0},{5,1},{6,2},{7,3},{8,12},{9,13},{10,... | collective-permute-start | bytes 786440 | tf_op jit(solution)/shard_map/ppermute | solution.py:274
  66.4 10.5 %collective-permute-start.9 = (bf16[4,128,128]{2,1,0:T(8,128)(2,1)S(1)}, bf16[4,128,128]{2,1,0:T(8,128)(2,1)S(1)}, u32[]{:S(2)}, u32[]{:S(2)}) collective-permute-start(bf16[4,128,128]{2,1,0:T(8,128)(2,1)S(1)} %get-tuple-element.112), channel_id=1, source_target_pairs={{0,8},{1,9},{2,10},{3,11},{4,12},{5,13},{6,14},{7,15},{8,0},{9,1},... | collective-permute-start | bytes 393224 | tf_op jit(solution)/shard_map/ppermute | solution.py:274
  69.4 14.9 %collective-permute-start.14 = (bf16[4,128,128]{2,1,0:T(8,128)(2,1)S(1)}, bf16[4,128,128]{2,1,0:T(8,128)(2,1)S(1)}, u32[]{:S(2)}, u32[]{:S(2)}) collective-permute-start(bf16[4,128,128]{2,1,0:T(8,128)(2,1)S(1)} %get-tuple-element.109), channel_id=1, source_target_pairs={{0,8},{1,9},{2,10},{3,11},{4,12},{5,13},{6,14},{7,15},{8,0},{9,1},... | collective-permute-start | bytes 393224 | tf_op jit(solution)/shard_map/ppermute | solution.py:274
  75.8 10.8 %collective-permute-start.13 = (bf16[4,128,128]{2,1,0:T(8,128)(2,1)S(1)}, bf16[4,128,128]{2,1,0:T(8,128)(2,1)S(1)}, u32[]{:S(2)}, u32[]{:S(2)}) collective-permute-start(bf16[4,128,128]{2,1,0:T(8,128)(2,1)S(1)} %get-tuple-element.110), channel_id=1, source_target_pairs={{0,8},{1,9},{2,10},{3,11},{4,12},{5,13},{6,14},{7,15},{8,0},{9,1},... | collective-permute-start | bytes 393224 | tf_op jit(solution)/shard_map/ppermute | solution.py:274
  90.9 12.1 %collective-permute-start.17 = (bf16[8,128,128]{2,1,0:T(8,128)(2,1)}, bf16[8,128,128]{2,1,0:T(8,128)(2,1)S(1)}, u32[]{:S(2)}, u32[]{:S(2)}) collective-permute-start(bf16[8,128,128]{2,1,0:T(8,128)(2,1)} %get-tuple-element.74.refs_0_), channel_id=1, source_target_pairs={{0,4},{1,5},{2,6},{3,7},{4,0},{5,1},{6,2},{7,3},{8,12},{9,13},{10,... | collective-permute-start | bytes 786440 | tf_op jit(solution)/shard_map/ppermute | solution.py:274
  90.9 8.1 %collective-permute-start.18 = (bf16[8,128,128]{2,1,0:T(8,128)(2,1)}, bf16[8,128,128]{2,1,0:T(8,128)(2,1)S(1)}, u32[]{:S(2)}, u32[]{:S(2)}) collective-permute-start(bf16[8,128,128]{2,1,0:T(8,128)(2,1)} %get-tuple-element.74.refs_0_), channel_id=1, source_target_pairs={{0,2},{1,3},{2,0},{3,1},{4,6},{5,7},{6,4},{7,5},{8,10},{9,11},{10,... | collective-permute-start | bytes 786440 | tf_op jit(solution)/shard_map/ppermute | solution.py:274
  92.3 14.6 %collective-permute-start.15 = (bf16[8,128,128]{2,1,0:T(8,128)(2,1)}, bf16[8,128,128]{2,1,0:T(8,128)(2,1)S(1)}, u32[]{:S(2)}, u32[]{:S(2)}) collective-permute-start(bf16[8,128,128]{2,1,0:T(8,128)(2,1)} %get-tuple-element.68), channel_id=1, source_target_pairs={{0,8},{1,9},{2,10},{3,11},{4,12},{5,13},{6,14},{7,15},{8,0},{9,1},... | collective-permute-start | bytes 786440 | tf_op jit(solution)/shard_map/ppermute | solution.py:274
  96.0 9.2 %collective-permute-start.16 = (f32[144,256]{1,0:T(8,128)S(1)}, f32[144,256]{1,0:T(8,128)S(1)}, u32[]{:S(2)}, u32[]{:S(2)}) collective-permute-start(f32[144,256]{1,0:T(8,128)S(1)} %constant_dynamic-slice_fusion), channel_id=1, source_target_pairs={{0,1},{1,0},{2,3},{3,2},{4,5},{5,4},{6,7},{7,6},{8,9},{9,8},{10,11... | collective-permute-start | bytes 442376 | tf_op jit(solution)/shard_map/ppermute | solution.py:274
  103.0 8.3 %collective-permute-start.24 = (bf16[8,128,128]{2,1,0:T(8,128)(2,1)S(1)}, bf16[8,128,128]{2,1,0:T(8,128)(2,1)S(1)}, u32[]{:S(2)}, u32[]{:S(2)}) collective-permute-start(bf16[8,128,128]{2,1,0:T(8,128)(2,1)S(1)} %collective-permute-done.17.refs_2_), channel_id=1, source_target_pairs={{0,2},{1,3},{2,0},{3,1},{4,6},{5,7},{6,4},{7,5},{8,10},{9,11},{10,... | collective-permute-start | bytes 786440 | tf_op jit(solution)/shard_map/ppermute | solution.py:274
  106.9 9.4 %collective-permute-start.23 = (bf16[8,128,128]{2,1,0:T(8,128)(2,1)S(1)}, bf16[8,128,128]{2,1,0:T(8,128)(2,1)S(1)}, u32[]{:S(2)}, u32[]{:S(2)}) collective-permute-start(bf16[8,128,128]{2,1,0:T(8,128)(2,1)S(1)} %pad_maximum_fusion.4), channel_id=1, source_target_pairs={{0,4},{1,5},{2,6},{3,7},{4,0},{5,1},{6,2},{7,3},{8,12},{9,13},{10,... | collective-permute-start | bytes 786440 | tf_op jit(solution)/shard_map/ppermute | solution.py:274
  107.0 15.3 %collective-permute-start.32 = (bf16[8,128,128]{2,1,0:T(8,128)(2,1)}, bf16[8,128,128]{2,1,0:T(8,128)(2,1)S(1)}, u32[]{:S(2)}, u32[]{:S(2)}) collective-permute-start(bf16[8,128,128]{2,1,0:T(8,128)(2,1)} %get-tuple-element.74.refs_0_), channel_id=1, source_target_pairs={{0,1},{1,0},{2,3},{3,2},{4,5},{5,4},{6,7},{7,6},{8,9},{9,8},{10,11... | collective-permute-start | bytes 786440 | tf_op jit(solution)/shard_map/ppermute | solution.py:274
  107.1 21.7 %collective-permute-start.19 = (bf16[8,128,128]{2,1,0:T(8,128)(2,1)}, bf16[8,128,128]{2,1,0:T(8,128)(2,1)S(1)}, u32[]{:S(2)}, u32[]{:S(2)}) collective-permute-start(bf16[8,128,128]{2,1,0:T(8,128)(2,1)} %get-tuple-element.74.refs_0_), channel_id=1, source_target_pairs={{0,8},{1,9},{2,10},{3,11},{4,12},{5,13},{6,14},{7,15},{8,0},{9,1},... | collective-permute-start | bytes 786440 | tf_op jit(solution)/shard_map/ppermute | solution.py:274
  109.9 18.8 %collective-permute-start.21 = (bf16[8,128,128]{2,1,0:T(8,128)(2,1)}, bf16[8,128,128]{2,1,0:T(8,128)(2,1)S(1)}, u32[]{:S(2)}, u32[]{:S(2)}) collective-permute-start(bf16[8,128,128]{2,1,0:T(8,128)(2,1)} %get-tuple-element.74.refs_0_), channel_id=1, source_target_pairs={{0,12},{1,13},{2,14},{3,15},{4,8},{5,9},{6,10},{7,11},{8,4},{9,5},... | collective-permute-start | bytes 786440 | tf_op jit(solution)/shard_map/ppermute | solution.py:274
  111.4 9.2 %collective-permute-start.26 = (bf16[8,128,128]{2,1,0:T(8,128)(2,1)S(1)}, bf16[8,128,128]{2,1,0:T(8,128)(2,1)S(1)}, u32[]{:S(2)}, u32[]{:S(2)}) collective-permute-start(bf16[8,128,128]{2,1,0:T(8,128)(2,1)S(1)} %pad_maximum_fusion.5), channel_id=1, source_target_pairs={{0,2},{1,3},{2,0},{3,1},{4,6},{5,7},{6,4},{7,5},{8,10},{9,11},{10,... | collective-permute-start | bytes 786440 | tf_op jit(solution)/shard_map/ppermute | solution.py:274
  116.4 14.5 %collective-permute-start.25 = (bf16[16,128,128]{2,1,0:T(8,128)(2,1)S(1)}, bf16[16,128,128]{2,1,0:T(8,128)(2,1)S(1)}, u32[]{:S(2)}, u32[]{:S(2)}) collective-permute-start(bf16[16,128,128]{2,1,0:T(8,128)(2,1)S(1)} %pad_maximum_fusion.2), channel_id=1, source_target_pairs={{0,2},{1,3},{2,0},{3,1},{4,6},{5,7},{6,4},{7,5},{8,10},{9,11},{10,... | collective-permute-start | bytes 1572872 | tf_op jit(solution)/shard_map/ppermute | solution.py:274
  122.3 17.3 %collective-permute-start.27 = (bf16[16,128,128]{2,1,0:T(8,128)(2,1)S(1)}, bf16[16,128,128]{2,1,0:T(8,128)(2,1)S(1)}, u32[]{:S(2)}, u32[]{:S(2)}) collective-permute-start(bf16[16,128,128]{2,1,0:T(8,128)(2,1)S(1)} %pad_maximum_fusion.3), channel_id=1, source_target_pairs={{0,4},{1,5},{2,6},{3,7},{4,0},{5,1},{6,2},{7,3},{8,12},{9,13},{10,... | collective-permute-start | bytes 1572872 | tf_op jit(solution)/shard_map/ppermute | solution.py:274
  139.6 9.0 %collective-permute-start.34 = (bf16[32,128,128]{2,1,0:T(8,128)(2,1)S(1)}, bf16[32,128,128]{2,1,0:T(8,128)(2,1)S(1)}, u32[]{:S(2)}, u32[]{:S(2)}) collective-permute-start(bf16[32,128,128]{2,1,0:T(8,128)(2,1)S(1)} %pad_maximum_fusion.refs_0_), channel_id=1, source_target_pairs={{0,1},{1,0},{2,3},{3,2},{4,5},{5,4},{6,7},{7,6},{8,9},{9,8},{10,11... | collective-permute-start | bytes 3145736 | tf_op jit(solution)/shard_map/ppermute | solution.py:274
  139.8 8.8 %collective-permute-start.33 = (bf16[32,128,128]{2,1,0:T(8,128)(2,1)S(1)}, bf16[32,128,128]{2,1,0:T(8,128)(2,1)S(1)}, u32[]{:S(2)}, u32[]{:S(2)}) collective-permute-start(bf16[32,128,128]{2,1,0:T(8,128)(2,1)S(1)} %pad_maximum_fusion.1.refs_2_), channel_id=1, source_target_pairs={{0,1},{1,0},{2,3},{3,2},{4,5},{5,4},{6,7},{7,6},{8,9},{9,8},{10,11... | collective-permute-start | bytes 3145736 | tf_op jit(solution)/shard_map/ppermute | solution.py:274
  142.0 16.4 %collective-permute-start.22 = (bf16[8,128,128]{2,1,0:T(8,128)(2,1)S(1)}, bf16[8,128,128]{2,1,0:T(8,128)(2,1)S(1)}, u32[]{:S(2)}, u32[]{:S(2)}) collective-permute-start(bf16[8,128,128]{2,1,0:T(8,128)(2,1)S(1)} %collective-permute-done.19.refs_1_), channel_id=1, source_target_pairs={{0,2},{1,3},{2,0},{3,1},{4,6},{5,7},{6,4},{7,5},{8,10},{9,11},{10,... | collective-permute-start | bytes 786440 | tf_op jit(solution)/shard_map/ppermute | solution.py:274
  142.5 17.4 %collective-permute-start.36 = (bf16[8,128,128]{2,1,0:T(8,128)(2,1)S(1)}, bf16[8,128,128]{2,1,0:T(8,128)(2,1)S(1)}, u32[]{:S(2)}, u32[]{:S(2)}) collective-permute-start(bf16[8,128,128]{2,1,0:T(8,128)(2,1)S(1)} %collective-permute-done.21.refs_3_), channel_id=1, source_target_pairs={{0,2},{1,3},{2,0},{3,1},{4,6},{5,7},{6,4},{7,5},{8,10},{9,11},{10,... | collective-permute-start | bytes 786440 | tf_op jit(solution)/shard_map/ppermute | solution.py:274
  146.2 11.4 %collective-permute-start.42 = (f32[144,256]{1,0:T(8,128)S(1)}, f32[144,256]{1,0:T(8,128)S(1)}, u32[]{:S(2)}, u32[]{:S(2)}) collective-permute-start(f32[144,256]{1,0:T(8,128)S(1)} %add.131), channel_id=1, source_target_pairs={{0,8},{1,9},{2,10},{3,11},{4,12},{5,13},{6,14},{7,15},{8,0},{9,1},... | collective-permute-start | bytes 442376 | tf_op jit(solution)/shard_map/ppermute | solution.py:274
  158.4 14.5 %collective-permute-start.41 = (bf16[2048,128]{1,0:T(8,128)(2,1)}, bf16[2048,128]{1,0:T(8,128)(2,1)S(1)}, u32[]{:S(2)}, u32[]{:S(2)}) collective-permute-start(bf16[2048,128]{1,0:T(8,128)(2,1)} %bitcast.24), channel_id=1, source_target_pairs={{0,16},{16,0},{1,17},{17,1},{2,18},{18,2},{3,19},{19,3},{4,20},{20... | collective-permute-start | bytes 1572872 | tf_op jit(solution)/shard_map/ppermute | solution.py:274
  (39 other events, 334.0 us)

commit v4 on v3

--- a/solution.py
+++ b/solution.py
@@ -180,7 +180,7 @@
     over_blocks(live, copies, one_slot)
 
     def write(at, _):
-        out[at] = totals[at].T.astype(out.dtype)
+        out[at] = totals[at].astype(out.dtype).T
         return 0
 
     lax.fori_loop(0, cols, write, 0)
@@ -418,8 +418,8 @@
         got[1] = take(got[1])
         parts_b = [jnp.concatenate([part, more]) for part, more in zip(parts_b, got)]
         taken[0] = after(taken[0], *parts_b)
-        totals.step(take)
         if at == 0:
+            totals.step(take)
             for mask in late:
                 pieces[mask] = take(pieces[mask])
                 crossed[mask] = cross(pieces[mask])
@@ -427,19 +427,21 @@
     pieces_b = [after(parts_b[0], *taken), core_b[0], parts_b[1], core_b[1]]
 
     part_b = input_grad(pieces_b, (order_0, order_1), BF16 if row_count == 2 else F32)
+    totals.got, part_b = lax.optimization_barrier((totals.got, part_b))
+    totals.step()
     for mask in late:
         crossed[mask] = after(crossed[mask], part_b)
         core[mask] = [swap(piece[mask], "col", 1) for piece in (pieces, crossed)]
     pieces_a = [pieces[mask] for mask in masks] + [crossed[mask] for mask in masks]
     pieces_a = pieces_a + [core[mask][0] for mask in masks] + [core[mask][1] for mask in masks]
     part_a = input_grad(pieces_a, (order_0,), F32)
+    totals.got, part_a = lax.optimization_barrier((totals.got, part_a))
     if row_count == 2:
         theirs = swap(part_b, "row", 1)
         grad_x = (part_a + theirs.astype(F32)).astype(BF16)
     else:
         partial_x = jnp.concatenate([part_a, part_b], axis=1)
         grad_x = lax.psum_scatter(partial_x, "row", scatter_dimension=1, tiled=True).astype(BF16)
-    totals.got = after(totals.got, part_b)
     sums = totals.finish() * (cols * size * count) ** (-0.5)
     return out, grad_x, sums[:width], sums[width]
 

time: 175 us -> 171 us (0.977)
  starting transfers between devices: 52.1 us -> 48.9 us
    ppermute x44, starting transfers between devices: 52.1 us -> 48.9 us  [swap(): lax.ppermute(array, axis, [(at, at ^ bit) for at in range(lax.axis_size(a...]
    unnamed x54 -> x56, local copies, waits for them, and re-layouts: 3.73 us -> 3.28 us
  transfers between devices with their start and end apart: 44 -> 44, of which waited for: 21 -> 23; matrix products, arithmetic and copies ran while one was open for 5% -> 5% of each run, Pallas kernels for 17% -> 17%
where the time goes in v4:
time: 171 us
  waiting for transfers between devices  74.8 us (44%)
  starting transfers between devices  48.9 us (29%)
  Pallas kernels  32.5 us (19%)
  other arithmetic  6.73 us (4%)
  local copies, waits for them, and re-layouts  6.49 us (4%)
  between operations  1.82 us (1%)
    ppermute x44, waiting for transfers between devices, swap(): lax.ppermute(array, axis, [(at, at ^ bit) for at in range(lax.axis_size(a...  74.8 us
    ppermute x44, starting transfers between devices, swap(): lax.ppermute(array, axis, [(at, at ^ bit) for at in range(lax.axis_size(a...  48.9 us
    pallas_call x2, Pallas kernels, backward_blocks(): pl.pallas_call(functools.partial(backward_kernel, plan, per_device, lengt...  15.4 us
    pallas_call x2, Pallas kernels, forward_blocks(): pl.pallas_call(functools.partial(forward_kernel, plan, per_device), in_sp...  13.5 us
    convert_element_type x10, other arithmetic, add(): return (x.astype(F32) + y.astype(F32)).astype(BF16)  5.32 us
    pallas_call x1, Pallas kernels, dense(): pl.pallas_call(dense_kernel, in_specs=[pl.BlockSpec(memory_space=pltpu.SM...  3.67 us
  transfers between devices with their start and end apart: 44, of which 23 were waited for; matrix products, arithmetic and copies ran while one was open for 5% of the time, Pallas kernels for 17%

profile of v4, /device:TPU:0, one launch (start us, length us, event | category | flops | bytes accessed | tf_op | source)
XLA Modules:
  0.0 171.2 jit_solution(16039309361402314266)
XLA Ops:
  0.6 3.0 %collective-permute-start.1 = (bf16[2048,128]{1,0:T(8,128)(2,1)}, bf16[2048,128]{1,0:T(8,128)(2,1)S(1)}, u32[]{:S(2)}, u32[]{:S(2)}) collective-permute-start(bf16[2048,128]{1,0:T(8,128)(2,1)} %param.7), channel_id=1, source_target_pairs={{0,16},{16,0},{1,17},{17,1},{2,18},{18,2},{3,19},{19,3},{4,20},{20... | collective-permute-start | bytes 1572872 | tf_op jit(solution)/shard_map/ppermute | solution.py:274
  4.3 6.6 %forward_blocks.2 = (bf16[64,128,128]{2,1,0:T(8,128)(2,1)}, bf16[64,128,128]{2,1,0:T(8,128)(2,1)}) custom-call(s32[1]{0:T(128)} %bitcast.11.live, s32[1]{0:T(128)} %bitcast.2.me, s32[2,256]{1,0:T(2,128)} %bitcast.24, bf16[256,128,128]{2,1,0:T(8,128)(2,1)} %bitcast.17, bf16[16,128,128]{2,1,0:T(8,128)(2,1)} %bitcast.21), custom_call_target="tpu_custom_call" | custom-call | flops 4294967296 | bytes 16777216 | tf_op jit(solution)/shard_map/forward_blocks/pallas_call | solution.py:134
  12.4 3.4 %collective-permute-done.1 = bf16[2048,128]{1,0:T(8,128)(2,1)S(1)} collective-permute-done((bf16[2048,128]{1,0:T(8,128)(2,1)}, bf16[2048,128]{1,0:T(8,128)(2,1)S(1)}, u32[]{:S(2)}, u32[]{:S(2)}) %collective-permute-start.1) | collective-permute-done | bytes 524320 | tf_op jit(solution)/shard_map/ppermute | solution.py:274
  16.6 6.9 %forward_blocks.3 = (bf16[64,128,128]{2,1,0:T(8,128)(2,1)}, bf16[64,128,128]{2,1,0:T(8,128)(2,1)}) custom-call(s32[1]{0:T(128)} %bitcast.12.live, s32[1]{0:T(128)} %bitcast.2.me, s32[2,256]{1,0:T(2,128)} %bitcast.25, bf16[256,128,128]{2,1,0:T(8,128)(2,1)} %bitcast.18, bf16[16,128,128]{2,1,0:T(8,128)(2,1)} %bitcast.23), custom_call_target="tpu_custom_call" | custom-call | flops 4294967296 | bytes 16777216 | tf_op jit(solution)/shard_map/forward_blocks/pallas_call | solution.py:134
  26.2 2.6 %collective-permute-done.3 = bf16[64,128,128]{2,1,0:T(8,128)(2,1)S(1)} collective-permute-done((bf16[64,128,128]{2,1,0:T(8,128)(2,1)}, bf16[64,128,128]{2,1,0:T(8,128)(2,1)S(1)}, u32[]{:S(2)}, u32[]{:S(2)}) %collective-permute-start.3) | collective-permute-done | bytes 2097184 | tf_op jit(solution)/shard_map/ppermute | solution.py:274
  30.0 2.0 %collective-permute-start.5 = (bf16[16,128,128]{2,1,0:T(8,128)(2,1)S(1)}, bf16[16,128,128]{2,1,0:T(8,128)(2,1)S(1)}, u32[]{:S(2)}, u32[]{:S(2)}) collective-permute-start(bf16[16,128,128]{2,1,0:T(8,128)(2,1)S(1)} %get-tuple-element.101), channel_id=1, source_target_pairs={{0,2},{1,3},{2,0},{3,1},{4,6},{5,7},{6,4},{7,5},{8,10},{9,11},{10,... | collective-permute-start | bytes 1572872 | tf_op jit(solution)/shard_map/ppermute | solution.py:274
  31.9 8.5 %collective-permute-done.2 = bf16[16,128,128]{2,1,0:T(8,128)(2,1)S(1)} collective-permute-done((bf16[16,128,128]{2,1,0:T(8,128)(2,1)S(1)}, bf16[16,128,128]{2,1,0:T(8,128)(2,1)S(1)}, u32[]{:S(2)}, u32[]{:S(2)}) %collective-permute-start.2) | collective-permute-done | bytes 524320 | tf_op jit(solution)/shard_map/ppermute | solution.py:274
  42.2 2.4 %collective-permute-done.6 = bf16[16,128,128]{2,1,0:T(8,128)(2,1)S(1)} collective-permute-done((bf16[16,128,128]{2,1,0:T(8,128)(2,1)S(1)}, bf16[16,128,128]{2,1,0:T(8,128)(2,1)S(1)}, u32[]{:S(2)}, u32[]{:S(2)}) %collective-permute-start.6) | collective-permute-done | bytes 524320 | tf_op jit(solution)/shard_map/ppermute | solution.py:274
  44.7 7.0 %collective-permute-done.5 = bf16[16,128,128]{2,1,0:T(8,128)(2,1)S(1)} collective-permute-done((bf16[16,128,128]{2,1,0:T(8,128)(2,1)S(1)}, bf16[16,128,128]{2,1,0:T(8,128)(2,1)S(1)}, u32[]{:S(2)}, u32[]{:S(2)}) %collective-permute-start.5) | collective-permute-done | bytes 524320 | tf_op jit(solution)/shard_map/ppermute | solution.py:274
  52.6 4.1 %collective-permute-start.7 = (bf16[4,128,128]{2,1,0:T(8,128)(2,1)S(1)}, bf16[4,128,128]{2,1,0:T(8,128)(2,1)S(1)}, u32[]{:S(2)}, u32[]{:S(2)}) collective-permute-start(bf16[4,128,128]{2,1,0:T(8,128)(2,1)S(1)} %get-tuple-element.118), channel_id=1, source_target_pairs={{0,8},{1,9},{2,10},{3,11},{4,12},{5,13},{6,14},{7,15},{8,0},{9,1},... | collective-permute-start | bytes 393224 | tf_op jit(solution)/shard_map/ppermute | solution.py:274
  58.3 2.8 %collective-permute-done.8 = bf16[8,128,128]{2,1,0:T(8,128)(2,1)S(1)} collective-permute-done((bf16[8,128,128]{2,1,0:T(8,128)(2,1)S(1)}, bf16[8,128,128]{2,1,0:T(8,128)(2,1)S(1)}, u32[]{:S(2)}, u32[]{:S(2)}) %collective-permute-start.8) | collective-permute-done | bytes 262176 | tf_op jit(solution)/shard_map/ppermute | solution.py:274
  61.1 1.7 %collective-permute-done.10 = bf16[16,128,128]{2,1,0:T(8,128)(2,1)S(1)} collective-permute-done((bf16[16,128,128]{2,1,0:T(8,128)(2,1)S(1)}, bf16[16,128,128]{2,1,0:T(8,128)(2,1)S(1)}, u32[]{:S(2)}, u32[]{:S(2)}) %collective-permute-start.10) | collective-permute-done | bytes 524320 | tf_op jit(solution)/shard_map/ppermute | solution.py:274
  64.4 3.5 %collective-permute-start.9 = (bf16[4,128,128]{2,1,0:T(8,128)(2,1)S(1)}, bf16[4,128,128]{2,1,0:T(8,128)(2,1)S(1)}, u32[]{:S(2)}, u32[]{:S(2)}) collective-permute-start(bf16[4,128,128]{2,1,0:T(8,128)(2,1)S(1)} %get-tuple-element.116), channel_id=1, source_target_pairs={{0,8},{1,9},{2,10},{3,11},{4,12},{5,13},{6,14},{7,15},{8,0},{9,1},... | collective-permute-start | bytes 393224 | tf_op jit(solution)/shard_map/ppermute | solution.py:274
  69.9 2.8 %collective-permute-done.11 = bf16[8,128,128]{2,1,0:T(8,128)(2,1)S(1)} collective-permute-done((bf16[8,128,128]{2,1,0:T(8,128)(2,1)S(1)}, bf16[8,128,128]{2,1,0:T(8,128)(2,1)S(1)}, u32[]{:S(2)}, u32[]{:S(2)}) %collective-permute-start.11) | collective-permute-done | bytes 262176 | tf_op jit(solution)/shard_map/ppermute | solution.py:274
  74.8 7.5 %collective-permute-done.14.refs_7_ = bf16[4,128,128]{2,1,0:T(8,128)(2,1)S(1)} collective-permute-done((bf16[4,128,128]{2,1,0:T(8,128)(2,1)S(1)}, bf16[4,128,128]{2,1,0:T(8,128)(2,1)S(1)}, u32[]{:S(2)}, u32[]{:S(2)}) %collective-permute-start.14) | collective-permute-done | bytes 131104 | tf_op jit(solution)/shard_map/ppermute | solution.py:274
  82.3 2.2 %collective-permute-done.13.refs_5_ = bf16[4,128,128]{2,1,0:T(8,128)(2,1)S(1)} collective-permute-done((bf16[4,128,128]{2,1,0:T(8,128)(2,1)S(1)}, bf16[4,128,128]{2,1,0:T(8,128)(2,1)S(1)}, u32[]{:S(2)}, u32[]{:S(2)}) %collective-permute-start.13) | collective-permute-done | bytes 131104 | tf_op jit(solution)/shard_map/ppermute | solution.py:274
  85.2 3.7 %dense_layer.1 = (bf16[1024,256]{1,0:T(8,128)(2,1)}, bf16[8,128,128]{2,1,0:T(8,128)(2,1)}, bf16[8,128,128]{2,1,0:T(8,128)(2,1)}, f32[288,256]{1,0:T(8,128)}) custom-call(s32[1]{0:T(128)} %bitcast.first, bf16[4,128,128]{2,1,0:T(8,128)(2,1)} %get-tuple-element.119.refs_0_, bf16[4,128,128]{2,1,0:T(8,128)(2,1)} %copy-done.24, ...), custom_call_target="tpu_custom_call" | custom-call | flops 536870912 | bytes 2097152 | tf_op jit(solution)/shard_map/dense_layer/pallas_call | solution.py:255
  90.4 2.4 %collective-permute-start.25 = (bf16[8,128,128]{2,1,0:T(8,128)(2,1)}, bf16[8,128,128]{2,1,0:T(8,128)(2,1)S(1)}, u32[]{:S(2)}, u32[]{:S(2)}) collective-permute-start(bf16[8,128,128]{2,1,0:T(8,128)(2,1)} %get-tuple-element.71), channel_id=1, source_target_pairs={{0,8},{1,9},{2,10},{3,11},{4,12},{5,13},{6,14},{7,15},{8,0},{9,1},... | collective-permute-start | bytes 786440 | tf_op jit(solution)/shard_map/ppermute | solution.py:274
  94.9 2.0 %collective-permute-done.17.refs_4_ = bf16[8,128,128]{2,1,0:T(8,128)(2,1)S(1)} collective-permute-done((bf16[8,128,128]{2,1,0:T(8,128)(2,1)}, bf16[8,128,128]{2,1,0:T(8,128)(2,1)S(1)}, u32[]{:S(2)}, u32[]{:S(2)}) %collective-permute-start.17) | collective-permute-done | bytes 262176 | tf_op jit(solution)/shard_map/ppermute | solution.py:274
  96.9 4.1 %collective-permute-done.16.refs_2_ = bf16[8,128,128]{2,1,0:T(8,128)(2,1)S(1)} collective-permute-done((bf16[8,128,128]{2,1,0:T(8,128)(2,1)}, bf16[8,128,128]{2,1,0:T(8,128)(2,1)S(1)}, u32[]{:S(2)}, u32[]{:S(2)}) %collective-permute-start.16) | collective-permute-done | bytes 262176 | tf_op jit(solution)/shard_map/ppermute | solution.py:274
  101.0 2.4 %collective-permute-start.20 = (bf16[8,128,128]{2,1,0:T(8,128)(2,1)S(1)}, bf16[8,128,128]{2,1,0:T(8,128)(2,1)S(1)}, u32[]{:S(2)}, u32[]{:S(2)}) collective-permute-start(bf16[8,128,128]{2,1,0:T(8,128)(2,1)S(1)} %collective-permute-done.16.refs_2_), channel_id=1, source_target_pairs={{0,2},{1,3},{2,0},{3,1},{4,6},{5,7},{6,4},{7,5},{8,10},{9,11},{10,... | collective-permute-start | bytes 786440 | tf_op jit(solution)/shard_map/ppermute | solution.py:274
  104.9 2.5 %collective-permute-start.28 = (bf16[8,128,128]{2,1,0:T(8,128)(2,1)}, bf16[8,128,128]{2,1,0:T(8,128)(2,1)S(1)}, u32[]{:S(2)}, u32[]{:S(2)}) collective-permute-start(bf16[8,128,128]{2,1,0:T(8,128)(2,1)} %get-tuple-element.77.refs_0_), channel_id=1, source_target_pairs={{0,12},{1,13},{2,14},{3,15},{4,8},{5,9},{6,10},{7,11},{8,4},{9,5},... | collective-permute-start | bytes 786440 | tf_op jit(solution)/shard_map/ppermute | solution.py:274
  108.5 1.7 %collective-permute-start.31 = (bf16[8,128,128]{2,1,0:T(8,128)(2,1)S(1)}, bf16[8,128,128]{2,1,0:T(8,128)(2,1)S(1)}, u32[]{:S(2)}, u32[]{:S(2)}) collective-permute-start(bf16[8,128,128]{2,1,0:T(8,128)(2,1)S(1)} %pad_maximum_fusion.5), channel_id=1, source_target_pairs={{0,2},{1,3},{2,0},{3,1},{4,6},{5,7},{6,4},{7,5},{8,10},{9,11},{10,... | collective-permute-start | bytes 786440 | tf_op jit(solution)/shard_map/ppermute | solution.py:274
  112.3 5.4 %collective-permute-done.31 = bf16[8,128,128]{2,1,0:T(8,128)(2,1)S(1)} collective-permute-done((bf16[8,128,128]{2,1,0:T(8,128)(2,1)S(1)}, bf16[8,128,128]{2,1,0:T(8,128)(2,1)S(1)}, u32[]{:S(2)}, u32[]{:S(2)}) %collective-permute-start.31) | collective-permute-done | bytes 262176 | tf_op jit(solution)/shard_map/ppermute | solution.py:274
  117.7 4.0 %collective-permute-start.18 = (f32[144,256]{1,0:T(8,128)S(1)}, f32[144,256]{1,0:T(8,128)S(1)}, u32[]{:S(2)}, u32[]{:S(2)}) collective-permute-start(f32[144,256]{1,0:T(8,128)S(1)} %dynamic-slice_add_fusion), channel_id=1, source_target_pairs={{0,16},{16,0},{1,17},{17,1},{2,18},{18,2},{3,19},{19,3},{4,20},{20... | collective-permute-start | bytes 442376 | tf_op jit(solution)/shard_map/ppermute | solution.py:274
  121.9 3.0 %collective-permute-done.18 = f32[144,256]{1,0:T(8,128)S(1)} collective-permute-done((f32[144,256]{1,0:T(8,128)S(1)}, f32[144,256]{1,0:T(8,128)S(1)}, u32[]{:S(2)}, u32[]{:S(2)}) %collective-permute-start.18) | collective-permute-done | bytes 147488 | tf_op jit(solution)/shard_map/ppermute | solution.py:274
  125.4 6.8 %collective-permute-done.29.refs_1_ = bf16[8,128,128]{2,1,0:T(8,128)(2,1)S(1)} collective-permute-done((bf16[8,128,128]{2,1,0:T(8,128)(2,1)}, bf16[8,128,128]{2,1,0:T(8,128)(2,1)S(1)}, u32[]{:S(2)}, u32[]{:S(2)}) %collective-permute-start.29) | collective-permute-done | bytes 262176 | tf_op jit(solution)/shard_map/ppermute | solution.py:274
  133.7 4.8 %collective-permute-done.19 = f32[144,256]{1,0:T(8,128)S(1)} collective-permute-done((f32[144,256]{1,0:T(8,128)S(1)}, f32[144,256]{1,0:T(8,128)S(1)}, u32[]{:S(2)}, u32[]{:S(2)}) %collective-permute-start.19) | collective-permute-done | bytes 147488 | tf_op jit(solution)/shard_map/ppermute | solution.py:274
  143.9 7.3 %backward_blocks.2 = bf16[16,128,128]{2,1,0:T(8,128)(2,1)} custom-call(s32[1]{0:T(128)} %bitcast.13.live, s32[1]{0:T(128)} %bitcast.2.me, s32[2,256]{1,0:T(2,128)} %bitcast.26, bf16[256,128,128]{2,1,0:T(8,128)(2,1)} %bitcast.19, bf16[32,128,128]{2,1,0:T(8,128)(2,1)} %copy-done.3, bf16[32,128,128]{2,1,0:T(8,128)(2,1)} %copy-done.6, ...), custom_call_target="tpu_custom_call" | custom-call | flops 4294967296 | bytes 16777216 | tf_op jit(solution)/shard_map/backward_blocks/pallas_call | solution.py:195
  151.2 2.2 %collective-permute-done.37.refs_7_ = bf16[8,128,128]{2,1,0:T(8,128)(2,1)S(1)} collective-permute-done((bf16[8,128,128]{2,1,0:T(8,128)(2,1)S(1)}, bf16[8,128,128]{2,1,0:T(8,128)(2,1)S(1)}, u32[]{:S(2)}, u32[]{:S(2)}) %collective-permute-start.37) | collective-permute-done | bytes 262176 | tf_op jit(solution)/shard_map/ppermute | solution.py:274
  153.9 2.7 %collective-permute-start.42 = (bf16[2048,128]{1,0:T(8,128)(2,1)}, bf16[2048,128]{1,0:T(8,128)(2,1)S(1)}, u32[]{:S(2)}, u32[]{:S(2)}) collective-permute-start(bf16[2048,128]{1,0:T(8,128)(2,1)} %bitcast.22), channel_id=1, source_target_pairs={{0,16},{16,0},{1,17},{17,1},{2,18},{18,2},{3,19},{19,3},{4,20},{20... | collective-permute-start | bytes 1572872 | tf_op jit(solution)/shard_map/ppermute | solution.py:274
  158.3 8.1 %backward_blocks.3 = f32[16,128,128]{2,1,0:T(8,128)} custom-call(s32[1]{0:T(128)} %bitcast.14.live, s32[1]{0:T(128)} %bitcast.2.me, s32[2,256]{1,0:T(2,128)} %bitcast.27, bf16[256,128,128]{2,1,0:T(8,128)(2,1)} %bitcast.20, bf16[8,128,128]{2,1,0:T(8,128)(2,1)} %get-tuple-element.77.refs_0_, bf16[8,128,128]{2,1,0:T(8,128)(2,1)} %copy-done.14, ...), custom_call_target="tpu_custom_call" | custom-call | flops 4294967296 | bytes 16777216 | tf_op jit(solution)/shard_map/backward_blocks/pallas_call | solution.py:195
  (146 shorter events, 39.4 us)
Async XLA Ops:
  0.6 15.2 %collective-permute-start.1 = (bf16[2048,128]{1,0:T(8,128)(2,1)}, bf16[2048,128]{1,0:T(8,128)(2,1)S(1)}, u32[]{:S(2)}, u32[]{:S(2)}) collective-permute-start(bf16[2048,128]{1,0:T(8,128)(2,1)} %param.7), channel_id=1, source_target_pairs={{0,16},{16,0},{1,17},{17,1},{2,18},{18,2},{3,19},{19,3},{4,20},{20... | collective-permute-start | bytes 1572872 | tf_op jit(solution)/shard_map/ppermute | solution.py:274
  10.9 13.9 %collective-permute-start = (bf16[64,128,128]{2,1,0:T(8,128)(2,1)}, bf16[64,128,128]{2,1,0:T(8,128)(2,1)S(1)}, u32[]{:S(2)}, u32[]{:S(2)}) collective-permute-start(bf16[64,128,128]{2,1,0:T(8,128)(2,1)} %get-tuple-element.51), channel_id=1, source_target_pairs={{0,1},{1,0},{2,3},{3,2},{4,5},{5,4},{6,7},{7,6},{8,9},{9,8},{10,11... | collective-permute-start | bytes 6291464 | tf_op jit(solution)/shard_map/ppermute | solution.py:274
  25.5 14.9 %collective-permute-start.2 = (bf16[16,128,128]{2,1,0:T(8,128)(2,1)S(1)}, bf16[16,128,128]{2,1,0:T(8,128)(2,1)S(1)}, u32[]{:S(2)}, u32[]{:S(2)}) collective-permute-start(bf16[16,128,128]{2,1,0:T(8,128)(2,1)S(1)} %get-tuple-element.102), channel_id=1, source_target_pairs={{0,2},{1,3},{2,0},{3,1},{4,6},{5,7},{6,4},{7,5},{8,10},{9,11},{10,... | collective-permute-start | bytes 1572872 | tf_op jit(solution)/shard_map/ppermute | solution.py:274
  29.8 14.8 %collective-permute-start.6 = (bf16[16,128,128]{2,1,0:T(8,128)(2,1)S(1)}, bf16[16,128,128]{2,1,0:T(8,128)(2,1)S(1)}, u32[]{:S(2)}, u32[]{:S(2)}) collective-permute-start(bf16[16,128,128]{2,1,0:T(8,128)(2,1)S(1)} %get-tuple-element.99), channel_id=1, source_target_pairs={{0,4},{1,5},{2,6},{3,7},{4,0},{5,1},{6,2},{7,3},{8,12},{9,13},{10,... | collective-permute-start | bytes 1572872 | tf_op jit(solution)/shard_map/ppermute | solution.py:274
  30.0 21.7 %collective-permute-start.5 = (bf16[16,128,128]{2,1,0:T(8,128)(2,1)S(1)}, bf16[16,128,128]{2,1,0:T(8,128)(2,1)S(1)}, u32[]{:S(2)}, u32[]{:S(2)}) collective-permute-start(bf16[16,128,128]{2,1,0:T(8,128)(2,1)S(1)} %get-tuple-element.101), channel_id=1, source_target_pairs={{0,2},{1,3},{2,0},{3,1},{4,6},{5,7},{6,4},{7,5},{8,10},{9,11},{10,... | collective-permute-start | bytes 1572872 | tf_op jit(solution)/shard_map/ppermute | solution.py:274
  40.5 11.2 %collective-permute-start.4 = (bf16[8,128,128]{2,1,0:T(8,128)(2,1)S(1)}, bf16[8,128,128]{2,1,0:T(8,128)(2,1)S(1)}, u32[]{:S(2)}, u32[]{:S(2)}) collective-permute-start(bf16[8,128,128]{2,1,0:T(8,128)(2,1)S(1)} %get-tuple-element.110), channel_id=1, source_target_pairs={{0,4},{1,5},{2,6},{3,7},{4,0},{5,1},{6,2},{7,3},{8,12},{9,13},{10,... | collective-permute-start | bytes 786440 | tf_op jit(solution)/shard_map/ppermute | solution.py:274
  40.6 22.2 %collective-permute-start.10 = (bf16[16,128,128]{2,1,0:T(8,128)(2,1)S(1)}, bf16[16,128,128]{2,1,0:T(8,128)(2,1)S(1)}, u32[]{:S(2)}, u32[]{:S(2)}) collective-permute-start(bf16[16,128,128]{2,1,0:T(8,128)(2,1)S(1)} %get-tuple-element.97), channel_id=1, source_target_pairs={{0,2},{1,3},{2,0},{3,1},{4,6},{5,7},{6,4},{7,5},{8,10},{9,11},{10,... | collective-permute-start | bytes 1572872 | tf_op jit(solution)/shard_map/ppermute | solution.py:274
  51.8 9.4 %collective-permute-start.8 = (bf16[8,128,128]{2,1,0:T(8,128)(2,1)S(1)}, bf16[8,128,128]{2,1,0:T(8,128)(2,1)S(1)}, u32[]{:S(2)}, u32[]{:S(2)}) collective-permute-start(bf16[8,128,128]{2,1,0:T(8,128)(2,1)S(1)} %get-tuple-element.109), channel_id=1, source_target_pairs={{0,4},{1,5},{2,6},{3,7},{4,0},{5,1},{6,2},{7,3},{8,12},{9,13},{10,... | collective-permute-start | bytes 786440 | tf_op jit(solution)/shard_map/ppermute | solution.py:274
  52.6 8.6 %collective-permute-start.7 = (bf16[4,128,128]{2,1,0:T(8,128)(2,1)S(1)}, bf16[4,128,128]{2,1,0:T(8,128)(2,1)S(1)}, u32[]{:S(2)}, u32[]{:S(2)}) collective-permute-start(bf16[4,128,128]{2,1,0:T(8,128)(2,1)S(1)} %get-tuple-element.118), channel_id=1, source_target_pairs={{0,8},{1,9},{2,10},{3,11},{4,12},{5,13},{6,14},{7,15},{8,0},{9,1},... | collective-permute-start | bytes 393224 | tf_op jit(solution)/shard_map/ppermute | solution.py:274
  56.8 11.1 %collective-permute-start.12 = (bf16[8,128,128]{2,1,0:T(8,128)(2,1)S(1)}, bf16[8,128,128]{2,1,0:T(8,128)(2,1)S(1)}, u32[]{:S(2)}, u32[]{:S(2)}) collective-permute-start(bf16[8,128,128]{2,1,0:T(8,128)(2,1)S(1)} %get-tuple-element.105), channel_id=1, source_target_pairs={{0,2},{1,3},{2,0},{3,1},{4,6},{5,7},{6,4},{7,5},{8,10},{9,11},{10,... | collective-permute-start | bytes 786440 | tf_op jit(solution)/shard_map/ppermute | solution.py:274
  63.0 9.7 %collective-permute-start.11 = (bf16[8,128,128]{2,1,0:T(8,128)(2,1)S(1)}, bf16[8,128,128]{2,1,0:T(8,128)(2,1)S(1)}, u32[]{:S(2)}, u32[]{:S(2)}) collective-permute-start(bf16[8,128,128]{2,1,0:T(8,128)(2,1)S(1)} %get-tuple-element.107), channel_id=1, source_target_pairs={{0,4},{1,5},{2,6},{3,7},{4,0},{5,1},{6,2},{7,3},{8,12},{9,13},{10,... | collective-permute-start | bytes 786440 | tf_op jit(solution)/shard_map/ppermute | solution.py:274
  64.4 10.4 %collective-permute-start.9 = (bf16[4,128,128]{2,1,0:T(8,128)(2,1)S(1)}, bf16[4,128,128]{2,1,0:T(8,128)(2,1)S(1)}, u32[]{:S(2)}, u32[]{:S(2)}) collective-permute-start(bf16[4,128,128]{2,1,0:T(8,128)(2,1)S(1)} %get-tuple-element.116), channel_id=1, source_target_pairs={{0,8},{1,9},{2,10},{3,11},{4,12},{5,13},{6,14},{7,15},{8,0},{9,1},... | collective-permute-start | bytes 393224 | tf_op jit(solution)/shard_map/ppermute | solution.py:274
  68.6 13.7 %collective-permute-start.14 = (bf16[4,128,128]{2,1,0:T(8,128)(2,1)S(1)}, bf16[4,128,128]{2,1,0:T(8,128)(2,1)S(1)}, u32[]{:S(2)}, u32[]{:S(2)}) collective-permute-start(bf16[4,128,128]{2,1,0:T(8,128)(2,1)S(1)} %get-tuple-element.113), channel_id=1, source_target_pairs={{0,8},{1,9},{2,10},{3,11},{4,12},{5,13},{6,14},{7,15},{8,0},{9,1},... | collective-permute-start | bytes 393224 | tf_op jit(solution)/shard_map/ppermute | solution.py:274
  73.5 11.1 %collective-permute-start.13 = (bf16[4,128,128]{2,1,0:T(8,128)(2,1)S(1)}, bf16[4,128,128]{2,1,0:T(8,128)(2,1)S(1)}, u32[]{:S(2)}, u32[]{:S(2)}) collective-permute-start(bf16[4,128,128]{2,1,0:T(8,128)(2,1)S(1)} %get-tuple-element.114), channel_id=1, source_target_pairs={{0,8},{1,9},{2,10},{3,11},{4,12},{5,13},{6,14},{7,15},{8,0},{9,1},... | collective-permute-start | bytes 393224 | tf_op jit(solution)/shard_map/ppermute | solution.py:274
  88.9 12.2 %collective-permute-start.16 = (bf16[8,128,128]{2,1,0:T(8,128)(2,1)}, bf16[8,128,128]{2,1,0:T(8,128)(2,1)S(1)}, u32[]{:S(2)}, u32[]{:S(2)}) collective-permute-start(bf16[8,128,128]{2,1,0:T(8,128)(2,1)} %get-tuple-element.77.refs_0_), channel_id=1, source_target_pairs={{0,4},{1,5},{2,6},{3,7},{4,0},{5,1},{6,2},{7,3},{8,12},{9,13},{10,... | collective-permute-start | bytes 786440 | tf_op jit(solution)/shard_map/ppermute | solution.py:274
  88.9 8.0 %collective-permute-start.17 = (bf16[8,128,128]{2,1,0:T(8,128)(2,1)}, bf16[8,128,128]{2,1,0:T(8,128)(2,1)S(1)}, u32[]{:S(2)}, u32[]{:S(2)}) collective-permute-start(bf16[8,128,128]{2,1,0:T(8,128)(2,1)} %get-tuple-element.77.refs_0_), channel_id=1, source_target_pairs={{0,2},{1,3},{2,0},{3,1},{4,6},{5,7},{6,4},{7,5},{8,10},{9,11},{10,... | collective-permute-start | bytes 786440 | tf_op jit(solution)/shard_map/ppermute | solution.py:274
  90.4 14.3 %collective-permute-start.25 = (bf16[8,128,128]{2,1,0:T(8,128)(2,1)}, bf16[8,128,128]{2,1,0:T(8,128)(2,1)S(1)}, u32[]{:S(2)}, u32[]{:S(2)}) collective-permute-start(bf16[8,128,128]{2,1,0:T(8,128)(2,1)} %get-tuple-element.71), channel_id=1, source_target_pairs={{0,8},{1,9},{2,10},{3,11},{4,12},{5,13},{6,14},{7,15},{8,0},{9,1},... | collective-permute-start | bytes 786440 | tf_op jit(solution)/shard_map/ppermute | solution.py:274
  93.8 9.6 %collective-permute-start.15 = (f32[144,256]{1,0:T(8,128)S(1)}, f32[144,256]{1,0:T(8,128)S(1)}, u32[]{:S(2)}, u32[]{:S(2)}) collective-permute-start(f32[144,256]{1,0:T(8,128)S(1)} %constant_dynamic-slice_fusion), channel_id=1, source_target_pairs={{0,1},{1,0},{2,3},{3,2},{4,5},{5,4},{6,7},{7,6},{8,9},{9,8},{10,11... | collective-permute-start | bytes 442376 | tf_op jit(solution)/shard_map/ppermute | solution.py:274
  104.8 17.0 %collective-permute-start.24 = (bf16[8,128,128]{2,1,0:T(8,128)(2,1)}, bf16[8,128,128]{2,1,0:T(8,128)(2,1)S(1)}, u32[]{:S(2)}, u32[]{:S(2)}) collective-permute-start(bf16[8,128,128]{2,1,0:T(8,128)(2,1)} %get-tuple-element.77.refs_0_), channel_id=1, source_target_pairs={{0,1},{1,0},{2,3},{3,2},{4,5},{5,4},{6,7},{7,6},{8,9},{9,8},{10,11... | collective-permute-start | bytes 786440 | tf_op jit(solution)/shard_map/ppermute | solution.py:274
  104.9 19.9 %collective-permute-start.28 = (bf16[8,128,128]{2,1,0:T(8,128)(2,1)}, bf16[8,128,128]{2,1,0:T(8,128)(2,1)S(1)}, u32[]{:S(2)}, u32[]{:S(2)}) collective-permute-start(bf16[8,128,128]{2,1,0:T(8,128)(2,1)} %get-tuple-element.77.refs_0_), channel_id=1, source_target_pairs={{0,12},{1,13},{2,14},{3,15},{4,8},{5,9},{6,10},{7,11},{8,4},{9,5},... | collective-permute-start | bytes 786440 | tf_op jit(solution)/shard_map/ppermute | solution.py:274
  107.4 24.8 %collective-permute-start.29 = (bf16[8,128,128]{2,1,0:T(8,128)(2,1)}, bf16[8,128,128]{2,1,0:T(8,128)(2,1)S(1)}, u32[]{:S(2)}, u32[]{:S(2)}) collective-permute-start(bf16[8,128,128]{2,1,0:T(8,128)(2,1)} %get-tuple-element.77.refs_0_), channel_id=1, source_target_pairs={{0,8},{1,9},{2,10},{3,11},{4,12},{5,13},{6,14},{7,15},{8,0},{9,1},... | collective-permute-start | bytes 786440 | tf_op jit(solution)/shard_map/ppermute | solution.py:274
  108.5 9.2 %collective-permute-start.31 = (bf16[8,128,128]{2,1,0:T(8,128)(2,1)S(1)}, bf16[8,128,128]{2,1,0:T(8,128)(2,1)S(1)}, u32[]{:S(2)}, u32[]{:S(2)}) collective-permute-start(bf16[8,128,128]{2,1,0:T(8,128)(2,1)S(1)} %pad_maximum_fusion.5), channel_id=1, source_target_pairs={{0,2},{1,3},{2,0},{3,1},{4,6},{5,7},{6,4},{7,5},{8,10},{9,11},{10,... | collective-permute-start | bytes 786440 | tf_op jit(solution)/shard_map/ppermute | solution.py:274
  111.7 20.5 %collective-permute-start.27 = (bf16[16,128,128]{2,1,0:T(8,128)(2,1)S(1)}, bf16[16,128,128]{2,1,0:T(8,128)(2,1)S(1)}, u32[]{:S(2)}, u32[]{:S(2)}) collective-permute-start(bf16[16,128,128]{2,1,0:T(8,128)(2,1)S(1)} %pad_maximum_fusion.2), channel_id=1, source_target_pairs={{0,2},{1,3},{2,0},{3,1},{4,6},{5,7},{6,4},{7,5},{8,10},{9,11},{10,... | collective-permute-start | bytes 1572872 | tf_op jit(solution)/shard_map/ppermute | solution.py:274
  121.8 16.9 %collective-permute-start.32 = (bf16[16,128,128]{2,1,0:T(8,128)(2,1)S(1)}, bf16[16,128,128]{2,1,0:T(8,128)(2,1)S(1)}, u32[]{:S(2)}, u32[]{:S(2)}) collective-permute-start(bf16[16,128,128]{2,1,0:T(8,128)(2,1)S(1)} %pad_maximum_fusion.3), channel_id=1, source_target_pairs={{0,4},{1,5},{2,6},{3,7},{4,0},{5,1},{6,2},{7,3},{8,12},{9,13},{10,... | collective-permute-start | bytes 1572872 | tf_op jit(solution)/shard_map/ppermute | solution.py:274
  124.9 8.0 %collective-permute-start.23 = (bf16[8,128,128]{2,1,0:T(8,128)(2,1)S(1)}, bf16[8,128,128]{2,1,0:T(8,128)(2,1)S(1)}, u32[]{:S(2)}, u32[]{:S(2)}) collective-permute-start(bf16[8,128,128]{2,1,0:T(8,128)(2,1)S(1)} %collective-permute-done.17.refs_4_), channel_id=1, source_target_pairs={{0,1},{1,0},{2,3},{3,2},{4,5},{5,4},{6,7},{7,6},{8,9},{9,8},{10,11... | collective-permute-start | bytes 786440 | tf_op jit(solution)/shard_map/ppermute | solution.py:274
  139.5 11.7 %collective-permute-start.36 = (bf16[8,128,128]{2,1,0:T(8,128)(2,1)S(1)}, bf16[8,128,128]{2,1,0:T(8,128)(2,1)S(1)}, u32[]{:S(2)}, u32[]{:S(2)}) collective-permute-start(bf16[8,128,128]{2,1,0:T(8,128)(2,1)S(1)} %collective-permute-done.29.refs_1_), channel_id=1, source_target_pairs={{0,2},{1,3},{2,0},{3,1},{4,6},{5,7},{6,4},{7,5},{8,10},{9,11},{10,... | collective-permute-start | bytes 786440 | tf_op jit(solution)/shard_map/ppermute | solution.py:274
  140.0 13.4 %collective-permute-start.37 = (bf16[8,128,128]{2,1,0:T(8,128)(2,1)S(1)}, bf16[8,128,128]{2,1,0:T(8,128)(2,1)S(1)}, u32[]{:S(2)}, u32[]{:S(2)}) collective-permute-start(bf16[8,128,128]{2,1,0:T(8,128)(2,1)S(1)} %collective-permute-done.28.refs_3_), channel_id=1, source_target_pairs={{0,2},{1,3},{2,0},{3,1},{4,6},{5,7},{6,4},{7,5},{8,10},{9,11},{10,... | collective-permute-start | bytes 786440 | tf_op jit(solution)/shard_map/ppermute | solution.py:274
  141.5 15.1 %collective-permute-start.38 = (bf16[8,128,128]{2,1,0:T(8,128)(2,1)S(1)}, bf16[8,128,128]{2,1,0:T(8,128)(2,1)S(1)}, u32[]{:S(2)}, u32[]{:S(2)}) collective-permute-start(bf16[8,128,128]{2,1,0:T(8,128)(2,1)S(1)} %collective-permute-done.29.refs_1_), channel_id=1, source_target_pairs={{0,1},{1,0},{2,3},{3,2},{4,5},{5,4},{6,7},{7,6},{8,9},{9,8},{10,11... | collective-permute-start | bytes 786440 | tf_op jit(solution)/shard_map/ppermute | solution.py:274
  141.6 15.9 %collective-permute-start.39 = (bf16[8,128,128]{2,1,0:T(8,128)(2,1)S(1)}, bf16[8,128,128]{2,1,0:T(8,128)(2,1)S(1)}, u32[]{:S(2)}, u32[]{:S(2)}) collective-permute-start(bf16[8,128,128]{2,1,0:T(8,128)(2,1)S(1)} %collective-permute-done.28.refs_3_), channel_id=1, source_target_pairs={{0,1},{1,0},{2,3},{3,2},{4,5},{5,4},{6,7},{7,6},{8,9},{9,8},{10,11... | collective-permute-start | bytes 786440 | tf_op jit(solution)/shard_map/ppermute | solution.py:274
  142.9 8.3 %collective-permute-start.30 = (f32[144,256]{1,0:T(8,128)S(1)}, f32[144,256]{1,0:T(8,128)S(1)}, u32[]{:S(2)}, u32[]{:S(2)}) collective-permute-start(f32[144,256]{1,0:T(8,128)S(1)} %add.129), channel_id=1, source_target_pairs={{0,4},{1,5},{2,6},{3,7},{4,0},{5,1},{6,2},{7,3},{8,12},{9,13},{10,... | collective-permute-start | bytes 442376 | tf_op jit(solution)/shard_map/ppermute | solution.py:274
  153.9 16.4 %collective-permute-start.42 = (bf16[2048,128]{1,0:T(8,128)(2,1)}, bf16[2048,128]{1,0:T(8,128)(2,1)S(1)}, u32[]{:S(2)}, u32[]{:S(2)}) collective-permute-start(bf16[2048,128]{1,0:T(8,128)(2,1)} %bitcast.22), channel_id=1, source_target_pairs={{0,16},{16,0},{1,17},{17,1},{2,18},{18,2},{3,19},{19,3},{4,20},{20... | collective-permute-start | bytes 1572872 | tf_op jit(solution)/shard_map/ppermute | solution.py:274
  156.7 9.8 %collective-permute-start.35 = (f32[144,256]{1,0:T(8,128)S(1)}, f32[144,256]{1,0:T(8,128)S(1)}, u32[]{:S(2)}, u32[]{:S(2)}) collective-permute-start(f32[144,256]{1,0:T(8,128)S(1)} %add.130), channel_id=1, source_target_pairs={{0,8},{1,9},{2,10},{3,11},{4,12},{5,13},{6,14},{7,15},{8,0},{9,1},... | collective-permute-start | bytes 442376 | tf_op jit(solution)/shard_map/ppermute | solution.py:274
  (40 other events, 317.6 us)

commit v5 on v4

--- a/solution.py
+++ b/solution.py
@@ -434,11 +434,11 @@
         core[mask] = [swap(piece[mask], "col", 1) for piece in (pieces, crossed)]
     pieces_a = [pieces[mask] for mask in masks] + [crossed[mask] for mask in masks]
     pieces_a = pieces_a + [core[mask][0] for mask in masks] + [core[mask][1] for mask in masks]
-    part_a = input_grad(pieces_a, (order_0,), F32)
+    part_a = input_grad(pieces_a, (order_0,), BF16 if row_count == 2 else F32)
     totals.got, part_a = lax.optimization_barrier((totals.got, part_a))
     if row_count == 2:
         theirs = swap(part_b, "row", 1)
-        grad_x = (part_a + theirs.astype(F32)).astype(BF16)
+        grad_x = add(part_a, theirs)
     else:
         partial_x = jnp.concatenate([part_a, part_b], axis=1)
         grad_x = lax.psum_scatter(partial_x, "row", scatter_dimension=1, tiled=True).astype(BF16)

time: 171 us -> 170 us (level)
  waiting for transfers between devices: 74.8 us -> 77 us
  starting transfers between devices: 48.9 us -> 46.7 us
    ppermute x44, waiting for transfers between devices: 74.8 us -> 77 us  [swap(): lax.ppermute(array, axis, [(at, at ^ bit) for at in range(lax.axis_size(a...]
    ppermute x44, starting transfers between devices: 48.9 us -> 46.7 us  [swap(): lax.ppermute(array, axis, [(at, at ^ bit) for at in range(lax.axis_size(a...]
    convert_element_type x10 -> x11, other arithmetic: 5.32 us -> 6.25 us  [add(): return (x.astype(F32) + y.astype(F32)).astype(BF16)]
  transfers between devices with their start and end apart: 44 -> 44, of which waited for: 23 -> 27; matrix products, arithmetic and copies ran while one was open for 5% -> 5% of each run, Pallas kernels for 17% -> 17%
where the time goes in v5:
time: 170 us; the launch traced here: 171 us
  waiting for transfers between devices  77 us (45%)
  starting transfers between devices  46.7 us (27%)
  Pallas kernels  31.9 us (19%)
  other arithmetic  6.76 us (4%)
  local copies, waits for them, and re-layouts  6.36 us (4%)
  between operations  1.81 us (1%)
    ppermute x44, waiting for transfers between devices, swap(): lax.ppermute(array, axis, [(at, at ^ bit) for at in range(lax.axis_size(a...  77 us
    ppermute x44, starting transfers between devices, swap(): lax.ppermute(array, axis, [(at, at ^ bit) for at in range(lax.axis_size(a...  46.7 us
    pallas_call x2, Pallas kernels, backward_blocks(): pl.pallas_call(functools.partial(backward_kernel, plan, per_device, lengt...  14.7 us
    pallas_call x2, Pallas kernels, forward_blocks(): pl.pallas_call(functools.partial(forward_kernel, plan, per_device), in_sp...  13.5 us
    convert_element_type x11, other arithmetic, add(): return (x.astype(F32) + y.astype(F32)).astype(BF16)  6.25 us
    pallas_call x1, Pallas kernels, dense(): pl.pallas_call(dense_kernel, in_specs=[pl.BlockSpec(memory_space=pltpu.SM...  3.67 us
  transfers between devices with their start and end apart: 44, of which 27 were waited for; matrix products, arithmetic and copies ran while one was open for 5% of the time, Pallas kernels for 17%

profile of v5, /device:TPU:0, one launch (start us, length us, event | category | flops | bytes accessed | tf_op | source)
XLA Modules:
  0.0 170.5 jit_solution(12018919012720731236)
XLA Ops:
  0.6 3.0 %collective-permute-start.1 = (bf16[2048,128]{1,0:T(8,128)(2,1)}, bf16[2048,128]{1,0:T(8,128)(2,1)S(1)}, u32[]{:S(2)}, u32[]{:S(2)}) collective-permute-start(bf16[2048,128]{1,0:T(8,128)(2,1)} %param.7), channel_id=1, source_target_pairs={{0,16},{16,0},{1,17},{17,1},{2,18},{18,2},{3,19},{19,3},{4,20},{20... | collective-permute-start | bytes 1572872 | tf_op jit(solution)/shard_map/ppermute | solution.py:274
  4.3 6.6 %forward_blocks.2 = (bf16[64,128,128]{2,1,0:T(8,128)(2,1)}, bf16[64,128,128]{2,1,0:T(8,128)(2,1)}) custom-call(s32[1]{0:T(128)} %bitcast.11.live, s32[1]{0:T(128)} %bitcast.2.me, s32[2,256]{1,0:T(2,128)} %bitcast.24, bf16[256,128,128]{2,1,0:T(8,128)(2,1)} %bitcast.17, bf16[16,128,128]{2,1,0:T(8,128)(2,1)} %bitcast.21), custom_call_target="tpu_custom_call" | custom-call | flops 4294967296 | bytes 16777216 | tf_op jit(solution)/shard_map/forward_blocks/pallas_call | solution.py:134
  11.0 4.8 %collective-permute-done.1 = bf16[2048,128]{1,0:T(8,128)(2,1)S(1)} collective-permute-done((bf16[2048,128]{1,0:T(8,128)(2,1)}, bf16[2048,128]{1,0:T(8,128)(2,1)S(1)}, u32[]{:S(2)}, u32[]{:S(2)}) %collective-permute-start.1) | collective-permute-done | bytes 524320 | tf_op jit(solution)/shard_map/ppermute | solution.py:274
  16.6 6.9 %forward_blocks.3 = (bf16[64,128,128]{2,1,0:T(8,128)(2,1)}, bf16[64,128,128]{2,1,0:T(8,128)(2,1)}) custom-call(s32[1]{0:T(128)} %bitcast.12.live, s32[1]{0:T(128)} %bitcast.2.me, s32[2,256]{1,0:T(2,128)} %bitcast.25, bf16[256,128,128]{2,1,0:T(8,128)(2,1)} %bitcast.18, bf16[16,128,128]{2,1,0:T(8,128)(2,1)} %bitcast.23), custom_call_target="tpu_custom_call" | custom-call | flops 4294967296 | bytes 16777216 | tf_op jit(solution)/shard_map/forward_blocks/pallas_call | solution.py:134
  24.4 1.8 %collective-permute-start.2 = (bf16[16,128,128]{2,1,0:T(8,128)(2,1)S(1)}, bf16[16,128,128]{2,1,0:T(8,128)(2,1)S(1)}, u32[]{:S(2)}, u32[]{:S(2)}) collective-permute-start(bf16[16,128,128]{2,1,0:T(8,128)(2,1)S(1)} %get-tuple-element.102), channel_id=1, source_target_pairs={{0,2},{1,3},{2,0},{3,1},{4,6},{5,7},{6,4},{7,5},{8,10},{9,11},{10,... | collective-permute-start | bytes 1572872 | tf_op jit(solution)/shard_map/ppermute | solution.py:274
  26.2 1.8 %collective-permute-done.3 = bf16[64,128,128]{2,1,0:T(8,128)(2,1)S(1)} collective-permute-done((bf16[64,128,128]{2,1,0:T(8,128)(2,1)}, bf16[64,128,128]{2,1,0:T(8,128)(2,1)S(1)}, u32[]{:S(2)}, u32[]{:S(2)}) %collective-permute-start.3) | collective-permute-done | bytes 2097184 | tf_op jit(solution)/shard_map/ppermute | solution.py:274
  29.0 1.9 %collective-permute-start.6 = (bf16[16,128,128]{2,1,0:T(8,128)(2,1)S(1)}, bf16[16,128,128]{2,1,0:T(8,128)(2,1)S(1)}, u32[]{:S(2)}, u32[]{:S(2)}) collective-permute-start(bf16[16,128,128]{2,1,0:T(8,128)(2,1)S(1)} %get-tuple-element.99), channel_id=1, source_target_pairs={{0,4},{1,5},{2,6},{3,7},{4,0},{5,1},{6,2},{7,3},{8,12},{9,13},{10,... | collective-permute-start | bytes 1572872 | tf_op jit(solution)/shard_map/ppermute | solution.py:274
  31.9 7.3 %collective-permute-done.2 = bf16[16,128,128]{2,1,0:T(8,128)(2,1)S(1)} collective-permute-done((bf16[16,128,128]{2,1,0:T(8,128)(2,1)S(1)}, bf16[16,128,128]{2,1,0:T(8,128)(2,1)S(1)}, u32[]{:S(2)}, u32[]{:S(2)}) %collective-permute-start.2) | collective-permute-done | bytes 524320 | tf_op jit(solution)/shard_map/ppermute | solution.py:274
  39.3 1.9 %collective-permute-start.4 = (bf16[8,128,128]{2,1,0:T(8,128)(2,1)S(1)}, bf16[8,128,128]{2,1,0:T(8,128)(2,1)S(1)}, u32[]{:S(2)}, u32[]{:S(2)}) collective-permute-start(bf16[8,128,128]{2,1,0:T(8,128)(2,1)S(1)} %get-tuple-element.110), channel_id=1, source_target_pairs={{0,4},{1,5},{2,6},{3,7},{4,0},{5,1},{6,2},{7,3},{8,12},{9,13},{10,... | collective-permute-start | bytes 786440 | tf_op jit(solution)/shard_map/ppermute | solution.py:274
  43.9 6.6 %collective-permute-done.5 = bf16[16,128,128]{2,1,0:T(8,128)(2,1)S(1)} collective-permute-done((bf16[16,128,128]{2,1,0:T(8,128)(2,1)S(1)}, bf16[16,128,128]{2,1,0:T(8,128)(2,1)S(1)}, u32[]{:S(2)}, u32[]{:S(2)}) %collective-permute-start.5) | collective-permute-done | bytes 524320 | tf_op jit(solution)/shard_map/ppermute | solution.py:274
  50.6 1.9 %collective-permute-start.8 = (bf16[8,128,128]{2,1,0:T(8,128)(2,1)S(1)}, bf16[8,128,128]{2,1,0:T(8,128)(2,1)S(1)}, u32[]{:S(2)}, u32[]{:S(2)}) collective-permute-start(bf16[8,128,128]{2,1,0:T(8,128)(2,1)S(1)} %get-tuple-element.109), channel_id=1, source_target_pairs={{0,4},{1,5},{2,6},{3,7},{4,0},{5,1},{6,2},{7,3},{8,12},{9,13},{10,... | collective-permute-start | bytes 786440 | tf_op jit(solution)/shard_map/ppermute | solution.py:274
  53.2 4.5 %collective-permute-start.7 = (bf16[4,128,128]{2,1,0:T(8,128)(2,1)S(1)}, bf16[4,128,128]{2,1,0:T(8,128)(2,1)S(1)}, u32[]{:S(2)}, u32[]{:S(2)}) collective-permute-start(bf16[4,128,128]{2,1,0:T(8,128)(2,1)S(1)} %get-tuple-element.118), channel_id=1, source_target_pairs={{0,8},{1,9},{2,10},{3,11},{4,12},{5,13},{6,14},{7,15},{8,0},{9,1},... | collective-permute-start | bytes 393224 | tf_op jit(solution)/shard_map/ppermute | solution.py:274
  61.8 3.9 %collective-permute-start.11 = (bf16[8,128,128]{2,1,0:T(8,128)(2,1)S(1)}, bf16[8,128,128]{2,1,0:T(8,128)(2,1)S(1)}, u32[]{:S(2)}, u32[]{:S(2)}) collective-permute-start(bf16[8,128,128]{2,1,0:T(8,128)(2,1)S(1)} %get-tuple-element.107), channel_id=1, source_target_pairs={{0,4},{1,5},{2,6},{3,7},{4,0},{5,1},{6,2},{7,3},{8,12},{9,13},{10,... | collective-permute-start | bytes 786440 | tf_op jit(solution)/shard_map/ppermute | solution.py:274
  66.4 2.5 %collective-permute-start.9 = (bf16[4,128,128]{2,1,0:T(8,128)(2,1)S(1)}, bf16[4,128,128]{2,1,0:T(8,128)(2,1)S(1)}, u32[]{:S(2)}, u32[]{:S(2)}) collective-permute-start(bf16[4,128,128]{2,1,0:T(8,128)(2,1)S(1)} %get-tuple-element.116), channel_id=1, source_target_pairs={{0,8},{1,9},{2,10},{3,11},{4,12},{5,13},{6,14},{7,15},{8,0},{9,1},... | collective-permute-start | bytes 393224 | tf_op jit(solution)/shard_map/ppermute | solution.py:274
  70.4 3.4 %collective-permute-done.11 = bf16[8,128,128]{2,1,0:T(8,128)(2,1)S(1)} collective-permute-done((bf16[8,128,128]{2,1,0:T(8,128)(2,1)S(1)}, bf16[8,128,128]{2,1,0:T(8,128)(2,1)S(1)}, u32[]{:S(2)}, u32[]{:S(2)}) %collective-permute-start.11) | collective-permute-done | bytes 262176 | tf_op jit(solution)/shard_map/ppermute | solution.py:274
  74.6 2.2 %collective-permute-start.13 = (bf16[4,128,128]{2,1,0:T(8,128)(2,1)S(1)}, bf16[4,128,128]{2,1,0:T(8,128)(2,1)S(1)}, u32[]{:S(2)}, u32[]{:S(2)}) collective-permute-start(bf16[4,128,128]{2,1,0:T(8,128)(2,1)S(1)} %get-tuple-element.114), channel_id=1, source_target_pairs={{0,8},{1,9},{2,10},{3,11},{4,12},{5,13},{6,14},{7,15},{8,0},{9,1},... | collective-permute-start | bytes 393224 | tf_op jit(solution)/shard_map/ppermute | solution.py:274
  76.8 7.4 %collective-permute-done.14.refs_7_ = bf16[4,128,128]{2,1,0:T(8,128)(2,1)S(1)} collective-permute-done((bf16[4,128,128]{2,1,0:T(8,128)(2,1)S(1)}, bf16[4,128,128]{2,1,0:T(8,128)(2,1)S(1)}, u32[]{:S(2)}, u32[]{:S(2)}) %collective-permute-start.14) | collective-permute-done | bytes 131104 | tf_op jit(solution)/shard_map/ppermute | solution.py:274
  84.3 2.1 %collective-permute-done.13.refs_5_ = bf16[4,128,128]{2,1,0:T(8,128)(2,1)S(1)} collective-permute-done((bf16[4,128,128]{2,1,0:T(8,128)(2,1)S(1)}, bf16[4,128,128]{2,1,0:T(8,128)(2,1)S(1)}, u32[]{:S(2)}, u32[]{:S(2)}) %collective-permute-start.13) | collective-permute-done | bytes 131104 | tf_op jit(solution)/shard_map/ppermute | solution.py:274
  87.0 3.7 %dense_layer.1 = (bf16[1024,256]{1,0:T(8,128)(2,1)}, bf16[8,128,128]{2,1,0:T(8,128)(2,1)}, bf16[8,128,128]{2,1,0:T(8,128)(2,1)}, f32[288,256]{1,0:T(8,128)}) custom-call(s32[1]{0:T(128)} %bitcast.first, bf16[4,128,128]{2,1,0:T(8,128)(2,1)} %get-tuple-element.119.refs_0_, bf16[4,128,128]{2,1,0:T(8,128)(2,1)} %copy-done.24, ...), custom_call_target="tpu_custom_call" | custom-call | flops 536870912 | bytes 2097152 | tf_op jit(solution)/shard_map/dense_layer/pallas_call | solution.py:255
  92.2 2.2 %collective-permute-start.25 = (bf16[8,128,128]{2,1,0:T(8,128)(2,1)}, bf16[8,128,128]{2,1,0:T(8,128)(2,1)S(1)}, u32[]{:S(2)}, u32[]{:S(2)}) collective-permute-start(bf16[8,128,128]{2,1,0:T(8,128)(2,1)} %get-tuple-element.71), channel_id=1, source_target_pairs={{0,8},{1,9},{2,10},{3,11},{4,12},{5,13},{6,14},{7,15},{8,0},{9,1},... | collective-permute-start | bytes 786440 | tf_op jit(solution)/shard_map/ppermute | solution.py:274
  96.4 2.1 %collective-permute-done.17.refs_4_ = bf16[8,128,128]{2,1,0:T(8,128)(2,1)S(1)} collective-permute-done((bf16[8,128,128]{2,1,0:T(8,128)(2,1)}, bf16[8,128,128]{2,1,0:T(8,128)(2,1)S(1)}, u32[]{:S(2)}, u32[]{:S(2)}) %collective-permute-start.17) | collective-permute-done | bytes 262176 | tf_op jit(solution)/shard_map/ppermute | solution.py:274
  98.6 4.0 %collective-permute-done.16.refs_2_ = bf16[8,128,128]{2,1,0:T(8,128)(2,1)S(1)} collective-permute-done((bf16[8,128,128]{2,1,0:T(8,128)(2,1)}, bf16[8,128,128]{2,1,0:T(8,128)(2,1)S(1)}, u32[]{:S(2)}, u32[]{:S(2)}) %collective-permute-start.16) | collective-permute-done | bytes 262176 | tf_op jit(solution)/shard_map/ppermute | solution.py:274
  102.6 2.4 %collective-permute-start.20 = (bf16[8,128,128]{2,1,0:T(8,128)(2,1)S(1)}, bf16[8,128,128]{2,1,0:T(8,128)(2,1)S(1)}, u32[]{:S(2)}, u32[]{:S(2)}) collective-permute-start(bf16[8,128,128]{2,1,0:T(8,128)(2,1)S(1)} %collective-permute-done.16.refs_2_), channel_id=1, source_target_pairs={{0,2},{1,3},{2,0},{3,1},{4,6},{5,7},{6,4},{7,5},{8,10},{9,11},{10,... | collective-permute-start | bytes 786440 | tf_op jit(solution)/shard_map/ppermute | solution.py:274
  106.6 2.4 %collective-permute-start.28 = (bf16[8,128,128]{2,1,0:T(8,128)(2,1)}, bf16[8,128,128]{2,1,0:T(8,128)(2,1)S(1)}, u32[]{:S(2)}, u32[]{:S(2)}) collective-permute-start(bf16[8,128,128]{2,1,0:T(8,128)(2,1)} %get-tuple-element.77.refs_0_), channel_id=1, source_target_pairs={{0,12},{1,13},{2,14},{3,15},{4,8},{5,9},{6,10},{7,11},{8,4},{9,5},... | collective-permute-start | bytes 786440 | tf_op jit(solution)/shard_map/ppermute | solution.py:274
  110.2 1.7 %collective-permute-start.31 = (bf16[8,128,128]{2,1,0:T(8,128)(2,1)S(1)}, bf16[8,128,128]{2,1,0:T(8,128)(2,1)S(1)}, u32[]{:S(2)}, u32[]{:S(2)}) collective-permute-start(bf16[8,128,128]{2,1,0:T(8,128)(2,1)S(1)} %pad_maximum_fusion.5), channel_id=1, source_target_pairs={{0,2},{1,3},{2,0},{3,1},{4,6},{5,7},{6,4},{7,5},{8,10},{9,11},{10,... | collective-permute-start | bytes 786440 | tf_op jit(solution)/shard_map/ppermute | solution.py:274
  114.0 5.4 %collective-permute-done.31 = bf16[8,128,128]{2,1,0:T(8,128)(2,1)S(1)} collective-permute-done((bf16[8,128,128]{2,1,0:T(8,128)(2,1)S(1)}, bf16[8,128,128]{2,1,0:T(8,128)(2,1)S(1)}, u32[]{:S(2)}, u32[]{:S(2)}) %collective-permute-start.31) | collective-permute-done | bytes 262176 | tf_op jit(solution)/shard_map/ppermute | solution.py:274
  120.7 3.8 %collective-permute-done.18 = f32[144,256]{1,0:T(8,128)S(1)} collective-permute-done((f32[144,256]{1,0:T(8,128)S(1)}, f32[144,256]{1,0:T(8,128)S(1)}, u32[]{:S(2)}, u32[]{:S(2)}) %collective-permute-start.18) | collective-permute-done | bytes 147488 | tf_op jit(solution)/shard_map/ppermute | solution.py:274
  125.1 8.7 %collective-permute-done.29.refs_1_ = bf16[8,128,128]{2,1,0:T(8,128)(2,1)S(1)} collective-permute-done((bf16[8,128,128]{2,1,0:T(8,128)(2,1)}, bf16[8,128,128]{2,1,0:T(8,128)(2,1)S(1)}, u32[]{:S(2)}, u32[]{:S(2)}) %collective-permute-start.29) | collective-permute-done | bytes 262176 | tf_op jit(solution)/shard_map/ppermute | solution.py:274
  135.4 4.8 %collective-permute-done.19 = f32[144,256]{1,0:T(8,128)S(1)} collective-permute-done((f32[144,256]{1,0:T(8,128)S(1)}, f32[144,256]{1,0:T(8,128)S(1)}, u32[]{:S(2)}, u32[]{:S(2)}) %collective-permute-start.19) | collective-permute-done | bytes 147488 | tf_op jit(solution)/shard_map/ppermute | solution.py:274
  145.5 7.3 %backward_blocks.2 = bf16[16,128,128]{2,1,0:T(8,128)(2,1)} custom-call(s32[1]{0:T(128)} %bitcast.13.live, s32[1]{0:T(128)} %bitcast.2.me, s32[2,256]{1,0:T(2,128)} %bitcast.26, bf16[256,128,128]{2,1,0:T(8,128)(2,1)} %bitcast.19, bf16[32,128,128]{2,1,0:T(8,128)(2,1)} %copy-done.2, bf16[32,128,128]{2,1,0:T(8,128)(2,1)} %copy-done.6, ...), custom_call_target="tpu_custom_call" | custom-call | flops 4294967296 | bytes 16777216 | tf_op jit(solution)/shard_map/backward_blocks/pallas_call | solution.py:195
  152.8 2.2 %collective-permute-done.37.refs_7_ = bf16[8,128,128]{2,1,0:T(8,128)(2,1)S(1)} collective-permute-done((bf16[8,128,128]{2,1,0:T(8,128)(2,1)S(1)}, bf16[8,128,128]{2,1,0:T(8,128)(2,1)S(1)}, u32[]{:S(2)}, u32[]{:S(2)}) %collective-permute-start.37) | collective-permute-done | bytes 262176 | tf_op jit(solution)/shard_map/ppermute | solution.py:274
  157.7 7.5 %backward_blocks.3 = bf16[16,128,128]{2,1,0:T(8,128)(2,1)} custom-call(s32[1]{0:T(128)} %bitcast.14.live, s32[1]{0:T(128)} %bitcast.2.me, s32[2,256]{1,0:T(2,128)} %bitcast.27, bf16[256,128,128]{2,1,0:T(8,128)(2,1)} %bitcast.20, bf16[8,128,128]{2,1,0:T(8,128)(2,1)} %get-tuple-element.77.refs_0_, bf16[8,128,128]{2,1,0:T(8,128)(2,1)} %copy-done.14, ...), custom_call_target="tpu_custom_call" | custom-call | flops 4294967296 | bytes 16777216 | tf_op jit(solution)/shard_map/backward_blocks/pallas_call | solution.py:195
  (146 shorter events, 40.0 us)
Async XLA Ops:
  0.6 15.2 %collective-permute-start.1 = (bf16[2048,128]{1,0:T(8,128)(2,1)}, bf16[2048,128]{1,0:T(8,128)(2,1)S(1)}, u32[]{:S(2)}, u32[]{:S(2)}) collective-permute-start(bf16[2048,128]{1,0:T(8,128)(2,1)} %param.7), channel_id=1, source_target_pairs={{0,16},{16,0},{1,17},{17,1},{2,18},{18,2},{3,19},{19,3},{4,20},{20... | collective-permute-start | bytes 1572872 | tf_op jit(solution)/shard_map/ppermute | solution.py:274
  10.9 12.7 %collective-permute-start = (bf16[64,128,128]{2,1,0:T(8,128)(2,1)}, bf16[64,128,128]{2,1,0:T(8,128)(2,1)S(1)}, u32[]{:S(2)}, u32[]{:S(2)}) collective-permute-start(bf16[64,128,128]{2,1,0:T(8,128)(2,1)} %get-tuple-element.51), channel_id=1, source_target_pairs={{0,1},{1,0},{2,3},{3,2},{4,5},{5,4},{6,7},{7,6},{8,9},{9,8},{10,11... | collective-permute-start | bytes 6291464 | tf_op jit(solution)/shard_map/ppermute | solution.py:274
  24.4 14.8 %collective-permute-start.2 = (bf16[16,128,128]{2,1,0:T(8,128)(2,1)S(1)}, bf16[16,128,128]{2,1,0:T(8,128)(2,1)S(1)}, u32[]{:S(2)}, u32[]{:S(2)}) collective-permute-start(bf16[16,128,128]{2,1,0:T(8,128)(2,1)S(1)} %get-tuple-element.102), channel_id=1, source_target_pairs={{0,2},{1,3},{2,0},{3,1},{4,6},{5,7},{6,4},{7,5},{8,10},{9,11},{10,... | collective-permute-start | bytes 1572872 | tf_op jit(solution)/shard_map/ppermute | solution.py:274
  29.0 14.8 %collective-permute-start.6 = (bf16[16,128,128]{2,1,0:T(8,128)(2,1)S(1)}, bf16[16,128,128]{2,1,0:T(8,128)(2,1)S(1)}, u32[]{:S(2)}, u32[]{:S(2)}) collective-permute-start(bf16[16,128,128]{2,1,0:T(8,128)(2,1)S(1)} %get-tuple-element.99), channel_id=1, source_target_pairs={{0,4},{1,5},{2,6},{3,7},{4,0},{5,1},{6,2},{7,3},{8,12},{9,13},{10,... | collective-permute-start | bytes 1572872 | tf_op jit(solution)/shard_map/ppermute | solution.py:274
  30.9 19.5 %collective-permute-start.5 = (bf16[16,128,128]{2,1,0:T(8,128)(2,1)S(1)}, bf16[16,128,128]{2,1,0:T(8,128)(2,1)S(1)}, u32[]{:S(2)}, u32[]{:S(2)}) collective-permute-start(bf16[16,128,128]{2,1,0:T(8,128)(2,1)S(1)} %get-tuple-element.101), channel_id=1, source_target_pairs={{0,2},{1,3},{2,0},{3,1},{4,6},{5,7},{6,4},{7,5},{8,10},{9,11},{10,... | collective-permute-start | bytes 1572872 | tf_op jit(solution)/shard_map/ppermute | solution.py:274
  39.3 11.2 %collective-permute-start.4 = (bf16[8,128,128]{2,1,0:T(8,128)(2,1)S(1)}, bf16[8,128,128]{2,1,0:T(8,128)(2,1)S(1)}, u32[]{:S(2)}, u32[]{:S(2)}) collective-permute-start(bf16[8,128,128]{2,1,0:T(8,128)(2,1)S(1)} %get-tuple-element.110), channel_id=1, source_target_pairs={{0,4},{1,5},{2,6},{3,7},{4,0},{5,1},{6,2},{7,3},{8,12},{9,13},{10,... | collective-permute-start | bytes 786440 | tf_op jit(solution)/shard_map/ppermute | solution.py:274
  41.2 20.5 %collective-permute-start.10 = (bf16[16,128,128]{2,1,0:T(8,128)(2,1)S(1)}, bf16[16,128,128]{2,1,0:T(8,128)(2,1)S(1)}, u32[]{:S(2)}, u32[]{:S(2)}) collective-permute-start(bf16[16,128,128]{2,1,0:T(8,128)(2,1)S(1)} %get-tuple-element.97), channel_id=1, source_target_pairs={{0,2},{1,3},{2,0},{3,1},{4,6},{5,7},{6,4},{7,5},{8,10},{9,11},{10,... | collective-permute-start | bytes 1572872 | tf_op jit(solution)/shard_map/ppermute | solution.py:274
  50.6 10.4 %collective-permute-start.8 = (bf16[8,128,128]{2,1,0:T(8,128)(2,1)S(1)}, bf16[8,128,128]{2,1,0:T(8,128)(2,1)S(1)}, u32[]{:S(2)}, u32[]{:S(2)}) collective-permute-start(bf16[8,128,128]{2,1,0:T(8,128)(2,1)S(1)} %get-tuple-element.109), channel_id=1, source_target_pairs={{0,4},{1,5},{2,6},{3,7},{4,0},{5,1},{6,2},{7,3},{8,12},{9,13},{10,... | collective-permute-start | bytes 786440 | tf_op jit(solution)/shard_map/ppermute | solution.py:274
  57.8 11.1 %collective-permute-start.12 = (bf16[8,128,128]{2,1,0:T(8,128)(2,1)S(1)}, bf16[8,128,128]{2,1,0:T(8,128)(2,1)S(1)}, u32[]{:S(2)}, u32[]{:S(2)}) collective-permute-start(bf16[8,128,128]{2,1,0:T(8,128)(2,1)S(1)} %get-tuple-element.105), channel_id=1, source_target_pairs={{0,2},{1,3},{2,0},{3,1},{4,6},{5,7},{6,4},{7,5},{8,10},{9,11},{10,... | collective-permute-start | bytes 786440 | tf_op jit(solution)/shard_map/ppermute | solution.py:274
  61.8 12.0 %collective-permute-start.11 = (bf16[8,128,128]{2,1,0:T(8,128)(2,1)S(1)}, bf16[8,128,128]{2,1,0:T(8,128)(2,1)S(1)}, u32[]{:S(2)}, u32[]{:S(2)}) collective-permute-start(bf16[8,128,128]{2,1,0:T(8,128)(2,1)S(1)} %get-tuple-element.107), channel_id=1, source_target_pairs={{0,4},{1,5},{2,6},{3,7},{4,0},{5,1},{6,2},{7,3},{8,12},{9,13},{10,... | collective-permute-start | bytes 786440 | tf_op jit(solution)/shard_map/ppermute | solution.py:274
  66.4 10.4 %collective-permute-start.9 = (bf16[4,128,128]{2,1,0:T(8,128)(2,1)S(1)}, bf16[4,128,128]{2,1,0:T(8,128)(2,1)S(1)}, u32[]{:S(2)}, u32[]{:S(2)}) collective-permute-start(bf16[4,128,128]{2,1,0:T(8,128)(2,1)S(1)} %get-tuple-element.116), channel_id=1, source_target_pairs={{0,8},{1,9},{2,10},{3,11},{4,12},{5,13},{6,14},{7,15},{8,0},{9,1},... | collective-permute-start | bytes 393224 | tf_op jit(solution)/shard_map/ppermute | solution.py:274
  69.6 14.6 %collective-permute-start.14 = (bf16[4,128,128]{2,1,0:T(8,128)(2,1)S(1)}, bf16[4,128,128]{2,1,0:T(8,128)(2,1)S(1)}, u32[]{:S(2)}, u32[]{:S(2)}) collective-permute-start(bf16[4,128,128]{2,1,0:T(8,128)(2,1)S(1)} %get-tuple-element.113), channel_id=1, source_target_pairs={{0,8},{1,9},{2,10},{3,11},{4,12},{5,13},{6,14},{7,15},{8,0},{9,1},... | collective-permute-start | bytes 393224 | tf_op jit(solution)/shard_map/ppermute | solution.py:274
  74.6 11.8 %collective-permute-start.13 = (bf16[4,128,128]{2,1,0:T(8,128)(2,1)S(1)}, bf16[4,128,128]{2,1,0:T(8,128)(2,1)S(1)}, u32[]{:S(2)}, u32[]{:S(2)}) collective-permute-start(bf16[4,128,128]{2,1,0:T(8,128)(2,1)S(1)} %get-tuple-element.114), channel_id=1, source_target_pairs={{0,8},{1,9},{2,10},{3,11},{4,12},{5,13},{6,14},{7,15},{8,0},{9,1},... | collective-permute-start | bytes 393224 | tf_op jit(solution)/shard_map/ppermute | solution.py:274
  90.7 11.9 %collective-permute-start.16 = (bf16[8,128,128]{2,1,0:T(8,128)(2,1)}, bf16[8,128,128]{2,1,0:T(8,128)(2,1)S(1)}, u32[]{:S(2)}, u32[]{:S(2)}) collective-permute-start(bf16[8,128,128]{2,1,0:T(8,128)(2,1)} %get-tuple-element.77.refs_0_), channel_id=1, source_target_pairs={{0,4},{1,5},{2,6},{3,7},{4,0},{5,1},{6,2},{7,3},{8,12},{9,13},{10,... | collective-permute-start | bytes 786440 | tf_op jit(solution)/shard_map/ppermute | solution.py:274
  90.7 7.9 %collective-permute-start.17 = (bf16[8,128,128]{2,1,0:T(8,128)(2,1)}, bf16[8,128,128]{2,1,0:T(8,128)(2,1)S(1)}, u32[]{:S(2)}, u32[]{:S(2)}) collective-permute-start(bf16[8,128,128]{2,1,0:T(8,128)(2,1)} %get-tuple-element.77.refs_0_), channel_id=1, source_target_pairs={{0,2},{1,3},{2,0},{3,1},{4,6},{5,7},{6,4},{7,5},{8,10},{9,11},{10,... | collective-permute-start | bytes 786440 | tf_op jit(solution)/shard_map/ppermute | solution.py:274
  92.2 14.1 %collective-permute-start.25 = (bf16[8,128,128]{2,1,0:T(8,128)(2,1)}, bf16[8,128,128]{2,1,0:T(8,128)(2,1)S(1)}, u32[]{:S(2)}, u32[]{:S(2)}) collective-permute-start(bf16[8,128,128]{2,1,0:T(8,128)(2,1)} %get-tuple-element.71), channel_id=1, source_target_pairs={{0,8},{1,9},{2,10},{3,11},{4,12},{5,13},{6,14},{7,15},{8,0},{9,1},... | collective-permute-start | bytes 786440 | tf_op jit(solution)/shard_map/ppermute | solution.py:274
  95.4 9.7 %collective-permute-start.15 = (f32[144,256]{1,0:T(8,128)S(1)}, f32[144,256]{1,0:T(8,128)S(1)}, u32[]{:S(2)}, u32[]{:S(2)}) collective-permute-start(f32[144,256]{1,0:T(8,128)S(1)} %constant_dynamic-slice_fusion), channel_id=1, source_target_pairs={{0,1},{1,0},{2,3},{3,2},{4,5},{5,4},{6,7},{7,6},{8,9},{9,8},{10,11... | collective-permute-start | bytes 442376 | tf_op jit(solution)/shard_map/ppermute | solution.py:274
  106.5 13.1 %collective-permute-start.24 = (bf16[8,128,128]{2,1,0:T(8,128)(2,1)}, bf16[8,128,128]{2,1,0:T(8,128)(2,1)S(1)}, u32[]{:S(2)}, u32[]{:S(2)}) collective-permute-start(bf16[8,128,128]{2,1,0:T(8,128)(2,1)} %get-tuple-element.77.refs_0_), channel_id=1, source_target_pairs={{0,1},{1,0},{2,3},{3,2},{4,5},{5,4},{6,7},{7,6},{8,9},{9,8},{10,11... | collective-permute-start | bytes 786440 | tf_op jit(solution)/shard_map/ppermute | solution.py:274
  106.6 18.0 %collective-permute-start.28 = (bf16[8,128,128]{2,1,0:T(8,128)(2,1)}, bf16[8,128,128]{2,1,0:T(8,128)(2,1)S(1)}, u32[]{:S(2)}, u32[]{:S(2)}) collective-permute-start(bf16[8,128,128]{2,1,0:T(8,128)(2,1)} %get-tuple-element.77.refs_0_), channel_id=1, source_target_pairs={{0,12},{1,13},{2,14},{3,15},{4,8},{5,9},{6,10},{7,11},{8,4},{9,5},... | collective-permute-start | bytes 786440 | tf_op jit(solution)/shard_map/ppermute | solution.py:274
  109.0 24.8 %collective-permute-start.29 = (bf16[8,128,128]{2,1,0:T(8,128)(2,1)}, bf16[8,128,128]{2,1,0:T(8,128)(2,1)S(1)}, u32[]{:S(2)}, u32[]{:S(2)}) collective-permute-start(bf16[8,128,128]{2,1,0:T(8,128)(2,1)} %get-tuple-element.77.refs_0_), channel_id=1, source_target_pairs={{0,8},{1,9},{2,10},{3,11},{4,12},{5,13},{6,14},{7,15},{8,0},{9,1},... | collective-permute-start | bytes 786440 | tf_op jit(solution)/shard_map/ppermute | solution.py:274
  110.2 9.2 %collective-permute-start.31 = (bf16[8,128,128]{2,1,0:T(8,128)(2,1)S(1)}, bf16[8,128,128]{2,1,0:T(8,128)(2,1)S(1)}, u32[]{:S(2)}, u32[]{:S(2)}) collective-permute-start(bf16[8,128,128]{2,1,0:T(8,128)(2,1)S(1)} %pad_maximum_fusion.5), channel_id=1, source_target_pairs={{0,2},{1,3},{2,0},{3,1},{4,6},{5,7},{6,4},{7,5},{8,10},{9,11},{10,... | collective-permute-start | bytes 786440 | tf_op jit(solution)/shard_map/ppermute | solution.py:274
  113.4 20.5 %collective-permute-start.27 = (bf16[16,128,128]{2,1,0:T(8,128)(2,1)S(1)}, bf16[16,128,128]{2,1,0:T(8,128)(2,1)S(1)}, u32[]{:S(2)}, u32[]{:S(2)}) collective-permute-start(bf16[16,128,128]{2,1,0:T(8,128)(2,1)S(1)} %pad_maximum_fusion.2), channel_id=1, source_target_pairs={{0,2},{1,3},{2,0},{3,1},{4,6},{5,7},{6,4},{7,5},{8,10},{9,11},{10,... | collective-permute-start | bytes 1572872 | tf_op jit(solution)/shard_map/ppermute | solution.py:274
  119.6 20.7 %collective-permute-start.32 = (bf16[16,128,128]{2,1,0:T(8,128)(2,1)S(1)}, bf16[16,128,128]{2,1,0:T(8,128)(2,1)S(1)}, u32[]{:S(2)}, u32[]{:S(2)}) collective-permute-start(bf16[16,128,128]{2,1,0:T(8,128)(2,1)S(1)} %pad_maximum_fusion.3), channel_id=1, source_target_pairs={{0,4},{1,5},{2,6},{3,7},{4,0},{5,1},{6,2},{7,3},{8,12},{9,13},{10,... | collective-permute-start | bytes 1572872 | tf_op jit(solution)/shard_map/ppermute | solution.py:274
  124.6 9.9 %collective-permute-start.23 = (bf16[8,128,128]{2,1,0:T(8,128)(2,1)S(1)}, bf16[8,128,128]{2,1,0:T(8,128)(2,1)S(1)}, u32[]{:S(2)}, u32[]{:S(2)}) collective-permute-start(bf16[8,128,128]{2,1,0:T(8,128)(2,1)S(1)} %collective-permute-done.17.refs_4_), channel_id=1, source_target_pairs={{0,1},{1,0},{2,3},{3,2},{4,5},{5,4},{6,7},{7,6},{8,9},{9,8},{10,11... | collective-permute-start | bytes 786440 | tf_op jit(solution)/shard_map/ppermute | solution.py:274
  124.6 9.9 %collective-permute-start.22 = (bf16[8,128,128]{2,1,0:T(8,128)(2,1)S(1)}, bf16[8,128,128]{2,1,0:T(8,128)(2,1)S(1)}, u32[]{:S(2)}, u32[]{:S(2)}) collective-permute-start(bf16[8,128,128]{2,1,0:T(8,128)(2,1)S(1)} %collective-permute-done.16.refs_2_), channel_id=1, source_target_pairs={{0,1},{1,0},{2,3},{3,2},{4,5},{5,4},{6,7},{7,6},{8,9},{9,8},{10,11... | collective-permute-start | bytes 786440 | tf_op jit(solution)/shard_map/ppermute | solution.py:274
  141.1 11.7 %collective-permute-start.36 = (bf16[8,128,128]{2,1,0:T(8,128)(2,1)S(1)}, bf16[8,128,128]{2,1,0:T(8,128)(2,1)S(1)}, u32[]{:S(2)}, u32[]{:S(2)}) collective-permute-start(bf16[8,128,128]{2,1,0:T(8,128)(2,1)S(1)} %collective-permute-done.29.refs_1_), channel_id=1, source_target_pairs={{0,2},{1,3},{2,0},{3,1},{4,6},{5,7},{6,4},{7,5},{8,10},{9,11},{10,... | collective-permute-start | bytes 786440 | tf_op jit(solution)/shard_map/ppermute | solution.py:274
  141.7 13.4 %collective-permute-start.37 = (bf16[8,128,128]{2,1,0:T(8,128)(2,1)S(1)}, bf16[8,128,128]{2,1,0:T(8,128)(2,1)S(1)}, u32[]{:S(2)}, u32[]{:S(2)}) collective-permute-start(bf16[8,128,128]{2,1,0:T(8,128)(2,1)S(1)} %collective-permute-done.28.refs_3_), channel_id=1, source_target_pairs={{0,2},{1,3},{2,0},{3,1},{4,6},{5,7},{6,4},{7,5},{8,10},{9,11},{10,... | collective-permute-start | bytes 786440 | tf_op jit(solution)/shard_map/ppermute | solution.py:274
  143.2 12.7 %collective-permute-start.38 = (bf16[8,128,128]{2,1,0:T(8,128)(2,1)S(1)}, bf16[8,128,128]{2,1,0:T(8,128)(2,1)S(1)}, u32[]{:S(2)}, u32[]{:S(2)}) collective-permute-start(bf16[8,128,128]{2,1,0:T(8,128)(2,1)S(1)} %collective-permute-done.29.refs_1_), channel_id=1, source_target_pairs={{0,1},{1,0},{2,3},{3,2},{4,5},{5,4},{6,7},{7,6},{8,9},{9,8},{10,11... | collective-permute-start | bytes 786440 | tf_op jit(solution)/shard_map/ppermute | solution.py:274
  143.2 12.7 %collective-permute-start.39 = (bf16[8,128,128]{2,1,0:T(8,128)(2,1)S(1)}, bf16[8,128,128]{2,1,0:T(8,128)(2,1)S(1)}, u32[]{:S(2)}, u32[]{:S(2)}) collective-permute-start(bf16[8,128,128]{2,1,0:T(8,128)(2,1)S(1)} %collective-permute-done.28.refs_3_), channel_id=1, source_target_pairs={{0,1},{1,0},{2,3},{3,2},{4,5},{5,4},{6,7},{7,6},{8,9},{9,8},{10,11... | collective-permute-start | bytes 786440 | tf_op jit(solution)/shard_map/ppermute | solution.py:274
  144.6 8.2 %collective-permute-start.30 = (f32[144,256]{1,0:T(8,128)S(1)}, f32[144,256]{1,0:T(8,128)S(1)}, u32[]{:S(2)}, u32[]{:S(2)}) collective-permute-start(f32[144,256]{1,0:T(8,128)S(1)} %add.129), channel_id=1, source_target_pairs={{0,4},{1,5},{2,6},{3,7},{4,0},{5,1},{6,2},{7,3},{8,12},{9,13},{10,... | collective-permute-start | bytes 442376 | tf_op jit(solution)/shard_map/ppermute | solution.py:274
  155.6 14.0 %collective-permute-start.42 = (bf16[2048,128]{1,0:T(8,128)(2,1)}, bf16[2048,128]{1,0:T(8,128)(2,1)S(1)}, u32[]{:S(2)}, u32[]{:S(2)}) collective-permute-start(bf16[2048,128]{1,0:T(8,128)(2,1)} %bitcast.22), channel_id=1, source_target_pairs={{0,16},{16,0},{1,17},{17,1},{2,18},{18,2},{3,19},{19,3},{4,20},{20... | collective-permute-start | bytes 1572872 | tf_op jit(solution)/shard_map/ppermute | solution.py:274
  155.9 9.4 %collective-permute-start.35 = (f32[144,256]{1,0:T(8,128)S(1)}, f32[144,256]{1,0:T(8,128)S(1)}, u32[]{:S(2)}, u32[]{:S(2)}) collective-permute-start(f32[144,256]{1,0:T(8,128)S(1)} %add.130), channel_id=1, source_target_pairs={{0,8},{1,9},{2,10},{3,11},{4,12},{5,13},{6,14},{7,15},{8,0},{9,1},... | collective-permute-start | bytes 442376 | tf_op jit(solution)/shard_map/ppermute | solution.py:274
  (40 other events, 312.2 us)
